TPU v7x, 32 devices: a whole 2x2x4 slice. The times are simulated.
32 devices in a mesh: group: 4 (over y, core), fsdp: 8 (over z, x).
Axes of the slice: x: 2, y: 2, z: 4, core: 2. Of those that a mesh axis runs over, the one named last changes fastest.
Arguments:
- tokens: bfloat16 [4, 3072, 4096], P('group', 'fsdp'), may hold values from -6 to 6
- targets: bfloat16 [4, 3072, 512], P('group', 'fsdp'), may hold values from -6 to 6
- params: float32 [4, 4096, 512], P('group', 'fsdp'), may hold values from -6 to 6
- momentum: float32 [4, 4096, 512], P('group', 'fsdp'), may hold values from -6 to 6
- push_weight: float32 [4], P('group'), may hold values from 0.5 to 2
Outputs:
- new_params: float32 [4, 4096, 512], P('group', 'fsdp')
- new_momentum: float32 [4, 4096, 512], P('group', 'fsdp')
All inputs are finite; a program needn't handle non-finite values.
Results may differ from a plain program's by a relative error of at most 0.0031.
Values may be sent and summed in bfloat16 or wider, within the bound.
No kernel may reach another device: no remote copies, remote signals or barrier semaphores. Data moves between devices by JAX's collectives and lax.ppermute only.
A program may use at most 64 MiB of HBM per device.

v0:
```python
import jax
import jax.numpy as jnp
from jax import lax
from jax.sharding import PartitionSpec as P

STEPS = 2


def from_behind(value, axis, steps):
    count = lax.axis_size(axis)
    pairs = [(source, (source + steps) % count) for source in range(count)]
    return lax.ppermute(value, axis, pairs)


def shards(tokens, targets, params, momentum, push_weight):
    inputs = tokens[0]
    target = targets[0].astype(jnp.float32)
    shard_now = params[0]
    moment = momentum[0]
    weight = push_weight
    key_scale = inputs.shape[1] ** (-0.5)
    for round_index in range(STEPS):
        debiased = (shard_now / weight[0]).astype(jnp.bfloat16)
        raw_keys = jnp.dot(
            inputs,
            lax.all_gather(debiased, "fsdp", axis=0, tiled=True),
            preferred_element_type=jnp.float32,
        )
        residual = key_scale * raw_keys - target
        grad_out = (key_scale * residual).astype(jnp.bfloat16)
        gradient = lax.psum_scatter(
            lax.dot_general(
                inputs, grad_out, (((0,), (0,)), ((), ())), preferred_element_type=jnp.float32
            ),
            "fsdp",
            scatter_dimension=0,
            tiled=True,
        )
        moment = 0.9 * moment + gradient
        shard_now = shard_now - 0.2 * moment
        half_shard = 0.5 * shard_now
        half_weight = 0.5 * weight
        got_shard, got_weight = from_behind((half_shard, half_weight), "group", 2**round_index)
        shard_now = half_shard + got_shard
        weight = half_weight + got_weight
    return ((shard_now / weight[0])[None], moment[None])


def solution(mesh):
    return jax.shard_map(
        shards,
        mesh=mesh,
        in_specs=(
            P("group", "fsdp", None),
            P("group", "fsdp", None),
            P("group", "fsdp", None),
            P("group", "fsdp", None),
            P("group"),
        ),
        out_specs=(P("group", "fsdp", None), P("group", "fsdp", None)),
        check_vma=False,
    )
```

profile of v0, /device:TPU:0, one launch (start us, length us, event | category | flops | bytes accessed | tf_op | source)
XLA Modules:
  0.0 542.4 jit_solution(7792523782229687795)
XLA Ops:
  7.2 0.0 copy-start
  7.2 0.0 all-gather.3.cloned.1.call-start
  8.0 2.7 copy.7
  10.8 2.1 fusion.40
  12.9 0.0 all-gather.3.cloned.1.call-update
  12.9 0.0 reduce-scatter.3.cloned.1.call-start
  13.0 77.8 %all-gather.3.cloned.1.call-done = bf16[4096,512]{0,1:T(8,128)(2,1)} async-done(((bf16[512,512]{0,1:T(8,128)(2,1)}), bf16[4096,512]{0,1:T(8,128)(2,1)}) %all-gather.3.cloned.1.call-update) | async-done | bytes 4194320 | tf_op jit(solution)/shard_map/all_gather | solution.py:26
  90.8 9.6 %convolution_bitcast_fusion.1 = f32[4096,512]{0,1:T(8,128)} fusion(bf16[1,384,4096]{2,1,0:T(8,128)(2,1)S(1)} %copy-done, bf16[4096,512]{0,1:T(8,128)(2,1)} %all-gather.3.cloned.1.call-done, bf16[1,384,512]{2,1,0:T(8,128)(2,1)S(1)} %copy-done.1), kind=kOutput, calls=%fused_computation.1 | convolution fusion | flops 3222208512 | bytes 16121856 | tf_op jit(solution)/shard_map/dot_general | solution.py:32
  100.4 0.0 reduce-scatter.3.cloned.1.call-update
  100.4 0.0 all-gather.5.cloned.1.call-start
  100.5 2.5 copy.8
  103.0 145.1 %reduce-scatter.3.cloned.1.call-done = f32[512,512]{0,1:T(8,128)} async-done(((f32[4096,512]{0,1:T(8,128)}), f32[512,512]{0,1:T(8,128)}) %reduce-scatter.3.cloned.1.call-update) | async-done | bytes 1048592 | tf_op jit(solution)/shard_map/reduce_scatter | solution.py:31
  248.1 2.2 fusion.41
  250.3 0.1 collective-permute-start
  250.4 2.4 collective-permute-start.1
  252.8 11.8 %collective-permute-done.1 = f32[1]{0:T(128)} collective-permute-done((f32[1]{0:T(128)}, f32[1]{0:T(128)}, u32[]{:S(2)}, u32[]{:S(2)}) %collective-permute-start.1) | collective-permute-done | bytes 36 | tf_op jit(solution)/shard_map/ppermute | solution.py:12
  265.3 0.0 collective-permute-done
  265.3 1.4 divide_convert_fusion
  266.7 0.0 all-gather.5.cloned.1.call-update
  266.7 0.0 reduce-scatter.5.cloned.1.call-start
  266.7 74.1 %all-gather.5.cloned.1.call-done = bf16[4096,512]{0,1:T(8,128)(2,1)} async-done(((bf16[512,512]{0,1:T(8,128)(2,1)}), bf16[4096,512]{0,1:T(8,128)(2,1)}) %all-gather.5.cloned.1.call-update) | async-done | bytes 4194320 | tf_op jit(solution)/shard_map/all_gather | solution.py:26
  340.9 9.6 %convolution_bitcast_fusion = f32[4096,512]{0,1:T(8,128)} fusion(bf16[1,384,4096]{2,1,0:T(8,128)(2,1)S(1)} %copy-done, bf16[4096,512]{0,1:T(8,128)(2,1)} %all-gather.5.cloned.1.call-done, bf16[1,384,512]{2,1,0:T(8,128)(2,1)S(1)} %copy-done.1), kind=kOutput, calls=%fused_computation | convolution fusion | flops 3222208512 | bytes 16121856 | tf_op jit(solution)/shard_map/dot_general | solution.py:32
  350.4 0.0 reduce-scatter.5.cloned.1.call-update
  350.4 147.8 %reduce-scatter.5.cloned.1.call-done = f32[512,512]{0,1:T(8,128)} async-done(((f32[4096,512]{0,1:T(8,128)}), f32[512,512]{0,1:T(8,128)}) %reduce-scatter.5.cloned.1.call-update) | async-done | bytes 1048592 | tf_op jit(solution)/shard_map/reduce_scatter | solution.py:31
  498.2 4.0 fusion.44
  502.2 1.5 collective-permute-start.2
  503.7 22.8 %collective-permute-start.3 = (f32[1]{0:T(128)}, f32[1]{0:T(128)}, u32[]{:S(2)}, u32[]{:S(2)}) collective-permute-start(f32[1]{0:T(128)} %mul.59), channel_id=1, source_target_pairs={{0,16},{8,24},{16,0},{24,8},{1,17},{9,25},{17,1},{25,9},{2,18},{10... | collective-permute-start | bytes 20 | tf_op jit(solution)/shard_map/ppermute | solution.py:12
  526.5 1.0 collective-permute-done.3
  528.1 2.5 copy.10
  530.6 0.0 collective-permute-done.2
  530.6 2.7 divide_bitcast_fusion
  533.4 2.5 copy.9
  (3 shorter events, 0.0 us)
Async XLA Ops:
  7.2 83.6 %copy-start = (bf16[1,384,4096]{2,1,0:T(8,128)(2,1)S(1)}, bf16[1,384,4096]{2,1,0:T(8,128)(2,1)}, u32[]{:S(2)}) copy-start(bf16[1,384,4096]{2,1,0:T(8,128)(2,1)} %param.5) | copy-start | bytes 9437188
  7.2 83.6 %copy-start.1 = (bf16[1,384,512]{2,1,0:T(8,128)(2,1)S(1)}, bf16[1,384,512]{2,1,0:T(8,128)(2,1)}, u32[]{:S(2)}) copy-start(bf16[1,384,512]{2,1,0:T(8,128)(2,1)} %param.6) | copy-start | bytes 1179652
  7.2 83.6 %all-gather.3.cloned.1.call-start = ((), (), s32[]{:S(2)}) async-start(), calls=%async_computation.2 | async-start | bytes 4718592 | tf_op jit(solution)/shard_map/all_gather | solution.py:26
  12.9 235.2 %reduce-scatter.3.cloned.1.call-start = ((), (), s32[]{:S(2)}) async-start(), calls=%async_computation.3 | async-start | bytes 9437184 | tf_op jit(solution)/shard_map/reduce_scatter | solution.py:31
  100.4 240.5 %all-gather.5.cloned.1.call-start = ((), (), s32[]{:S(2)}) async-start(), calls=%async_computation.4 | async-start | bytes 4718592 | tf_op jit(solution)/shard_map/all_gather | solution.py:26
  250.3 14.9 %collective-permute-start = (f32[512,512]{0,1:T(8,128)S(1)}, f32[512,512]{0,1:T(8,128)S(1)}, u32[]{:S(2)}, u32[]{:S(2)}) collective-permute-start(f32[512,512]{0,1:T(8,128)S(1)} %fusion.41), channel_id=1, source_target_pairs={{0,8},{8,16},{16,24},{24,0},{1,9},{9,17},{17,25},{25,1},{2,10},{10... | collective-permute-start | bytes 3145736 | tf_op jit(solution)/shard_map/ppermute | solution.py:12
  250.4 14.2 %collective-permute-start.1 = (f32[1]{0:T(128)}, f32[1]{0:T(128)}, u32[]{:S(2)}, u32[]{:S(2)}) collective-permute-start(f32[1]{0:T(128)} %mul.53), channel_id=1, source_target_pairs={{0,8},{8,16},{16,24},{24,0},{1,9},{9,17},{17,25},{25,1},{2,10},{10... | collective-permute-start | bytes 20 | tf_op jit(solution)/shard_map/ppermute | solution.py:12
  266.7 231.5 %reduce-scatter.5.cloned.1.call-start = ((), (), s32[]{:S(2)}) async-start(), calls=%async_computation.5 | async-start | bytes 9437184 | tf_op jit(solution)/shard_map/reduce_scatter | solution.py:31
  502.2 28.4 %collective-permute-start.2 = (f32[512,512]{0,1:T(8,128)}, f32[512,512]{0,1:T(8,128)}, u32[]{:S(2)}, u32[]{:S(2)}) collective-permute-start(f32[512,512]{0,1:T(8,128)} %get-tuple-element.7), channel_id=1, source_target_pairs={{0,16},{8,24},{16,0},{24,8},{1,17},{9,25},{17,1},{25,9},{2,18},{10... | collective-permute-start | bytes 3145736 | tf_op jit(solution)/shard_map/ppermute | solution.py:12
  503.7 23.8 %collective-permute-start.3 = (f32[1]{0:T(128)}, f32[1]{0:T(128)}, u32[]{:S(2)}, u32[]{:S(2)}) collective-permute-start(f32[1]{0:T(128)} %mul.59), channel_id=1, source_target_pairs={{0,16},{8,24},{16,0},{24,8},{1,17},{9,25},{17,1},{25,9},{2,18},{10... | collective-permute-start | bytes 20 | tf_op jit(solution)/shard_map/ppermute | solution.py:12
Sparse Core Ops, SparseCore 0:
  13.1 77.7 all-gather.2
  100.5 147.5 reduce-scatter.2
  266.8 74.0 all-gather.4
  350.6 147.5 reduce-scatter.4
where the time goes:
time: 543 us; the launch traced here: 542 us
  waiting for transfers between devices  458 us (84%)
  starting transfers between devices  26.9 us (5%)
  matrix products  19.1 us (4%)
  between operations  15.9 us (3%)
  other arithmetic  12.5 us (2%)
  local copies, waits for them, and re-layouts  10.4 us (2%)
    reduce_scatter x2, waiting for transfers between devices, shards(): lax.psum_scatter(lax.dot_general(inputs, grad_out, (((0,), (0,)), ((), ()...  293 us
    all_gather x2, waiting for transfers between devices, shards(): lax.all_gather(debiased, 'fsdp', axis=0, tiled=True)  152 us
    ppermute x4, starting transfers between devices, from_behind(): return lax.ppermute(value, axis, pairs)  26.7 us
    dot_general x2, matrix products, shards(): lax.dot_general(inputs, grad_out, (((0,), (0,)), ((), ())), preferred_ele...  19.1 us
    ppermute x4, waiting for transfers between devices, from_behind(): return lax.ppermute(value, axis, pairs)  12.8 us
  transfers between devices with their start and end apart: 8, of which 6 were waited for; matrix products, arithmetic and copies ran while one was open for 1% of the time, Pallas kernels for 0%

commit v1 on v0

v1 whole, which is shorter than its diff:
```python
import jax
import jax.numpy as jnp
from jax import lax
from jax.sharding import PartitionSpec as P

STEPS = 2
CHUNKS = 2


def from_behind(value, axis, steps):
    count = lax.axis_size(axis)
    pairs = [(source, (source + steps) % count) for source in range(count)]
    return lax.ppermute(value, axis, pairs)


def shards(tokens, targets, params, momentum, push_weight):
    inputs = tokens[0]
    rows, width = inputs.shape
    features = params.shape[2]
    count = lax.axis_size("fsdp")
    lane = lax.rem(lax.axis_index("fsdp"), 2)
    swap = [(i, i ^ 1) for i in range(count)]
    lines = [list(range(0, count, 2)), list(range(1, count, 2))]
    key_scale = width ** (-0.5)
    part = features // CHUNKS

    def chunk(array, c):
        return array[:, c * part : (c + 1) * part]

    weights = [push_weight]
    for step in range(STEPS):
        weights.append(0.5 * weights[-1] + 0.5 * from_behind(weights[-1], "group", 2**step))

    state = [chunk(params[0], c) for c in range(CHUNKS)]
    moment = [chunk(momentum[0], c) for c in range(CHUNKS)]
    target = [chunk(targets[0], c).astype(jnp.float32) for c in range(CHUNKS)]

    columns = inputs.reshape(rows, count // 2, 2, width // count)
    mine = lax.dynamic_index_in_dim(columns, lane, 2, keepdims=False)
    theirs = lax.dynamic_index_in_dim(columns, 1 - lane, 2, keepdims=False)
    mine = mine.reshape(rows, width // 2)
    theirs = lax.ppermute(theirs.reshape(rows, width // 2), "fsdp", swap)

    for step in range(STEPS):
        for c in range(CHUNKS):
            debiased = (state[c] / weights[step][0]).astype(jnp.bfloat16)
            gathered = lax.all_gather(
                debiased, "fsdp", axis=0, tiled=True, axis_index_groups=lines
            )
            before = state[c] - (0.2 * 0.9) * moment[c]
            before = 0.5 * (before + from_behind(before, "group", 2**step))
            own = key_scale * jnp.dot(mine, gathered, preferred_element_type=jnp.float32)
            own = own - target[c]
            other = key_scale * jnp.dot(theirs, gathered, preferred_element_type=jnp.float32)
            sent = jnp.concatenate([other, own]).astype(jnp.bfloat16)
            got = lax.ppermute(sent, "fsdp", swap).astype(jnp.float32)
            own_grad = (key_scale * (own + got[:rows])).astype(jnp.bfloat16)
            other_grad = (key_scale * (other + got[rows:])).astype(jnp.bfloat16)
            contract = (((0,), (0,)), ((), ()))
            partial = lax.dot_general(
                mine, own_grad, contract, preferred_element_type=jnp.float32
            ) + lax.dot_general(theirs, other_grad, contract, preferred_element_type=jnp.float32)
            gradient = lax.psum_scatter(
                partial.astype(jnp.bfloat16),
                "fsdp",
                scatter_dimension=0,
                axis_index_groups=lines,
                tiled=True,
            )
            behind = from_behind(gradient, "group", 2**step).astype(jnp.float32)
            gradient = gradient.astype(jnp.float32)
            moment[c] = 0.9 * moment[c] + gradient
            state[c] = before - 0.1 * (gradient + behind)
    new_params = jnp.concatenate([s / weights[STEPS][0] for s in state], axis=1)
    return new_params[None], jnp.concatenate(moment, axis=1)[None]


def solution(mesh):
    return jax.shard_map(
        shards,
        mesh=mesh,
        in_specs=(
            P("group", "fsdp", None),
            P("group", "fsdp", None),
            P("group", "fsdp", None),
            P("group", "fsdp", None),
            P("group"),
        ),
        out_specs=(P("group", "fsdp", None), P("group", "fsdp", None)),
        check_vma=False,
    )
```

time: 543 us -> 275 us (0.51)
  waiting for transfers between devices: 458 us -> 197 us
    reduce_scatter x2 -> x4, waiting for transfers between devices: 293 us -> 79.4 us  [shards(): lax.psum_scatter(partial.astype(jnp.bfloat16), 'fsdp', scatter_dimension=...]
    all_gather x2 -> x4, waiting for transfers between devices: 152 us -> 40.6 us  [shards(): lax.all_gather(debiased, 'fsdp', axis=0, tiled=True, axis_index_groups=li...]
    ppermute x0 -> x5, waiting for transfers between devices: none -> 70.8 us  [the longest x4 36.3 us: shards(): got = lax.ppermute(sent, 'fsdp', swap).astype(jnp.float32)]
    ppermute x4 -> x10, starting transfers between devices: 26.7 us -> 14 us  [from_behind(): return lax.ppermute(value, axis, pairs)]
    ppermute x0 -> x5, starting transfers between devices: none -> 9.35 us  [the longest x4 6.41 us: shards(): got = lax.ppermute(sent, 'fsdp', swap).astype(jnp.float32)]
    ppermute x4 -> x10, waiting for transfers between devices: 12.8 us -> 5.39 us  [from_behind(): return lax.ppermute(value, axis, pairs)]
    sub x0 -> x2, other arithmetic: none -> 6.56 us  [shards(): before = state[c] - 0.2 * 0.9 * moment[c]]
    unnamed x8 -> x25, local copies, waits for them, and re-layouts: 10.4 us -> 3.82 us
  transfers between devices with their start and end apart: 8 -> 23, of which waited for: 6 -> 14; matrix products, arithmetic and copies ran while one was open for 1% -> 10% of each run, Pallas kernels for 0% -> 0%
where the time goes in v1:
time: 275 us
  waiting for transfers between devices  197 us (72%)
  starting transfers between devices  23.8 us (9%)
  matrix products  19.8 us (7%)
  between operations  16.4 us (6%)
  other arithmetic  10.6 us (4%)
  local copies, waits for them, and re-layouts  7.18 us (3%)
    reduce_scatter x4, waiting for transfers between devices, shards(): lax.psum_scatter(partial.astype(jnp.bfloat16), 'fsdp', scatter_dimension=...  79.4 us
    all_gather x4, waiting for transfers between devices, shards(): lax.all_gather(debiased, 'fsdp', axis=0, tiled=True, axis_index_groups=li...  40.6 us
    ppermute x4, waiting for transfers between devices, shards(): got = lax.ppermute(sent, 'fsdp', swap).astype(jnp.float32)  36.3 us
    ppermute x1, waiting for transfers between devices, shards(): theirs = lax.ppermute(theirs.reshape(rows, width // 2), 'fsdp', swap)  34.5 us
    ppermute x10, starting transfers between devices, from_behind(): return lax.ppermute(value, axis, pairs)  14 us
    dot_general x4, matrix products, shards(): jnp.dot(theirs, gathered, preferred_element_type=jnp.float32)  7.69 us
    dot_general x4, matrix products, shards(): lax.dot_general(theirs, other_grad, contract, preferred_element_type=jnp....  6.79 us
    sub x2, other arithmetic, shards(): before = state[c] - 0.2 * 0.9 * moment[c]  6.56 us
  transfers between devices with their start and end apart: 23, of which 14 were waited for; matrix products, arithmetic and copies ran while one was open for 10% of the time, Pallas kernels for 0%

profile of v1, /device:TPU:0, one launch (start us, length us, event | category | flops | bytes accessed | tf_op | source)
XLA Modules:
  0.0 274.7 jit_solution(3422246803084221514)
XLA Ops:
  7.9 2.9 %multiply_subtract_fusion.3 = (f32[512,256]{1,0:T(8,128)}, f32[512,256]{1,0:T(8,128)}, bf16[512,256]{1,0:T(8,128)(2,1)}, bf16[512,256]{1,0:T(8,128)(2,1)}) fusion(f32[512,512]{1,0:T(8,128)} %bitcast.47, f32[512,512]{1,0:T(8,128)} %bitcast.54, f32[]{:T(128)} %bitcast.37), kind=kLoop, calls=%fused_computation.47 | loop fusion | flops 1048576 | bytes 3670020 | tf_op jit(solution)/shard_map/sub | solution.py:50
  10.8 2.8 %copy.7 = bf16[1,384,4096]{1,2,0:T(8,128)(2,1)} copy(bf16[1,384,4096]{2,1,0:T(8,128)(2,1)S(1)} %copy-done.5) | data formatting | bytes 6291456 | tf_op args[0]
  13.6 3.4 %constant_dynamic-slice_fusion = (bf16[384,4,1,512]{0,3,2,1:T(8,128)(2,1)}, bf16[384,4,1,512]{0,3,2,1:T(8,128)(2,1)S(1)}) fusion(bf16[384,4,2,512]{0,3,2,1:T(8,128)(2,1)} %bitcast.46, s32[]{:T(128)S(6)} %select_n.8, s32[]{:T(128)S(6)} %select_n.7), kind=kLoop, calls=%fused_computation.88 | loop fusion | bytes 6291464 | tf_op jit(solution)/shard_map/jit(dynamic_index_in_dim)/dynamic_slice | solution.py:40
  17.0 2.9 %collective-permute-start.1 = (bf16[384,2048]{0,1:T(8,128)(2,1)}, bf16[384,2048]{0,1:T(8,128)(2,1)S(1)}, u32[]{:S(2)}, u32[]{:S(2)}) collective-permute-start(bf16[384,2048]{0,1:T(8,128)(2,1)} %bitcast.6), channel_id=1, source_target_pairs={{0,1},{1,0},{2,3},{3,2},{4,5},{5,4},{6,7},{7,6},{8,9},{9,8},{10,11... | collective-permute-start | bytes 4718600 | tf_op jit(solution)/shard_map/ppermute | solution.py:42
  20.0 34.5 %collective-permute-done.1 = bf16[384,2048]{0,1:T(8,128)(2,1)S(1)} collective-permute-done((bf16[384,2048]{0,1:T(8,128)(2,1)}, bf16[384,2048]{0,1:T(8,128)(2,1)S(1)}, u32[]{:S(2)}, u32[]{:S(2)}) %collective-permute-start.1) | collective-permute-done | bytes 1572896 | tf_op jit(solution)/shard_map/ppermute | solution.py:42
  54.5 1.9 fusion.65
  57.1 1.8 collective-permute-start.10
  59.0 8.6 %collective-permute-done.10 = bf16[768,256]{1,0:T(8,128)(2,1)S(1)} collective-permute-done((bf16[768,256]{1,0:T(8,128)(2,1)S(1)}, bf16[768,256]{1,0:T(8,128)(2,1)S(1)}, u32[]{:S(2)}, u32[]{:S(2)}) %collective-permute-start.10) | collective-permute-done | bytes 393248 | tf_op jit(solution)/shard_map/ppermute | solution.py:56
  68.3 1.7 fusion.2
  71.2 1.9 fusion.63
  75.3 9.2 %collective-permute-done.2 = bf16[768,256]{1,0:T(8,128)(2,1)S(1)} collective-permute-done((bf16[768,256]{1,0:T(8,128)(2,1)S(1)}, bf16[768,256]{1,0:T(8,128)(2,1)S(1)}, u32[]{:S(2)}, u32[]{:S(2)}) %collective-permute-start.2) | collective-permute-done | bytes 393248 | tf_op jit(solution)/shard_map/ppermute | solution.py:56
  85.3 1.7 fusion
  87.1 1.6 collective-permute-start.9
  88.7 12.0 %reduce-scatter.9.cloned.1.call-done = bf16[512,256]{1,0:T(8,128)(2,1)} async-done(((bf16[2048,256]{1,0:T(8,128)(2,1)}), bf16[512,256]{1,0:T(8,128)(2,1)}) %reduce-scatter.9.cloned.1.call-update) | async-done | bytes 262160 | tf_op jit(solution)/shard_map/reduce_scatter | solution.py:63
  100.7 28.6 %reduce-scatter.5.cloned.1.call-done = bf16[512,256]{1,0:T(8,128)(2,1)} async-done(((bf16[2048,256]{1,0:T(8,128)(2,1)}), bf16[512,256]{1,0:T(8,128)(2,1)}) %reduce-scatter.5.cloned.1.call-update) | async-done | bytes 262160 | tf_op jit(solution)/shard_map/reduce_scatter | solution.py:63
  129.3 1.6 collective-permute-start.5
  130.9 4.4 %collective-permute-done.5 = f32[1]{0:T(128)} collective-permute-done((f32[1]{0:T(128)}, f32[1]{0:T(128)}, u32[]{:S(2)}, u32[]{:S(2)}) %collective-permute-start.5) | collective-permute-done | bytes 36 | tf_op jit(solution)/shard_map/ppermute | solution.py:13
  136.0 3.7 %multiply_subtract_fusion.2 = (f32[512,256]{1,0:T(8,128)}, bf16[512,256]{1,0:T(8,128)(2,1)}, bf16[512,256]{1,0:T(8,128)(2,1)}, f32[512,256]{1,0:T(8,128)}) fusion(bf16[512,256]{1,0:T(8,128)(2,1)} %reduce-scatter.5.cloned.1.call-done, f32[512,512]{1,0:T(8,128)} %bitcast.48, bf16[512,256]{1,0:T(8,128)(2,1)S(1)} %collective-permute-done.3, ...), kind=kLoop, calls=%fused_computation.45 | loop fusion | flops 3407872 | bytes 5767172 | tf_op jit(solution)/shard_map/sub | solution.py:50
  140.3 26.1 %all-gather.11.cloned.1.call-done = bf16[2048,256]{1,0:T(8,128)(2,1)} async-done(((bf16[512,256]{1,0:T(8,128)(2,1)}), bf16[2048,256]{1,0:T(8,128)(2,1)}) %all-gather.11.cloned.1.call-update) | async-done | bytes 1048592 | tf_op jit(solution)/shard_map/all_gather | solution.py:47
  166.5 1.9 fusion.69
  170.6 9.2 %collective-permute-done.13 = bf16[768,256]{1,0:T(8,128)(2,1)S(1)} collective-permute-done((bf16[768,256]{1,0:T(8,128)(2,1)S(1)}, bf16[768,256]{1,0:T(8,128)(2,1)S(1)}, u32[]{:S(2)}, u32[]{:S(2)}) %collective-permute-start.13) | collective-permute-done | bytes 393248 | tf_op jit(solution)/shard_map/ppermute | solution.py:56
  180.6 1.7 fusion.3
  182.6 13.3 %all-gather.7.cloned.1.call-done = bf16[2048,256]{1,0:T(8,128)(2,1)} async-done(((bf16[512,256]{1,0:T(8,128)(2,1)}), bf16[2048,256]{1,0:T(8,128)(2,1)}) %all-gather.7.cloned.1.call-update) | async-done | bytes 1048592 | tf_op jit(solution)/shard_map/all_gather | solution.py:47
  195.9 1.9 fusion.67
  198.5 1.5 collective-permute-start.6
  200.1 9.2 %collective-permute-done.6 = bf16[768,256]{1,0:T(8,128)(2,1)S(1)} collective-permute-done((bf16[768,256]{1,0:T(8,128)(2,1)S(1)}, bf16[768,256]{1,0:T(8,128)(2,1)S(1)}, u32[]{:S(2)}, u32[]{:S(2)}) %collective-permute-start.6) | collective-permute-done | bytes 393248 | tf_op jit(solution)/shard_map/ppermute | solution.py:56
  210.1 1.7 fusion.1
  213.9 11.5 %reduce-scatter.11.cloned.1.call-done = bf16[512,256]{1,0:T(8,128)(2,1)} async-done(((bf16[2048,256]{1,0:T(8,128)(2,1)}), bf16[512,256]{1,0:T(8,128)(2,1)}) %reduce-scatter.11.cloned.1.call-update) | async-done | bytes 262160 | tf_op jit(solution)/shard_map/reduce_scatter | solution.py:63
  226.9 27.3 %reduce-scatter.7.cloned.1.call-done = bf16[512,256]{1,0:T(8,128)(2,1)} async-done(((bf16[2048,256]{1,0:T(8,128)(2,1)}), bf16[512,256]{1,0:T(8,128)(2,1)}) %reduce-scatter.7.cloned.1.call-update) | async-done | bytes 262160 | tf_op jit(solution)/shard_map/reduce_scatter | solution.py:63
  255.7 5.7 %collective-permute-start.8 = (f32[1]{0:T(128)}, f32[1]{0:T(128)}, u32[]{:S(2)}, u32[]{:S(2)}) collective-permute-start(f32[1]{0:T(128)} %add.104), channel_id=1, source_target_pairs={{0,16},{8,24},{16,0},{24,8},{1,17},{9,25},{17,1},{25,9},{2,18},{10... | collective-permute-start | bytes 20 | tf_op jit(solution)/shard_map/ppermute | solution.py:13
  264.1 2.1 convert_add_fusion.4
  266.3 1.6 maximum_bitcast_fusion
  (76 shorter events, 18.0 us)
Async XLA Ops:
  7.2 47.4 %all-gather.9.cloned.1.call-start = ((), (), s32[]{:S(2)}) async-start(), calls=%async_computation.8 | async-start | bytes 1310720 | tf_op jit(solution)/shard_map/all_gather | solution.py:47
  7.9 3.0 %copy-start.5 = (bf16[1,384,4096]{2,1,0:T(8,128)(2,1)S(1)}, bf16[1,384,4096]{2,1,0:T(8,128)(2,1)}, u32[]{:S(2)}) copy-start(bf16[1,384,4096]{2,1,0:T(8,128)(2,1)} %param.5) | copy-start | bytes 9437188
  10.8 60.4 %all-gather.5.cloned.1.call-start = ((), (), s32[]{:S(2)}) async-start(), calls=%async_computation.4 | async-start | bytes 1310720 | tf_op jit(solution)/shard_map/all_gather | solution.py:47
  17.0 37.5 %collective-permute-start.1 = (bf16[384,2048]{0,1:T(8,128)(2,1)}, bf16[384,2048]{0,1:T(8,128)(2,1)S(1)}, u32[]{:S(2)}, u32[]{:S(2)}) collective-permute-start(bf16[384,2048]{0,1:T(8,128)(2,1)} %bitcast.6), channel_id=1, source_target_pairs={{0,1},{1,0},{2,3},{3,2},{4,5},{5,4},{6,7},{7,6},{8,9},{9,8},{10,11... | collective-permute-start | bytes 4718600 | tf_op jit(solution)/shard_map/ppermute | solution.py:42
  20.0 36.5 %copy-start.7 = (bf16[1,384,512]{2,1,0:T(8,128)(2,1)S(1)}, bf16[1,384,512]{2,1,0:T(8,128)(2,1)}, u32[]{:S(2)}) copy-start(bf16[1,384,512]{2,1,0:T(8,128)(2,1)} %param.6) | copy-start | bytes 1179652
  20.0 80.7 %reduce-scatter.9.cloned.1.call-start = ((), (), s32[]{:S(2)}) async-start(), calls=%async_computation.9 | async-start | bytes 1310720 | tf_op jit(solution)/shard_map/reduce_scatter | solution.py:63
  54.5 2.0 copy-start.1
  57.1 10.4 %collective-permute-start.10 = (bf16[768,256]{1,0:T(8,128)(2,1)S(1)}, bf16[768,256]{1,0:T(8,128)(2,1)S(1)}, u32[]{:S(2)}, u32[]{:S(2)}) collective-permute-start(bf16[768,256]{1,0:T(8,128)(2,1)S(1)} %pad_maximum_fusion.2), channel_id=1, source_target_pairs={{0,1},{1,0},{2,3},{3,2},{4,5},{5,4},{6,7},{7,6},{8,9},{9,8},{10,11... | collective-permute-start | bytes 1179656 | tf_op jit(solution)/shard_map/ppermute | solution.py:56
  70.0 59.3 %reduce-scatter.5.cloned.1.call-start = ((), (), s32[]{:S(2)}) async-start(), calls=%async_computation.5 | async-start | bytes 1310720 | tf_op jit(solution)/shard_map/reduce_scatter | solution.py:63
  71.2 1.9 copy-start.2
  73.7 10.8 %collective-permute-start.2 = (bf16[768,256]{1,0:T(8,128)(2,1)S(1)}, bf16[768,256]{1,0:T(8,128)(2,1)S(1)}, u32[]{:S(2)}, u32[]{:S(2)}) collective-permute-start(bf16[768,256]{1,0:T(8,128)(2,1)S(1)} %pad_maximum_fusion), channel_id=1, source_target_pairs={{0,1},{1,0},{2,3},{3,2},{4,5},{5,4},{6,7},{7,6},{8,9},{9,8},{10,11... | collective-permute-start | bytes 1179656 | tf_op jit(solution)/shard_map/ppermute | solution.py:56
  87.0 79.4 %all-gather.11.cloned.1.call-start = ((), (), s32[]{:S(2)}) async-start(), calls=%async_computation.10 | async-start | bytes 1310720 | tf_op jit(solution)/shard_map/all_gather | solution.py:47
  87.1 48.9 %collective-permute-start = (f32[512,256]{1,0:T(8,128)}, f32[512,256]{1,0:T(8,128)}, u32[]{:S(2)}, u32[]{:S(2)}) collective-permute-start(f32[512,256]{1,0:T(8,128)} %get-tuple-element.4), channel_id=1, source_target_pairs={{0,8},{8,16},{16,24},{24,0},{1,9},{9,17},{17,25},{25,1},{2,10},{10... | collective-permute-start | bytes 1572872 | tf_op jit(solution)/shard_map/ppermute | solution.py:13
  87.1 48.8 %collective-permute-start.9 = (f32[512,256]{1,0:T(8,128)}, f32[512,256]{1,0:T(8,128)}, u32[]{:S(2)}, u32[]{:S(2)}) collective-permute-start(f32[512,256]{1,0:T(8,128)} %get-tuple-element.5), channel_id=1, source_target_pairs={{0,8},{8,16},{16,24},{24,0},{1,9},{9,17},{17,25},{25,1},{2,10},{10... | collective-permute-start | bytes 1572872 | tf_op jit(solution)/shard_map/ppermute | solution.py:13
  100.7 35.3 %collective-permute-start.11 = (bf16[512,256]{1,0:T(8,128)(2,1)}, bf16[512,256]{1,0:T(8,128)(2,1)}, u32[]{:S(2)}, u32[]{:S(2)}) collective-permute-start(bf16[512,256]{1,0:T(8,128)(2,1)} %reduce-scatter.9.cloned.1.call-done), channel_id=1, source_target_pairs={{0,8},{8,16},{16,24},{24,0},{1,9},{9,17},{17,25},{25,1},{2,10},{10... | collective-permute-start | bytes 786440 | tf_op jit(solution)/shard_map/ppermute | solution.py:13
  129.3 6.7 %collective-permute-start.3 = (bf16[512,256]{1,0:T(8,128)(2,1)}, bf16[512,256]{1,0:T(8,128)(2,1)S(1)}, u32[]{:S(2)}, u32[]{:S(2)}) collective-permute-start(bf16[512,256]{1,0:T(8,128)(2,1)} %reduce-scatter.5.cloned.1.call-done), channel_id=1, source_target_pairs={{0,8},{8,16},{16,24},{24,0},{1,9},{9,17},{17,25},{25,1},{2,10},{10... | collective-permute-start | bytes 786440 | tf_op jit(solution)/shard_map/ppermute | solution.py:13
  129.3 6.0 %collective-permute-start.5 = (f32[1]{0:T(128)}, f32[1]{0:T(128)}, u32[]{:S(2)}, u32[]{:S(2)}) collective-permute-start(f32[1]{0:T(128)} %param.9), channel_id=1, source_target_pairs={{0,8},{8,16},{16,24},{24,0},{1,9},{9,17},{17,25},{25,1},{2,10},{10... | collective-permute-start | bytes 20 | tf_op jit(solution)/shard_map/ppermute | solution.py:13
  139.7 56.2 %all-gather.7.cloned.1.call-start = ((), (), s32[]{:S(2)}) async-start(), calls=%async_computation.6 | async-start | bytes 1310720 | tf_op jit(solution)/shard_map/all_gather | solution.py:47
  140.3 85.2 %reduce-scatter.11.cloned.1.call-start = ((), (), s32[]{:S(2)}) async-start(), calls=%async_computation.11 | async-start | bytes 1310720 | tf_op jit(solution)/shard_map/reduce_scatter | solution.py:63
  166.5 1.9 copy-start.4
  169.1 10.8 %collective-permute-start.13 = (bf16[768,256]{1,0:T(8,128)(2,1)S(1)}, bf16[768,256]{1,0:T(8,128)(2,1)S(1)}, u32[]{:S(2)}, u32[]{:S(2)}) collective-permute-start(bf16[768,256]{1,0:T(8,128)(2,1)S(1)} %pad_maximum_fusion.3), channel_id=1, source_target_pairs={{0,1},{1,0},{2,3},{3,2},{4,5},{5,4},{6,7},{7,6},{8,9},{9,8},{10,11... | collective-permute-start | bytes 1179656 | tf_op jit(solution)/shard_map/ppermute | solution.py:56
  182.3 71.9 %reduce-scatter.7.cloned.1.call-start = ((), (), s32[]{:S(2)}) async-start(), calls=%async_computation.7 | async-start | bytes 1310720 | tf_op jit(solution)/shard_map/reduce_scatter | solution.py:63
  195.9 1.9 copy-start.3
  198.5 10.8 %collective-permute-start.6 = (bf16[768,256]{1,0:T(8,128)(2,1)S(1)}, bf16[768,256]{1,0:T(8,128)(2,1)S(1)}, u32[]{:S(2)}, u32[]{:S(2)}) collective-permute-start(bf16[768,256]{1,0:T(8,128)(2,1)S(1)} %pad_maximum_fusion.1), channel_id=1, source_target_pairs={{0,1},{1,0},{2,3},{3,2},{4,5},{5,4},{6,7},{7,6},{8,9},{9,8},{10,11... | collective-permute-start | bytes 1179656 | tf_op jit(solution)/shard_map/ppermute | solution.py:56
  210.1 3.3 %copy-start.6 = (f32[512,256]{1,0:T(8,128)S(1)}, f32[512,256]{1,0:T(8,128)}, u32[]{:S(2)}) copy-start(f32[512,256]{1,0:T(8,128)} %get-tuple-element.6) | copy-start | bytes 1572868
  210.1 54.0 %copy-start.8 = (bf16[512,256]{1,0:T(8,128)(2,1)S(1)}, bf16[512,256]{1,0:T(8,128)(2,1)}, u32[]{:S(2)}) copy-start(bf16[512,256]{1,0:T(8,128)(2,1)} %reduce-scatter.9.cloned.1.call-done) | copy-start | bytes 786436
  211.8 52.3 %copy-start = (f32[1,512,512]{2,1,0:T(8,128)S(1)}, f32[1,512,512]{2,1,0:T(8,128)}, u32[]{:S(2)}) copy-start(f32[1,512,512]{2,1,0:T(8,128)} %param.8) | copy-start | bytes 3145732
  211.8 51.2 %collective-permute-start.12 = (f32[512,256]{1,0:T(8,128)}, f32[512,256]{1,0:T(8,128)S(1)}, u32[]{:S(2)}, u32[]{:S(2)}) collective-permute-start(f32[512,256]{1,0:T(8,128)} %get-tuple-element.13), channel_id=1, source_target_pairs={{0,16},{8,24},{16,0},{24,8},{1,17},{9,25},{17,1},{25,9},{2,18},{10... | collective-permute-start | bytes 1572872 | tf_op jit(solution)/shard_map/ppermute | solution.py:13
  213.4 49.7 %collective-permute-start.4 = (f32[512,256]{1,0:T(8,128)S(1)}, f32[512,256]{1,0:T(8,128)S(1)}, u32[]{:S(2)}, u32[]{:S(2)}) collective-permute-start(f32[512,256]{1,0:T(8,128)S(1)} %copy-done.6), channel_id=1, source_target_pairs={{0,16},{8,24},{16,0},{24,8},{1,17},{9,25},{17,1},{25,9},{2,18},{10... | collective-permute-start | bytes 1572872 | tf_op jit(solution)/shard_map/ppermute | solution.py:13
  225.5 37.7 %collective-permute-start.14 = (bf16[512,256]{1,0:T(8,128)(2,1)}, bf16[512,256]{1,0:T(8,128)(2,1)S(1)}, u32[]{:S(2)}, u32[]{:S(2)}) collective-permute-start(bf16[512,256]{1,0:T(8,128)(2,1)} %reduce-scatter.11.cloned.1.call-done), channel_id=1, source_target_pairs={{0,16},{8,24},{16,0},{24,8},{1,17},{9,25},{17,1},{25,9},{2,18},{10... | collective-permute-start | bytes 786440 | tf_op jit(solution)/shard_map/ppermute | solution.py:13
  254.3 8.9 %collective-permute-start.7 = (bf16[512,256]{1,0:T(8,128)(2,1)}, bf16[512,256]{1,0:T(8,128)(2,1)S(1)}, u32[]{:S(2)}, u32[]{:S(2)}) collective-permute-start(bf16[512,256]{1,0:T(8,128)(2,1)} %reduce-scatter.7.cloned.1.call-done), channel_id=1, source_target_pairs={{0,16},{8,24},{16,0},{24,8},{1,17},{9,25},{17,1},{25,9},{2,18},{10... | collective-permute-start | bytes 786440 | tf_op jit(solution)/shard_map/ppermute | solution.py:13
  255.7 6.7 %collective-permute-start.8 = (f32[1]{0:T(128)}, f32[1]{0:T(128)}, u32[]{:S(2)}, u32[]{:S(2)}) collective-permute-start(f32[1]{0:T(128)} %add.104), channel_id=1, source_target_pairs={{0,16},{8,24},{16,0},{24,8},{1,17},{9,25},{17,1},{25,9},{2,18},{10... | collective-permute-start | bytes 20 | tf_op jit(solution)/shard_map/ppermute | solution.py:13
  (3 other events, 2.7 us)
Sparse Core Ops, SparseCore 0:
  10.9 30.6 all-gather.8
  43.7 27.4 all-gather.4
  74.0 26.6 reduce-scatter.8
  103.5 25.7 reduce-scatter.4
  139.8 26.5 all-gather.10
  168.5 27.4 all-gather.6
  198.8 26.6 reduce-scatter.10
  228.4 25.7 reduce-scatter.6

commit v2 on v1

--- a/solution.py
+++ b/solution.py
@@ -20,7 +20,9 @@
     count = lax.axis_size("fsdp")
     lane = lax.rem(lax.axis_index("fsdp"), 2)
     swap = [(i, i ^ 1) for i in range(count)]
-    lines = [list(range(0, count, 2)), list(range(1, count, 2))]
+    half = count // 2
+    order = list(range(0, half, 2)) + list(range(1, half, 2))
+    lines = [[2 * place + side for place in order] for side in range(2)]
     key_scale = width ** (-0.5)
     part = features // CHUNKS
 
@@ -35,11 +37,17 @@
     moment = [chunk(momentum[0], c) for c in range(CHUNKS)]
     target = [chunk(targets[0], c).astype(jnp.float32) for c in range(CHUNKS)]
 
-    columns = inputs.reshape(rows, count // 2, 2, width // count)
-    mine = lax.dynamic_index_in_dim(columns, lane, 2, keepdims=False)
-    theirs = lax.dynamic_index_in_dim(columns, 1 - lane, 2, keepdims=False)
-    mine = mine.reshape(rows, width // 2)
-    theirs = lax.ppermute(theirs.reshape(rows, width // 2), "fsdp", swap)
+    block = width // count
+
+    def half_columns(side):
+        pieces = [
+            lax.dynamic_slice_in_dim(inputs, (2 * place + side) * block, block, 1)
+            for place in order
+        ]
+        return jnp.concatenate(pieces, axis=1)
+
+    theirs = lax.ppermute(half_columns(1 - lane), "fsdp", swap)
+    mine = half_columns(lane)
 
     for step in range(STEPS):
         for c in range(CHUNKS):
@@ -71,6 +79,7 @@
             gradient = gradient.astype(jnp.float32)
             moment[c] = 0.9 * moment[c] + gradient
             state[c] = before - 0.1 * (gradient + behind)
+            state[c], moment[c] = lax.optimization_barrier((state[c], moment[c]))
     new_params = jnp.concatenate([s / weights[STEPS][0] for s in state], axis=1)
     return new_params[None], jnp.concatenate(moment, axis=1)[None]
 

time: 275 us -> 422 us (1.53)
  waiting for transfers between devices: 197 us -> 337 us
  starting transfers between devices: 23.8 us -> 29.4 us
    all_gather x4, waiting for transfers between devices: 40.6 us -> 129 us  [shards(): lax.all_gather(debiased, 'fsdp', axis=0, tiled=True, axis_index_groups=li...]
    reduce_scatter x4, waiting for transfers between devices: 79.4 us -> 146 us  [shards(): lax.psum_scatter(partial.astype(jnp.bfloat16), 'fsdp', scatter_dimension=...]
    ppermute x1, waiting for transfers between devices: 34.5 us -> 0.01 us  [shards(): theirs = lax.ppermute(half_columns(1 - lane), 'fsdp', swap)]
    ppermute x10, waiting for transfers between devices: 5.39 us -> 25.1 us  [from_behind(): return lax.ppermute(value, axis, pairs)]
    ppermute x10, starting transfers between devices: 14 us -> 19.7 us  [from_behind(): return lax.ppermute(value, axis, pairs)]
  transfers between devices with their start and end apart: 23 -> 23, of which waited for: 14 -> 16; matrix products, arithmetic and copies ran while one was open for 10% -> 7% of each run, Pallas kernels for 0% -> 0%
where the time goes in v2:
time: 422 us
  waiting for transfers between devices  337 us (80%)
  starting transfers between devices  29.4 us (7%)
  matrix products  21.7 us (5%)
  between operations  16.6 us (4%)
  other arithmetic  14.1 us (3%)
    reduce_scatter x4, waiting for transfers between devices, shards(): lax.psum_scatter(partial.astype(jnp.bfloat16), 'fsdp', scatter_dimension=...  146 us
    all_gather x4, waiting for transfers between devices, shards(): lax.all_gather(debiased, 'fsdp', axis=0, tiled=True, axis_index_groups=li...  129 us
    ppermute x4, waiting for transfers between devices, shards(): got = lax.ppermute(sent, 'fsdp', swap).astype(jnp.float32)  37.5 us
    ppermute x10, waiting for transfers between devices, from_behind(): return lax.ppermute(value, axis, pairs)  25.1 us
    ppermute x10, starting transfers between devices, from_behind(): return lax.ppermute(value, axis, pairs)  19.7 us
  transfers between devices with their start and end apart: 23, of which 16 were waited for; matrix products, arithmetic and copies ran while one was open for 7% of the time, Pallas kernels for 0%

profile of v2, /device:TPU:0, one launch (start us, length us, event | category | flops | bytes accessed | tf_op | source)
XLA Modules:
  0.0 422.0 jit_solution(80098625307277017)
XLA Ops:
  7.9 2.1 divide_convert_fusion.3
  10.0 3.1 dynamic-slice_bitcast_fusion.3
  13.3 3.0 collective-permute-start.1
  16.4 41.1 %all-gather.5.cloned.1.call-done = bf16[2048,256]{1,0:T(8,128)(2,1)} async-done(((bf16[512,256]{1,0:T(8,128)(2,1)}), bf16[2048,256]{1,0:T(8,128)(2,1)}) %all-gather.5.cloned.1.call-update) | async-done | bytes 1048592 | tf_op jit(solution)/shard_map/all_gather | solution.py:55
  57.5 1.9 fusion.63
  61.9 9.4 %collective-permute-done.2 = bf16[768,256]{1,0:T(8,128)(2,1)S(1)} collective-permute-done((bf16[768,256]{1,0:T(8,128)(2,1)S(1)}, bf16[768,256]{1,0:T(8,128)(2,1)S(1)}, u32[]{:S(2)}, u32[]{:S(2)}) %collective-permute-start.2) | collective-permute-done | bytes 393248 | tf_op jit(solution)/shard_map/ppermute | solution.py:64
  72.1 1.8 fusion
  74.0 28.1 %all-gather.9.cloned.1.call-done = bf16[2048,256]{1,0:T(8,128)(2,1)} async-done(((bf16[512,256]{1,0:T(8,128)(2,1)}), bf16[2048,256]{1,0:T(8,128)(2,1)}) %all-gather.9.cloned.1.call-update) | async-done | bytes 1048592 | tf_op jit(solution)/shard_map/all_gather | solution.py:55
  102.0 1.9 fusion.61
  107.1 9.4 %collective-permute-done.10 = bf16[768,256]{1,0:T(8,128)(2,1)S(1)} collective-permute-done((bf16[768,256]{1,0:T(8,128)(2,1)S(1)}, bf16[768,256]{1,0:T(8,128)(2,1)S(1)}, u32[]{:S(2)}, u32[]{:S(2)}) %collective-permute-start.10) | collective-permute-done | bytes 393248 | tf_op jit(solution)/shard_map/ppermute | solution.py:64
  117.3 1.8 fusion.2
  119.1 27.7 %reduce-scatter.5.cloned.1.call-done = bf16[512,256]{1,0:T(8,128)(2,1)} async-done(((bf16[2048,256]{1,0:T(8,128)(2,1)}), bf16[512,256]{1,0:T(8,128)(2,1)}) %reduce-scatter.5.cloned.1.call-update) | async-done | bytes 262160 | tf_op jit(solution)/shard_map/reduce_scatter | solution.py:71
  146.8 46.4 %reduce-scatter.9.cloned.1.call-done = bf16[512,256]{1,0:T(8,128)(2,1)} async-done(((bf16[2048,256]{1,0:T(8,128)(2,1)}), bf16[512,256]{1,0:T(8,128)(2,1)}) %reduce-scatter.9.cloned.1.call-update) | async-done | bytes 262160 | tf_op jit(solution)/shard_map/reduce_scatter | solution.py:71
  193.2 2.6 convert_add_fusion.6
  195.8 1.6 collective-permute-start.3
  197.4 9.8 %collective-permute-done.5 = f32[1]{0:T(128)} collective-permute-done((f32[1]{0:T(128)}, f32[1]{0:T(128)}, u32[]{:S(2)}, u32[]{:S(2)}) %collective-permute-start.5) | collective-permute-done | bytes 36 | tf_op jit(solution)/shard_map/ppermute | solution.py:13
  208.9 1.6 collective-permute-start.11
  210.5 9.8 %collective-permute-done.11 = bf16[512,256]{1,0:T(8,128)(2,1)S(1)} collective-permute-done((bf16[512,256]{1,0:T(8,128)(2,1)S(1)}, bf16[512,256]{1,0:T(8,128)(2,1)S(1)}, u32[]{:S(2)}, u32[]{:S(2)}) %collective-permute-start.11) | collective-permute-done | bytes 262176 | tf_op jit(solution)/shard_map/ppermute | solution.py:13
  222.3 31.2 %all-gather.7.cloned.1.call-done = bf16[2048,256]{1,0:T(8,128)(2,1)} async-done(((bf16[512,256]{1,0:T(8,128)(2,1)}), bf16[2048,256]{1,0:T(8,128)(2,1)}) %all-gather.7.cloned.1.call-update) | async-done | bytes 1048592 | tf_op jit(solution)/shard_map/all_gather | solution.py:55
  253.6 2.0 fusion.67
  257.9 9.4 %collective-permute-done.6 = bf16[768,256]{1,0:T(8,128)(2,1)S(1)} collective-permute-done((bf16[768,256]{1,0:T(8,128)(2,1)S(1)}, bf16[768,256]{1,0:T(8,128)(2,1)S(1)}, u32[]{:S(2)}, u32[]{:S(2)}) %collective-permute-start.6) | collective-permute-done | bytes 393248 | tf_op jit(solution)/shard_map/ppermute | solution.py:64
  268.1 1.8 fusion.1
  270.2 28.4 %all-gather.11.cloned.1.call-done = bf16[2048,256]{1,0:T(8,128)(2,1)} async-done(((bf16[512,256]{1,0:T(8,128)(2,1)}), bf16[2048,256]{1,0:T(8,128)(2,1)}) %all-gather.11.cloned.1.call-update) | async-done | bytes 1048592 | tf_op jit(solution)/shard_map/all_gather | solution.py:55
  298.6 1.9 fusion.65
  302.9 9.4 %collective-permute-done.13 = bf16[768,256]{1,0:T(8,128)(2,1)S(1)} collective-permute-done((bf16[768,256]{1,0:T(8,128)(2,1)S(1)}, bf16[768,256]{1,0:T(8,128)(2,1)S(1)}, u32[]{:S(2)}, u32[]{:S(2)}) %collective-permute-start.13) | collective-permute-done | bytes 393248 | tf_op jit(solution)/shard_map/ppermute | solution.py:64
  313.1 1.8 fusion.3
  314.9 28.4 %reduce-scatter.7.cloned.1.call-done = bf16[512,256]{1,0:T(8,128)(2,1)} async-done(((bf16[2048,256]{1,0:T(8,128)(2,1)}), bf16[512,256]{1,0:T(8,128)(2,1)}) %reduce-scatter.7.cloned.1.call-update) | async-done | bytes 262160 | tf_op jit(solution)/shard_map/reduce_scatter | solution.py:71
  344.6 1.5 collective-permute-start.4
  346.7 43.1 %reduce-scatter.11.cloned.1.call-done = bf16[512,256]{1,0:T(8,128)(2,1)} async-done(((bf16[2048,256]{1,0:T(8,128)(2,1)}), bf16[512,256]{1,0:T(8,128)(2,1)}) %reduce-scatter.11.cloned.1.call-update) | async-done | bytes 262160 | tf_op jit(solution)/shard_map/reduce_scatter | solution.py:71
  391.0 1.5 collective-permute-start.12
  392.5 11.3 %collective-permute-start.8 = (f32[1]{0:T(128)}, f32[1]{0:T(128)}, u32[]{:S(2)}, u32[]{:S(2)}) collective-permute-start(f32[1]{0:T(128)} %add.153), channel_id=1, source_target_pairs={{0,16},{8,24},{16,0},{24,8},{1,17},{9,25},{17,1},{25,9},{2,18},{10... | collective-permute-start | bytes 20 | tf_op jit(solution)/shard_map/ppermute | solution.py:13
  408.4 4.3 %collective-permute-done.14 = bf16[512,256]{1,0:T(8,128)(2,1)S(1)} collective-permute-done((bf16[512,256]{1,0:T(8,128)(2,1)S(1)}, bf16[512,256]{1,0:T(8,128)(2,1)S(1)}, u32[]{:S(2)}, u32[]{:S(2)}) %collective-permute-start.14) | collective-permute-done | bytes 262176 | tf_op jit(solution)/shard_map/ppermute | solution.py:13
  (115 shorter events, 26.6 us)
Async XLA Ops:
  7.2 50.3 %all-gather.5.cloned.1.call-start = ((), (), s32[]{:S(2)}) async-start(), calls=%async_computation.4 | async-start | bytes 1310720 | tf_op jit(solution)/shard_map/all_gather | solution.py:55
  10.0 92.1 %all-gather.9.cloned.1.call-start = ((), (), s32[]{:S(2)}) async-start(), calls=%async_computation.8 | async-start | bytes 1310720 | tf_op jit(solution)/shard_map/all_gather | solution.py:55
  13.1 103.4 %copy-start.6 = (bf16[384,512]{1,0:T(8,128)(2,1)}, bf16[384,512]{1,0:T(8,128)(2,1)S(1)}, u32[]{:S(2)}) copy-start(bf16[384,512]{1,0:T(8,128)(2,1)S(1)} %get-tuple-element.20) | copy-start | bytes 1179652
  13.3 44.2 %collective-permute-start.1 = (bf16[384,2048]{1,0:T(8,128)(2,1)S(1)}, bf16[384,2048]{1,0:T(8,128)(2,1)S(1)}, u32[]{:S(2)}, u32[]{:S(2)}) collective-permute-start(bf16[384,2048]{1,0:T(8,128)(2,1)S(1)} %pad_maximum_fusion.1), channel_id=1, source_target_pairs={{0,1},{1,0},{2,3},{3,2},{4,5},{5,4},{6,7},{7,6},{8,9},{9,8},{10,11... | collective-permute-start | bytes 4718600 | tf_op jit(solution)/shard_map/ppermute | solution.py:49
  16.3 130.5 %reduce-scatter.5.cloned.1.call-start = ((), (), s32[]{:S(2)}) async-start(), calls=%async_computation.5 | async-start | bytes 1310720 | tf_op jit(solution)/shard_map/reduce_scatter | solution.py:71
  60.4 10.9 %collective-permute-start.2 = (bf16[768,256]{1,0:T(8,128)(2,1)S(1)}, bf16[768,256]{1,0:T(8,128)(2,1)S(1)}, u32[]{:S(2)}, u32[]{:S(2)}) collective-permute-start(bf16[768,256]{1,0:T(8,128)(2,1)S(1)} %pad_maximum_fusion.2), channel_id=1, source_target_pairs={{0,1},{1,0},{2,3},{3,2},{4,5},{5,4},{6,7},{7,6},{8,9},{9,8},{10,11... | collective-permute-start | bytes 1179656 | tf_op jit(solution)/shard_map/ppermute | solution.py:64
  73.9 30.0 %copy-start.9 = (bf16[384,512]{1,0:T(8,128)(2,1)S(1)}, bf16[384,512]{1,0:T(8,128)(2,1)}, u32[]{:S(2)}) copy-start(bf16[384,512]{1,0:T(8,128)(2,1)} %get-tuple-element.21) | copy-start | bytes 1179652
  73.9 30.0 %copy-start.13 = (bf16[384,512]{1,0:T(8,128)(2,1)S(1)}, bf16[384,512]{1,0:T(8,128)(2,1)}, u32[]{:S(2)}) copy-start(bf16[384,512]{1,0:T(8,128)(2,1)} %get-tuple-element.22) | copy-start | bytes 1179652
  73.9 30.0 %copy-start.17 = (bf16[384,512]{1,0:T(8,128)(2,1)S(1)}, bf16[384,512]{1,0:T(8,128)(2,1)}, u32[]{:S(2)}) copy-start(bf16[384,512]{1,0:T(8,128)(2,1)} %get-tuple-element.23) | copy-start | bytes 1179652
  73.9 119.3 %reduce-scatter.9.cloned.1.call-start = ((), (), s32[]{:S(2)}) async-start(), calls=%async_computation.9 | async-start | bytes 1310720 | tf_op jit(solution)/shard_map/reduce_scatter | solution.py:71
  105.5 10.9 %collective-permute-start.10 = (bf16[768,256]{1,0:T(8,128)(2,1)S(1)}, bf16[768,256]{1,0:T(8,128)(2,1)S(1)}, u32[]{:S(2)}, u32[]{:S(2)}) collective-permute-start(bf16[768,256]{1,0:T(8,128)(2,1)S(1)} %pad_maximum_fusion.4), channel_id=1, source_target_pairs={{0,1},{1,0},{2,3},{3,2},{4,5},{5,4},{6,7},{7,6},{8,9},{9,8},{10,11... | collective-permute-start | bytes 1179656 | tf_op jit(solution)/shard_map/ppermute | solution.py:64
  117.3 75.9 %copy-start = (f32[1,512,512]{2,1,0:T(8,128)S(1)}, f32[1,512,512]{2,1,0:T(8,128)}, u32[]{:S(2)}) copy-start(f32[1,512,512]{2,1,0:T(8,128)} %param.7) | copy-start | bytes 3145732
  119.1 134.4 %all-gather.7.cloned.1.call-start = ((), (), s32[]{:S(2)}) async-start(), calls=%async_computation.6 | async-start | bytes 1310720 | tf_op jit(solution)/shard_map/all_gather | solution.py:55
  195.8 13.1 %copy-start.1 = (f32[512,256]{1,0:T(8,128)S(1)}, f32[512,256]{1,0:T(8,128)}, u32[]{:S(2)}) copy-start(f32[512,256]{1,0:T(8,128)} %get-tuple-element.30) | copy-start | bytes 1572868
  195.8 13.1 %copy-start.4 = (bf16[512,256]{1,0:T(8,128)(2,1)S(1)}, bf16[512,256]{1,0:T(8,128)(2,1)}, u32[]{:S(2)}) copy-start(bf16[512,256]{1,0:T(8,128)(2,1)} %reduce-scatter.9.cloned.1.call-done) | copy-start | bytes 786436
  195.8 12.1 %collective-permute-start = (f32[512,256]{1,0:T(8,128)S(1)}, f32[512,256]{1,0:T(8,128)S(1)}, u32[]{:S(2)}, u32[]{:S(2)}) collective-permute-start(f32[512,256]{1,0:T(8,128)S(1)} %get-tuple-element.31), channel_id=1, source_target_pairs={{0,8},{8,16},{16,24},{24,0},{1,9},{9,17},{17,25},{25,1},{2,10},{10... | collective-permute-start | bytes 1572872 | tf_op jit(solution)/shard_map/ppermute | solution.py:13
  195.8 12.1 %collective-permute-start.3 = (bf16[512,256]{1,0:T(8,128)(2,1)S(1)}, bf16[512,256]{1,0:T(8,128)(2,1)S(1)}, u32[]{:S(2)}, u32[]{:S(2)}) collective-permute-start(bf16[512,256]{1,0:T(8,128)(2,1)S(1)} %copy-done.3), channel_id=1, source_target_pairs={{0,8},{8,16},{16,24},{24,0},{1,9},{9,17},{17,25},{25,1},{2,10},{10... | collective-permute-start | bytes 786440 | tf_op jit(solution)/shard_map/ppermute | solution.py:13
  197.4 9.8 %collective-permute-start.5 = (f32[1]{0:T(128)}, f32[1]{0:T(128)}, u32[]{:S(2)}, u32[]{:S(2)}) collective-permute-start(f32[1]{0:T(128)} %param.9), channel_id=1, source_target_pairs={{0,8},{8,16},{16,24},{24,0},{1,9},{9,17},{17,25},{25,1},{2,10},{10... | collective-permute-start | bytes 20 | tf_op jit(solution)/shard_map/ppermute | solution.py:13
  208.8 89.8 %all-gather.11.cloned.1.call-start = ((), (), s32[]{:S(2)}) async-start(), calls=%async_computation.10 | async-start | bytes 1310720 | tf_op jit(solution)/shard_map/all_gather | solution.py:55
  208.8 11.5 %collective-permute-start.9 = (f32[512,256]{1,0:T(8,128)S(1)}, f32[512,256]{1,0:T(8,128)S(1)}, u32[]{:S(2)}, u32[]{:S(2)}) collective-permute-start(f32[512,256]{1,0:T(8,128)S(1)} %copy-done.1), channel_id=1, source_target_pairs={{0,8},{8,16},{16,24},{24,0},{1,9},{9,17},{17,25},{25,1},{2,10},{10... | collective-permute-start | bytes 1572872 | tf_op jit(solution)/shard_map/ppermute | solution.py:13
  208.9 11.4 %collective-permute-start.11 = (bf16[512,256]{1,0:T(8,128)(2,1)S(1)}, bf16[512,256]{1,0:T(8,128)(2,1)S(1)}, u32[]{:S(2)}, u32[]{:S(2)}) collective-permute-start(bf16[512,256]{1,0:T(8,128)(2,1)S(1)} %copy-done.4), channel_id=1, source_target_pairs={{0,8},{8,16},{16,24},{24,0},{1,9},{9,17},{17,25},{25,1},{2,10},{10... | collective-permute-start | bytes 786440 | tf_op jit(solution)/shard_map/ppermute | solution.py:13
  222.2 33.3 %copy-start.7 = (bf16[384,512]{1,0:T(8,128)(2,1)S(1)}, bf16[384,512]{1,0:T(8,128)(2,1)}, u32[]{:S(2)}) copy-start(bf16[384,512]{1,0:T(8,128)(2,1)} %copy-done.6) | copy-start | bytes 1179652
  222.2 121.1 %reduce-scatter.7.cloned.1.call-start = ((), (), s32[]{:S(2)}) async-start(), calls=%async_computation.7 | async-start | bytes 1310720 | tf_op jit(solution)/shard_map/reduce_scatter | solution.py:71
  256.4 10.9 %collective-permute-start.6 = (bf16[768,256]{1,0:T(8,128)(2,1)S(1)}, bf16[768,256]{1,0:T(8,128)(2,1)S(1)}, u32[]{:S(2)}, u32[]{:S(2)}) collective-permute-start(bf16[768,256]{1,0:T(8,128)(2,1)S(1)} %pad_maximum_fusion.3), channel_id=1, source_target_pairs={{0,1},{1,0},{2,3},{3,2},{4,5},{5,4},{6,7},{7,6},{8,9},{9,8},{10,11... | collective-permute-start | bytes 1179656 | tf_op jit(solution)/shard_map/ppermute | solution.py:64
  269.9 119.9 %reduce-scatter.11.cloned.1.call-start = ((), (), s32[]{:S(2)}) async-start(), calls=%async_computation.11 | async-start | bytes 1310720 | tf_op jit(solution)/shard_map/reduce_scatter | solution.py:71
  301.4 10.9 %collective-permute-start.13 = (bf16[768,256]{1,0:T(8,128)(2,1)S(1)}, bf16[768,256]{1,0:T(8,128)(2,1)S(1)}, u32[]{:S(2)}, u32[]{:S(2)}) collective-permute-start(bf16[768,256]{1,0:T(8,128)(2,1)S(1)} %pad_maximum_fusion.5), channel_id=1, source_target_pairs={{0,1},{1,0},{2,3},{3,2},{4,5},{5,4},{6,7},{7,6},{8,9},{9,8},{10,11... | collective-permute-start | bytes 1179656 | tf_op jit(solution)/shard_map/ppermute | solution.py:64
  344.6 62.5 %collective-permute-start.4 = (f32[512,256]{1,0:T(8,128)S(1)}, f32[512,256]{1,0:T(8,128)}, u32[]{:S(2)}, u32[]{:S(2)}) collective-permute-start(f32[512,256]{1,0:T(8,128)S(1)} %get-tuple-element.35), channel_id=1, source_target_pairs={{0,16},{8,24},{16,0},{24,8},{1,17},{9,25},{17,1},{25,9},{2,18},{10... | collective-permute-start | bytes 1572872 | tf_op jit(solution)/shard_map/ppermute | solution.py:13
  346.1 61.0 %collective-permute-start.7 = (bf16[512,256]{1,0:T(8,128)(2,1)S(1)}, bf16[512,256]{1,0:T(8,128)(2,1)}, u32[]{:S(2)}, u32[]{:S(2)}) collective-permute-start(bf16[512,256]{1,0:T(8,128)(2,1)S(1)} %copy-done.2), channel_id=1, source_target_pairs={{0,16},{8,24},{16,0},{24,8},{1,17},{9,25},{17,1},{25,9},{2,18},{10... | collective-permute-start | bytes 786440 | tf_op jit(solution)/shard_map/ppermute | solution.py:13
  389.8 15.7 %copy-start.5 = (bf16[512,256]{1,0:T(8,128)(2,1)S(1)}, bf16[512,256]{1,0:T(8,128)(2,1)}, u32[]{:S(2)}) copy-start(bf16[512,256]{1,0:T(8,128)(2,1)} %reduce-scatter.11.cloned.1.call-done) | copy-start | bytes 786436
  391.0 21.7 %collective-permute-start.12 = (f32[512,256]{1,0:T(8,128)S(1)}, f32[512,256]{1,0:T(8,128)S(1)}, u32[]{:S(2)}, u32[]{:S(2)}) collective-permute-start(f32[512,256]{1,0:T(8,128)S(1)} %get-tuple-element.37), channel_id=1, source_target_pairs={{0,16},{8,24},{16,0},{24,8},{1,17},{9,25},{17,1},{25,9},{2,18},{10... | collective-permute-start | bytes 1572872 | tf_op jit(solution)/shard_map/ppermute | solution.py:13
  392.5 12.4 %collective-permute-start.8 = (f32[1]{0:T(128)}, f32[1]{0:T(128)}, u32[]{:S(2)}, u32[]{:S(2)}) collective-permute-start(f32[1]{0:T(128)} %add.153), channel_id=1, source_target_pairs={{0,16},{8,24},{16,0},{24,8},{1,17},{9,25},{17,1},{25,9},{2,18},{10... | collective-permute-start | bytes 20 | tf_op jit(solution)/shard_map/ppermute | solution.py:13
  405.6 7.1 %collective-permute-start.14 = (bf16[512,256]{1,0:T(8,128)(2,1)S(1)}, bf16[512,256]{1,0:T(8,128)(2,1)S(1)}, u32[]{:S(2)}, u32[]{:S(2)}) collective-permute-start(bf16[512,256]{1,0:T(8,128)(2,1)S(1)} %copy-done.5), channel_id=1, source_target_pairs={{0,16},{8,24},{16,0},{24,8},{1,17},{9,25},{17,1},{25,9},{2,18},{10... | collective-permute-start | bytes 786440 | tf_op jit(solution)/shard_map/ppermute | solution.py:13
  (18 other events, 37.3 us)
Sparse Core Ops, SparseCore 0:
  10.1 47.3 all-gather.4
  59.0 42.9 all-gather.8
  104.9 41.8 reduce-scatter.4
  149.6 43.5 reduce-scatter.8
  208.9 44.5 all-gather.6
  255.5 42.9 all-gather.10
  301.4 41.8 reduce-scatter.6
  346.3 43.5 reduce-scatter.10

commit v3 on v1

v3 whole, which is shorter than its diff:
```python
import jax
import jax.numpy as jnp
from jax import lax
from jax.sharding import PartitionSpec as P

STEPS = 2
CHUNKS = 2


def from_behind(value, axis, steps):
    count = lax.axis_size(axis)
    pairs = [(source, (source + steps) % count) for source in range(count)]
    return lax.ppermute(value, axis, pairs)


def shards(tokens, targets, params, momentum, push_weight):
    inputs = tokens[0]
    rows, width = inputs.shape
    features = params.shape[2]
    count = lax.axis_size("fsdp")
    half = count // 2
    block = width // count
    place = lax.div(lax.axis_index("fsdp"), 2)
    lane = lax.rem(lax.axis_index("fsdp"), 2)
    swap = [(i, i ^ 1) for i in range(count)]
    key_scale = width ** (-0.5)
    part = features // CHUNKS
    contract = (((0,), (0,)), ((), ()))

    def chunk(array, c):
        return array[:, c * part : (c + 1) * part]

    def half_columns(side):
        pieces = []
        for back in range(half):
            start = (2 * lax.rem(place - back + half, half) + side) * block
            pieces.append(lax.dynamic_slice_in_dim(inputs, start, block, 1))
        return jnp.concatenate(pieces, axis=1)

    theirs = lax.ppermute(half_columns(1 - lane), "fsdp", swap)
    mine = half_columns(lane)

    weights = [push_weight]
    for step in range(STEPS):
        weights.append(0.5 * weights[-1] + 0.5 * from_behind(weights[-1], "group", 2**step))

    state = [chunk(params[0], c) for c in range(CHUNKS)]
    moment = [chunk(momentum[0], c) for c in range(CHUNKS)]
    target = [chunk(targets[0], c).astype(jnp.float32) for c in range(CHUNKS)]

    for step in range(STEPS):
        before = []
        for c in range(CHUNKS):
            own = state[c] - (0.2 * 0.9) * moment[c]
            before.append(0.5 * (own + from_behind(own, "group", 2**step)))
        for c in range(CHUNKS):
            rows_in = (state[c] / weights[step][0]).astype(jnp.bfloat16)
            own = -target[c]
            other = 0.0
            for back in range(half):
                columns = slice(back * block, (back + 1) * block)
                own = own + key_scale * jnp.dot(
                    mine[:, columns], rows_in, preferred_element_type=jnp.float32
                )
                other = other + key_scale * jnp.dot(
                    theirs[:, columns], rows_in, preferred_element_type=jnp.float32
                )
                if back < half - 1:
                    rows_in = from_behind(rows_in, "fsdp", 2)
            sent = jnp.concatenate([other, own]).astype(jnp.bfloat16)
            got = lax.ppermute(sent, "fsdp", swap).astype(jnp.float32)
            own_grad = (key_scale * (own + got[:rows])).astype(jnp.bfloat16)
            other_grad = (key_scale * (other + got[rows:])).astype(jnp.bfloat16)

            def partial(back):
                columns = slice(back * block, (back + 1) * block)
                return lax.dot_general(
                    mine[:, columns], own_grad, contract, preferred_element_type=jnp.float32
                ) + lax.dot_general(
                    theirs[:, columns], other_grad, contract, preferred_element_type=jnp.float32
                )

            total = partial(1)
            for back in range(2, half + 1):
                total = from_behind(total.astype(jnp.bfloat16), "fsdp", 2)
                total = total.astype(jnp.float32) + partial(back % half)
            behind = from_behind(total.astype(jnp.bfloat16), "group", 2**step)
            moment[c] = 0.9 * moment[c] + total
            state[c] = before[c] - 0.1 * (total + behind.astype(jnp.float32))
            state[c], moment[c] = lax.optimization_barrier((state[c], moment[c]))
    new_params = jnp.concatenate([s / weights[STEPS][0] for s in state], axis=1)
    return new_params[None], jnp.concatenate(moment, axis=1)[None]


def solution(mesh):
    return jax.shard_map(
        shards,
        mesh=mesh,
        in_specs=(
            P("group", "fsdp", None),
            P("group", "fsdp", None),
            P("group", "fsdp", None),
            P("group", "fsdp", None),
            P("group"),
        ),
        out_specs=(P("group", "fsdp", None), P("group", "fsdp", None)),
        check_vma=False,
    )
```

time: 275 us -> 225 us (0.82)
  waiting for transfers between devices: 197 us -> 163 us
  between operations: 16.4 us -> 3.25 us
  matrix products: 19.8 us -> 25.5 us
  local copies, waits for them, and re-layouts: 7.18 us -> 1.54 us
  other arithmetic: 10.6 us -> 6.59 us
    ppermute x10 -> x34, waiting for transfers between devices: 5.39 us -> 137 us  [from_behind(): return lax.ppermute(value, axis, pairs)]
    reduce_scatter x4 -> x0, waiting for transfers between devices: 79.4 us -> none  [shards(): lax.psum_scatter(partial.astype(jnp.bfloat16), 'fsdp', scatter_dimension=...]
    all_gather x4 -> x0, waiting for transfers between devices: 40.6 us -> none  [shards(): lax.all_gather(debiased, 'fsdp', axis=0, tiled=True, axis_index_groups=li...]
    ppermute x1, waiting for transfers between devices: 34.5 us -> 3.61 us  [shards(): theirs = lax.ppermute(half_columns(1 - lane), 'fsdp', swap)]
    ppermute x4, waiting for transfers between devices: 36.3 us -> 22.4 us  [shards(): got = lax.ppermute(sent, 'fsdp', swap).astype(jnp.float32)]
    sub x2 -> x4, other arithmetic: 6.56 us -> 0.44 us  [the longest x2 0.28 us: shards(): state[c] = before[c] - 0.1 * (total + behind.astype(jnp.float32))]
    dot_general x16 -> x64, matrix products: 19.8 us -> 25.5 us  [the longest x16 9.31 us: shards(): jnp.dot(mine[:, columns], rows_in, preferred_element_type=jnp.float32)]
    unnamed x25 -> x8, local copies, waits for them, and re-layouts: 3.82 us -> 0.02 us
  transfers between devices with their start and end apart: 23 -> 39, of which waited for: 14 -> 34; matrix products, arithmetic and copies ran while one was open for 10% -> 12% of each run, Pallas kernels for 0% -> 0%
where the time goes in v3:
time: 225 us; the launch traced here: 224 us
  waiting for transfers between devices  163 us (72%)
  matrix products  25.5 us (11%)
  starting transfers between devices  24.3 us (11%)
  other arithmetic  6.59 us (3%)
  between operations  3.25 us (1%)
    ppermute x34, waiting for transfers between devices, from_behind(): return lax.ppermute(value, axis, pairs)  137 us
    ppermute x4, waiting for transfers between devices, shards(): got = lax.ppermute(sent, 'fsdp', swap).astype(jnp.float32)  22.4 us
    ppermute x34, starting transfers between devices, from_behind(): return lax.ppermute(value, axis, pairs)  17.5 us
    dot_general x16, matrix products, shards(): jnp.dot(mine[:, columns], rows_in, preferred_element_type=jnp.float32)  9.31 us
    dot_general x16, matrix products, partial(): lax.dot_general(mine[:, columns], own_grad, contract, preferred_element_t...  5.54 us
    dot_general x16, matrix products, partial(): lax.dot_general(theirs[:, columns], other_grad, contract, preferred_eleme...  5.51 us
    ppermute x4, starting transfers between devices, shards(): got = lax.ppermute(sent, 'fsdp', swap).astype(jnp.float32)  5.27 us
    dot_general x16, matrix products, shards(): jnp.dot(theirs[:, columns], rows_in, preferred_element_type=jnp.float32)  5.16 us
  transfers between devices with their start and end apart: 39, of which 34 were waited for; matrix products, arithmetic and copies ran while one was open for 12% of the time, Pallas kernels for 0%

profile of v3, /device:TPU:0, one launch (start us, length us, event | category | flops | bytes accessed | tf_op | source)
XLA Modules:
  0.0 224.4 jit_solution(13241584770606125001)
XLA Ops:
  2.6 3.1 %collective-permute-start.1 = (bf16[512,256]{1,0:T(8,128)(2,1)S(1)}, bf16[512,256]{1,0:T(8,128)(2,1)S(1)}, u32[]{:S(2)}, u32[]{:S(2)}) collective-permute-start(bf16[512,256]{1,0:T(8,128)(2,1)S(1)} %get-tuple-element.28), channel_id=1, source_target_pairs={{0,2},{1,3},{2,4},{3,5},{4,6},{5,7},{6,0},{7,1},{8,10},{9,11},{10,... | collective-permute-start | bytes 786440 | tf_op jit(solution)/shard_map/ppermute | solution.py:13
  15.9 4.7 %collective-permute-done.22 = bf16[512,256]{1,0:T(8,128)(2,1)} collective-permute-done((bf16[512,256]{1,0:T(8,128)(2,1)S(1)}, bf16[512,256]{1,0:T(8,128)(2,1)}, u32[]{:S(2)}, u32[]{:S(2)}) %collective-permute-start.22) | collective-permute-done | bytes 262176 | tf_op jit(solution)/shard_map/ppermute | solution.py:13
  23.2 2.9 %collective-permute-done.2 = bf16[512,256]{1,0:T(8,128)(2,1)S(1)} collective-permute-done((bf16[512,256]{1,0:T(8,128)(2,1)S(1)}, bf16[512,256]{1,0:T(8,128)(2,1)S(1)}, u32[]{:S(2)}, u32[]{:S(2)}) %collective-permute-start.2) | collective-permute-done | bytes 262176 | tf_op jit(solution)/shard_map/ppermute | solution.py:13
  26.1 5.7 %collective-permute-done.23 = bf16[512,256]{1,0:T(8,128)(2,1)S(1)} collective-permute-done((bf16[512,256]{1,0:T(8,128)(2,1)}, bf16[512,256]{1,0:T(8,128)(2,1)S(1)}, u32[]{:S(2)}, u32[]{:S(2)}) %collective-permute-start.23) | collective-permute-done | bytes 262176 | tf_op jit(solution)/shard_map/ppermute | solution.py:13
  33.3 4.1 %collective-permute-done.3 = bf16[512,256]{1,0:T(8,128)(2,1)S(1)} collective-permute-done((bf16[512,256]{1,0:T(8,128)(2,1)S(1)}, bf16[512,256]{1,0:T(8,128)(2,1)S(1)}, u32[]{:S(2)}, u32[]{:S(2)}) %collective-permute-start.3) | collective-permute-done | bytes 262176 | tf_op jit(solution)/shard_map/ppermute | solution.py:13
  37.7 4.4 %collective-permute-done.24 = bf16[512,256]{1,0:T(8,128)(2,1)S(1)} collective-permute-done((bf16[512,256]{1,0:T(8,128)(2,1)S(1)}, bf16[512,256]{1,0:T(8,128)(2,1)S(1)}, u32[]{:S(2)}, u32[]{:S(2)}) %collective-permute-start.24) | collective-permute-done | bytes 262176 | tf_op jit(solution)/shard_map/ppermute | solution.py:13
  42.3 3.6 %collective-permute-done.4 = bf16[384,2048]{1,0:T(8,128)(2,1)S(1)} collective-permute-done((bf16[384,2048]{1,0:T(8,128)(2,1)}, bf16[384,2048]{1,0:T(8,128)(2,1)S(1)}, u32[]{:S(2)}, u32[]{:S(2)}) %collective-permute-start.4) | collective-permute-done | bytes 1572896 | tf_op jit(solution)/shard_map/ppermute | solution.py:40
  51.3 8.8 %collective-permute-done.25 = bf16[768,256]{1,0:T(8,128)(2,1)S(1)} collective-permute-done((bf16[768,256]{1,0:T(8,128)(2,1)S(1)}, bf16[768,256]{1,0:T(8,128)(2,1)S(1)}, u32[]{:S(2)}, u32[]{:S(2)}) %collective-permute-start.25) | collective-permute-done | bytes 393248 | tf_op jit(solution)/shard_map/ppermute | solution.py:71
  61.7 4.1 %collective-permute-done.5 = bf16[768,256]{1,0:T(8,128)(2,1)S(1)} collective-permute-done((bf16[768,256]{1,0:T(8,128)(2,1)S(1)}, bf16[768,256]{1,0:T(8,128)(2,1)S(1)}, u32[]{:S(2)}, u32[]{:S(2)}) %collective-permute-start.5) | collective-permute-done | bytes 393248 | tf_op jit(solution)/shard_map/ppermute | solution.py:71
  70.5 7.7 %collective-permute-done.26 = bf16[512,256]{1,0:T(8,128)(2,1)S(1)} collective-permute-done((bf16[512,256]{1,0:T(8,128)(2,1)S(1)}, bf16[512,256]{1,0:T(8,128)(2,1)S(1)}, u32[]{:S(2)}, u32[]{:S(2)}) %collective-permute-start.26) | collective-permute-done | bytes 262176 | tf_op jit(solution)/shard_map/ppermute | solution.py:13
  78.6 5.2 %collective-permute-done.6 = bf16[512,256]{1,0:T(8,128)(2,1)S(1)} collective-permute-done((bf16[512,256]{1,0:T(8,128)(2,1)S(1)}, bf16[512,256]{1,0:T(8,128)(2,1)S(1)}, u32[]{:S(2)}, u32[]{:S(2)}) %collective-permute-start.6) | collective-permute-done | bytes 262176 | tf_op jit(solution)/shard_map/ppermute | solution.py:13
  84.2 5.4 %collective-permute-done.27 = bf16[512,256]{1,0:T(8,128)(2,1)S(1)} collective-permute-done((bf16[512,256]{1,0:T(8,128)(2,1)S(1)}, bf16[512,256]{1,0:T(8,128)(2,1)S(1)}, u32[]{:S(2)}, u32[]{:S(2)}) %collective-permute-start.27) | collective-permute-done | bytes 262176 | tf_op jit(solution)/shard_map/ppermute | solution.py:13
  90.1 5.2 %collective-permute-done.7 = bf16[512,256]{1,0:T(8,128)(2,1)S(1)} collective-permute-done((bf16[512,256]{1,0:T(8,128)(2,1)S(1)}, bf16[512,256]{1,0:T(8,128)(2,1)S(1)}, u32[]{:S(2)}, u32[]{:S(2)}) %collective-permute-start.7) | collective-permute-done | bytes 262176 | tf_op jit(solution)/shard_map/ppermute | solution.py:13
  96.0 3.8 %collective-permute-done.28 = bf16[512,256]{1,0:T(8,128)(2,1)S(1)} collective-permute-done((bf16[512,256]{1,0:T(8,128)(2,1)S(1)}, bf16[512,256]{1,0:T(8,128)(2,1)S(1)}, u32[]{:S(2)}, u32[]{:S(2)}) %collective-permute-start.28) | collective-permute-done | bytes 262176 | tf_op jit(solution)/shard_map/ppermute | solution.py:13
  99.9 4.0 %collective-permute-done.8 = bf16[512,256]{1,0:T(8,128)(2,1)S(1)} collective-permute-done((bf16[512,256]{1,0:T(8,128)(2,1)S(1)}, bf16[512,256]{1,0:T(8,128)(2,1)S(1)}, u32[]{:S(2)}, u32[]{:S(2)}) %collective-permute-start.8) | collective-permute-done | bytes 262176 | tf_op jit(solution)/shard_map/ppermute | solution.py:13
  106.1 9.9 %collective-permute-done.11 = f32[1]{0:T(128)} collective-permute-done((f32[1]{0:T(128)}, f32[1]{0:T(128)}, u32[]{:S(2)}, u32[]{:S(2)}) %collective-permute-start.11) | collective-permute-done | bytes 36 | tf_op jit(solution)/shard_map/ppermute | solution.py:13
  116.5 2.9 %collective-permute-start.20 = (f32[1]{0:T(128)}, f32[1]{0:T(128)}, u32[]{:S(2)}, u32[]{:S(2)}) collective-permute-start(f32[1]{0:T(128)} %add.360), channel_id=1, source_target_pairs={{0,16},{8,24},{16,0},{24,8},{1,17},{9,25},{17,1},{25,9},{2,18},{10... | collective-permute-start | bytes 20 | tf_op jit(solution)/shard_map/ppermute | solution.py:13
  123.0 3.7 %collective-permute-done.9 = bf16[512,256]{1,0:T(8,128)(2,1)S(1)} collective-permute-done((bf16[512,256]{1,0:T(8,128)(2,1)S(1)}, bf16[512,256]{1,0:T(8,128)(2,1)S(1)}, u32[]{:S(2)}, u32[]{:S(2)}) %collective-permute-start.9) | collective-permute-done | bytes 262176 | tf_op jit(solution)/shard_map/ppermute | solution.py:13
  126.6 5.6 %collective-permute-done = f32[512,256]{1,0:T(8,128)S(1)} collective-permute-done((f32[512,256]{1,0:T(8,128)S(1)}, f32[512,256]{1,0:T(8,128)S(1)}, u32[]{:S(2)}, u32[]{:S(2)}) %collective-permute-start) | collective-permute-done | bytes 524320 | tf_op jit(solution)/shard_map/ppermute | solution.py:13
  135.5 8.4 %collective-permute-done.12 = bf16[512,256]{1,0:T(8,128)(2,1)S(1)} collective-permute-done((bf16[512,256]{1,0:T(8,128)(2,1)S(1)}, bf16[512,256]{1,0:T(8,128)(2,1)S(1)}, u32[]{:S(2)}, u32[]{:S(2)}) %collective-permute-start.12) | collective-permute-done | bytes 262176 | tf_op jit(solution)/shard_map/ppermute | solution.py:13
  145.2 4.3 %collective-permute-done.32 = bf16[512,256]{1,0:T(8,128)(2,1)S(1)} collective-permute-done((bf16[512,256]{1,0:T(8,128)(2,1)S(1)}, bf16[512,256]{1,0:T(8,128)(2,1)S(1)}, u32[]{:S(2)}, u32[]{:S(2)}) %collective-permute-start.32) | collective-permute-done | bytes 262176 | tf_op jit(solution)/shard_map/ppermute | solution.py:13
  150.0 5.1 %collective-permute-done.13 = bf16[512,256]{1,0:T(8,128)(2,1)S(1)} collective-permute-done((bf16[512,256]{1,0:T(8,128)(2,1)S(1)}, bf16[512,256]{1,0:T(8,128)(2,1)S(1)}, u32[]{:S(2)}, u32[]{:S(2)}) %collective-permute-start.13) | collective-permute-done | bytes 262176 | tf_op jit(solution)/shard_map/ppermute | solution.py:13
  155.6 5.1 %collective-permute-done.33 = bf16[512,256]{1,0:T(8,128)(2,1)S(1)} collective-permute-done((bf16[512,256]{1,0:T(8,128)(2,1)S(1)}, bf16[512,256]{1,0:T(8,128)(2,1)S(1)}, u32[]{:S(2)}, u32[]{:S(2)}) %collective-permute-start.33) | collective-permute-done | bytes 262176 | tf_op jit(solution)/shard_map/ppermute | solution.py:13
  166.6 5.8 %collective-permute-done.34 = bf16[768,256]{1,0:T(8,128)(2,1)S(1)} collective-permute-done((bf16[768,256]{1,0:T(8,128)(2,1)S(1)}, bf16[768,256]{1,0:T(8,128)(2,1)S(1)}, u32[]{:S(2)}, u32[]{:S(2)}) %collective-permute-start.34) | collective-permute-done | bytes 393248 | tf_op jit(solution)/shard_map/ppermute | solution.py:71
  173.9 3.6 %collective-permute-done.15 = bf16[768,256]{1,0:T(8,128)(2,1)S(1)} collective-permute-done((bf16[768,256]{1,0:T(8,128)(2,1)S(1)}, bf16[768,256]{1,0:T(8,128)(2,1)S(1)}, u32[]{:S(2)}, u32[]{:S(2)}) %collective-permute-start.15) | collective-permute-done | bytes 393248 | tf_op jit(solution)/shard_map/ppermute | solution.py:71
  180.0 9.5 %collective-permute-done.35 = bf16[512,256]{1,0:T(8,128)(2,1)S(1)} collective-permute-done((bf16[512,256]{1,0:T(8,128)(2,1)S(1)}, bf16[512,256]{1,0:T(8,128)(2,1)S(1)}, u32[]{:S(2)}, u32[]{:S(2)}) %collective-permute-start.35) | collective-permute-done | bytes 262176 | tf_op jit(solution)/shard_map/ppermute | solution.py:13
  189.9 5.2 %collective-permute-done.16 = bf16[512,256]{1,0:T(8,128)(2,1)S(1)} collective-permute-done((bf16[512,256]{1,0:T(8,128)(2,1)S(1)}, bf16[512,256]{1,0:T(8,128)(2,1)S(1)}, u32[]{:S(2)}, u32[]{:S(2)}) %collective-permute-start.16) | collective-permute-done | bytes 262176 | tf_op jit(solution)/shard_map/ppermute | solution.py:13
  195.5 5.4 %collective-permute-done.36 = bf16[512,256]{1,0:T(8,128)(2,1)S(1)} collective-permute-done((bf16[512,256]{1,0:T(8,128)(2,1)S(1)}, bf16[512,256]{1,0:T(8,128)(2,1)S(1)}, u32[]{:S(2)}, u32[]{:S(2)}) %collective-permute-start.36) | collective-permute-done | bytes 262176 | tf_op jit(solution)/shard_map/ppermute | solution.py:13
  201.3 5.2 %collective-permute-done.17 = bf16[512,256]{1,0:T(8,128)(2,1)S(1)} collective-permute-done((bf16[512,256]{1,0:T(8,128)(2,1)S(1)}, bf16[512,256]{1,0:T(8,128)(2,1)S(1)}, u32[]{:S(2)}, u32[]{:S(2)}) %collective-permute-start.17) | collective-permute-done | bytes 262176 | tf_op jit(solution)/shard_map/ppermute | solution.py:13
  207.0 4.1 %collective-permute-done.37 = bf16[512,256]{1,0:T(8,128)(2,1)S(1)} collective-permute-done((bf16[512,256]{1,0:T(8,128)(2,1)S(1)}, bf16[512,256]{1,0:T(8,128)(2,1)S(1)}, u32[]{:S(2)}, u32[]{:S(2)}) %collective-permute-start.37) | collective-permute-done | bytes 262176 | tf_op jit(solution)/shard_map/ppermute | solution.py:13
  211.4 3.7 %collective-permute-done.18 = bf16[512,256]{1,0:T(8,128)(2,1)S(1)} collective-permute-done((bf16[512,256]{1,0:T(8,128)(2,1)S(1)}, bf16[512,256]{1,0:T(8,128)(2,1)S(1)}, u32[]{:S(2)}, u32[]{:S(2)}) %collective-permute-start.18) | collective-permute-done | bytes 262176 | tf_op jit(solution)/shard_map/ppermute | solution.py:13
  218.6 3.3 %collective-permute-done.19 = bf16[512,256]{1,0:T(8,128)(2,1)S(1)} collective-permute-done((bf16[512,256]{1,0:T(8,128)(2,1)S(1)}, bf16[512,256]{1,0:T(8,128)(2,1)S(1)}, u32[]{:S(2)}, u32[]{:S(2)}) %collective-permute-start.19) | collective-permute-done | bytes 262176 | tf_op jit(solution)/shard_map/ppermute | solution.py:13
  (142 shorter events, 57.8 us)
Async XLA Ops:
  2.6 12.2 %collective-permute-start.1 = (bf16[512,256]{1,0:T(8,128)(2,1)S(1)}, bf16[512,256]{1,0:T(8,128)(2,1)S(1)}, u32[]{:S(2)}, u32[]{:S(2)}) collective-permute-start(bf16[512,256]{1,0:T(8,128)(2,1)S(1)} %get-tuple-element.28), channel_id=1, source_target_pairs={{0,2},{1,3},{2,4},{3,5},{4,6},{5,7},{6,0},{7,1},{8,10},{9,11},{10,... | collective-permute-start | bytes 786440 | tf_op jit(solution)/shard_map/ppermute | solution.py:13
  5.6 14.9 %collective-permute-start.22 = (bf16[512,256]{1,0:T(8,128)(2,1)S(1)}, bf16[512,256]{1,0:T(8,128)(2,1)}, u32[]{:S(2)}, u32[]{:S(2)}) collective-permute-start(bf16[512,256]{1,0:T(8,128)(2,1)S(1)} %get-tuple-element.29), channel_id=1, source_target_pairs={{0,2},{1,3},{2,4},{3,5},{4,6},{5,7},{6,0},{7,1},{8,10},{9,11},{10,... | collective-permute-start | bytes 786440 | tf_op jit(solution)/shard_map/ppermute | solution.py:13
  10.2 35.8 %collective-permute-start.4 = (bf16[384,2048]{1,0:T(8,128)(2,1)}, bf16[384,2048]{1,0:T(8,128)(2,1)S(1)}, u32[]{:S(2)}, u32[]{:S(2)}) collective-permute-start(bf16[384,2048]{1,0:T(8,128)(2,1)} %pad_maximum_fusion), channel_id=1, source_target_pairs={{0,1},{1,0},{2,3},{3,2},{4,5},{5,4},{6,7},{7,6},{8,9},{9,8},{10,11... | collective-permute-start | bytes 4718600 | tf_op jit(solution)/shard_map/ppermute | solution.py:40
  14.8 11.2 %collective-permute-start.2 = (bf16[512,256]{1,0:T(8,128)(2,1)S(1)}, bf16[512,256]{1,0:T(8,128)(2,1)S(1)}, u32[]{:S(2)}, u32[]{:S(2)}) collective-permute-start(bf16[512,256]{1,0:T(8,128)(2,1)S(1)} %collective-permute-done.1), channel_id=1, source_target_pairs={{0,2},{1,3},{2,4},{3,5},{4,6},{5,7},{6,0},{7,1},{8,10},{9,11},{10,... | collective-permute-start | bytes 786440 | tf_op jit(solution)/shard_map/ppermute | solution.py:13
  20.5 11.2 %collective-permute-start.23 = (bf16[512,256]{1,0:T(8,128)(2,1)}, bf16[512,256]{1,0:T(8,128)(2,1)S(1)}, u32[]{:S(2)}, u32[]{:S(2)}) collective-permute-start(bf16[512,256]{1,0:T(8,128)(2,1)} %collective-permute-done.22), channel_id=1, source_target_pairs={{0,2},{1,3},{2,4},{3,5},{4,6},{5,7},{6,0},{7,1},{8,10},{9,11},{10,... | collective-permute-start | bytes 786440 | tf_op jit(solution)/shard_map/ppermute | solution.py:13
  26.0 11.4 %collective-permute-start.3 = (bf16[512,256]{1,0:T(8,128)(2,1)S(1)}, bf16[512,256]{1,0:T(8,128)(2,1)S(1)}, u32[]{:S(2)}, u32[]{:S(2)}) collective-permute-start(bf16[512,256]{1,0:T(8,128)(2,1)S(1)} %collective-permute-done.2), channel_id=1, source_target_pairs={{0,2},{1,3},{2,4},{3,5},{4,6},{5,7},{6,0},{7,1},{8,10},{9,11},{10,... | collective-permute-start | bytes 786440 | tf_op jit(solution)/shard_map/ppermute | solution.py:13
  31.8 10.3 %collective-permute-start.24 = (bf16[512,256]{1,0:T(8,128)(2,1)S(1)}, bf16[512,256]{1,0:T(8,128)(2,1)S(1)}, u32[]{:S(2)}, u32[]{:S(2)}) collective-permute-start(bf16[512,256]{1,0:T(8,128)(2,1)S(1)} %collective-permute-done.23), channel_id=1, source_target_pairs={{0,2},{1,3},{2,4},{3,5},{4,6},{5,7},{6,0},{7,1},{8,10},{9,11},{10,... | collective-permute-start | bytes 786440 | tf_op jit(solution)/shard_map/ppermute | solution.py:13
  48.0 12.1 %collective-permute-start.25 = (bf16[768,256]{1,0:T(8,128)(2,1)S(1)}, bf16[768,256]{1,0:T(8,128)(2,1)S(1)}, u32[]{:S(2)}, u32[]{:S(2)}) collective-permute-start(bf16[768,256]{1,0:T(8,128)(2,1)S(1)} %pad_maximum_fusion.3), channel_id=1, source_target_pairs={{0,1},{1,0},{2,3},{3,2},{4,5},{5,4},{6,7},{7,6},{8,9},{9,8},{10,11... | collective-permute-start | bytes 1179656 | tf_op jit(solution)/shard_map/ppermute | solution.py:71
  50.7 15.2 %collective-permute-start.5 = (bf16[768,256]{1,0:T(8,128)(2,1)S(1)}, bf16[768,256]{1,0:T(8,128)(2,1)S(1)}, u32[]{:S(2)}, u32[]{:S(2)}) collective-permute-start(bf16[768,256]{1,0:T(8,128)(2,1)S(1)} %pad_maximum_fusion.1), channel_id=1, source_target_pairs={{0,1},{1,0},{2,3},{3,2},{4,5},{5,4},{6,7},{7,6},{8,9},{9,8},{10,11... | collective-permute-start | bytes 1179656 | tf_op jit(solution)/shard_map/ppermute | solution.py:71
  67.1 11.1 %collective-permute-start.26 = (bf16[512,256]{1,0:T(8,128)(2,1)S(1)}, bf16[512,256]{1,0:T(8,128)(2,1)S(1)}, u32[]{:S(2)}, u32[]{:S(2)}) collective-permute-start(bf16[512,256]{1,0:T(8,128)(2,1)S(1)} %fusion.2), channel_id=1, source_target_pairs={{0,2},{1,3},{2,4},{3,5},{4,6},{5,7},{6,0},{7,1},{8,10},{9,11},{10,... | collective-permute-start | bytes 786440 | tf_op jit(solution)/shard_map/ppermute | solution.py:13
  69.4 14.4 %collective-permute-start.6 = (bf16[512,256]{1,0:T(8,128)(2,1)S(1)}, bf16[512,256]{1,0:T(8,128)(2,1)S(1)}, u32[]{:S(2)}, u32[]{:S(2)}) collective-permute-start(bf16[512,256]{1,0:T(8,128)(2,1)S(1)} %fusion), channel_id=1, source_target_pairs={{0,2},{1,3},{2,4},{3,5},{4,6},{5,7},{6,0},{7,1},{8,10},{9,11},{10,... | collective-permute-start | bytes 786440 | tf_op jit(solution)/shard_map/ppermute | solution.py:13
  78.6 11.1 %collective-permute-start.27 = (bf16[512,256]{1,0:T(8,128)(2,1)S(1)}, bf16[512,256]{1,0:T(8,128)(2,1)S(1)}, u32[]{:S(2)}, u32[]{:S(2)}) collective-permute-start(bf16[512,256]{1,0:T(8,128)(2,1)S(1)} %add_convert_fusion.3), channel_id=1, source_target_pairs={{0,2},{1,3},{2,4},{3,5},{4,6},{5,7},{6,0},{7,1},{8,10},{9,11},{10,... | collective-permute-start | bytes 786440 | tf_op jit(solution)/shard_map/ppermute | solution.py:13
  84.2 11.1 %collective-permute-start.7 = (bf16[512,256]{1,0:T(8,128)(2,1)S(1)}, bf16[512,256]{1,0:T(8,128)(2,1)S(1)}, u32[]{:S(2)}, u32[]{:S(2)}) collective-permute-start(bf16[512,256]{1,0:T(8,128)(2,1)S(1)} %add_convert_fusion.7), channel_id=1, source_target_pairs={{0,2},{1,3},{2,4},{3,5},{4,6},{5,7},{6,0},{7,1},{8,10},{9,11},{10,... | collective-permute-start | bytes 786440 | tf_op jit(solution)/shard_map/ppermute | solution.py:13
  90.0 9.9 %collective-permute-start.28 = (bf16[512,256]{1,0:T(8,128)(2,1)S(1)}, bf16[512,256]{1,0:T(8,128)(2,1)S(1)}, u32[]{:S(2)}, u32[]{:S(2)}) collective-permute-start(bf16[512,256]{1,0:T(8,128)(2,1)S(1)} %add_convert_fusion.2), channel_id=1, source_target_pairs={{0,2},{1,3},{2,4},{3,5},{4,6},{5,7},{6,0},{7,1},{8,10},{9,11},{10,... | collective-permute-start | bytes 786440 | tf_op jit(solution)/shard_map/ppermute | solution.py:13
  104.3 18.2 %collective-permute-start.21 = (f32[512,256]{1,0:T(8,128)S(1)}, f32[512,256]{1,0:T(8,128)S(1)}, u32[]{:S(2)}, u32[]{:S(2)}) collective-permute-start(f32[512,256]{1,0:T(8,128)S(1)} %get-tuple-element.26), channel_id=1, source_target_pairs={{0,8},{8,16},{16,24},{24,0},{1,9},{9,17},{17,25},{25,1},{2,10},{10... | collective-permute-start | bytes 1572872 | tf_op jit(solution)/shard_map/ppermute | solution.py:13
  104.4 18.1 %collective-permute-start.29 = (bf16[512,256]{1,0:T(8,128)(2,1)S(1)}, bf16[512,256]{1,0:T(8,128)(2,1)S(1)}, u32[]{:S(2)}, u32[]{:S(2)}) collective-permute-start(bf16[512,256]{1,0:T(8,128)(2,1)S(1)} %get-tuple-element.30), channel_id=1, source_target_pairs={{0,8},{8,16},{16,24},{24,0},{1,9},{9,17},{17,25},{25,1},{2,10},{10... | collective-permute-start | bytes 786440 | tf_op jit(solution)/shard_map/ppermute | solution.py:13
  106.0 9.9 %collective-permute-start.11 = (f32[1]{0:T(128)}, f32[1]{0:T(128)}, u32[]{:S(2)}, u32[]{:S(2)}) collective-permute-start(f32[1]{0:T(128)} %param.9), channel_id=1, source_target_pairs={{0,8},{8,16},{16,24},{24,0},{1,9},{9,17},{17,25},{25,1},{2,10},{10... | collective-permute-start | bytes 20 | tf_op jit(solution)/shard_map/ppermute | solution.py:13
  120.9 11.4 %collective-permute-start = (f32[512,256]{1,0:T(8,128)S(1)}, f32[512,256]{1,0:T(8,128)S(1)}, u32[]{:S(2)}, u32[]{:S(2)}) collective-permute-start(f32[512,256]{1,0:T(8,128)S(1)} %get-tuple-element.27), channel_id=1, source_target_pairs={{0,8},{8,16},{16,24},{24,0},{1,9},{9,17},{17,25},{25,1},{2,10},{10... | collective-permute-start | bytes 1572872 | tf_op jit(solution)/shard_map/ppermute | solution.py:13
  122.7 12.5 %collective-permute-start.31 = (bf16[512,256]{1,0:T(8,128)(2,1)S(1)}, bf16[512,256]{1,0:T(8,128)(2,1)S(1)}, u32[]{:S(2)}, u32[]{:S(2)}) collective-permute-start(bf16[512,256]{1,0:T(8,128)(2,1)S(1)} %get-tuple-element.47), channel_id=1, source_target_pairs={{0,2},{1,3},{2,4},{3,5},{4,6},{5,7},{6,0},{7,1},{8,10},{9,11},{10,... | collective-permute-start | bytes 786440 | tf_op jit(solution)/shard_map/ppermute | solution.py:13
  132.8 11.1 %collective-permute-start.12 = (bf16[512,256]{1,0:T(8,128)(2,1)S(1)}, bf16[512,256]{1,0:T(8,128)(2,1)S(1)}, u32[]{:S(2)}, u32[]{:S(2)}) collective-permute-start(bf16[512,256]{1,0:T(8,128)(2,1)S(1)} %get-tuple-element.45), channel_id=1, source_target_pairs={{0,2},{1,3},{2,4},{3,5},{4,6},{5,7},{6,0},{7,1},{8,10},{9,11},{10,... | collective-permute-start | bytes 786440 | tf_op jit(solution)/shard_map/ppermute | solution.py:13
  133.1 82.5 %collective-permute-start.30 = (f32[512,256]{1,0:T(8,128)S(1)}, f32[512,256]{1,0:T(8,128)S(1)}, u32[]{:S(2)}, u32[]{:S(2)}) collective-permute-start(f32[512,256]{1,0:T(8,128)S(1)} %get-tuple-element.46), channel_id=1, source_target_pairs={{0,16},{8,24},{16,0},{24,8},{1,17},{9,25},{17,1},{25,9},{2,18},{10... | collective-permute-start | bytes 1572872 | tf_op jit(solution)/shard_map/ppermute | solution.py:13
  134.7 83.9 %collective-permute-start.10 = (f32[512,256]{1,0:T(8,128)S(1)}, f32[512,256]{1,0:T(8,128)S(1)}, u32[]{:S(2)}, u32[]{:S(2)}) collective-permute-start(f32[512,256]{1,0:T(8,128)S(1)} %get-tuple-element.44), channel_id=1, source_target_pairs={{0,16},{8,24},{16,0},{24,8},{1,17},{9,25},{17,1},{25,9},{2,18},{10... | collective-permute-start | bytes 1572872 | tf_op jit(solution)/shard_map/ppermute | solution.py:13
  135.2 14.3 %collective-permute-start.32 = (bf16[512,256]{1,0:T(8,128)(2,1)S(1)}, bf16[512,256]{1,0:T(8,128)(2,1)S(1)}, u32[]{:S(2)}, u32[]{:S(2)}) collective-permute-start(bf16[512,256]{1,0:T(8,128)(2,1)S(1)} %collective-permute-done.31), channel_id=1, source_target_pairs={{0,2},{1,3},{2,4},{3,5},{4,6},{5,7},{6,0},{7,1},{8,10},{9,11},{10,... | collective-permute-start | bytes 786440 | tf_op jit(solution)/shard_map/ppermute | solution.py:13
  143.9 11.2 %collective-permute-start.13 = (bf16[512,256]{1,0:T(8,128)(2,1)S(1)}, bf16[512,256]{1,0:T(8,128)(2,1)S(1)}, u32[]{:S(2)}, u32[]{:S(2)}) collective-permute-start(bf16[512,256]{1,0:T(8,128)(2,1)S(1)} %collective-permute-done.12), channel_id=1, source_target_pairs={{0,2},{1,3},{2,4},{3,5},{4,6},{5,7},{6,0},{7,1},{8,10},{9,11},{10,... | collective-permute-start | bytes 786440 | tf_op jit(solution)/shard_map/ppermute | solution.py:13
  149.5 11.2 %collective-permute-start.33 = (bf16[512,256]{1,0:T(8,128)(2,1)S(1)}, bf16[512,256]{1,0:T(8,128)(2,1)S(1)}, u32[]{:S(2)}, u32[]{:S(2)}) collective-permute-start(bf16[512,256]{1,0:T(8,128)(2,1)S(1)} %collective-permute-done.32), channel_id=1, source_target_pairs={{0,2},{1,3},{2,4},{3,5},{4,6},{5,7},{6,0},{7,1},{8,10},{9,11},{10,... | collective-permute-start | bytes 786440 | tf_op jit(solution)/shard_map/ppermute | solution.py:13
  161.3 11.1 %collective-permute-start.34 = (bf16[768,256]{1,0:T(8,128)(2,1)S(1)}, bf16[768,256]{1,0:T(8,128)(2,1)S(1)}, u32[]{:S(2)}, u32[]{:S(2)}) collective-permute-start(bf16[768,256]{1,0:T(8,128)(2,1)S(1)} %pad_maximum_fusion.4), channel_id=1, source_target_pairs={{0,1},{1,0},{2,3},{3,2},{4,5},{5,4},{6,7},{7,6},{8,9},{9,8},{10,11... | collective-permute-start | bytes 1179656 | tf_op jit(solution)/shard_map/ppermute | solution.py:71
  165.0 12.5 %collective-permute-start.15 = (bf16[768,256]{1,0:T(8,128)(2,1)S(1)}, bf16[768,256]{1,0:T(8,128)(2,1)S(1)}, u32[]{:S(2)}, u32[]{:S(2)}) collective-permute-start(bf16[768,256]{1,0:T(8,128)(2,1)S(1)} %pad_maximum_fusion.2), channel_id=1, source_target_pairs={{0,1},{1,0},{2,3},{3,2},{4,5},{5,4},{6,7},{7,6},{8,9},{9,8},{10,11... | collective-permute-start | bytes 1179656 | tf_op jit(solution)/shard_map/ppermute | solution.py:71
  178.8 10.7 %collective-permute-start.35 = (bf16[512,256]{1,0:T(8,128)(2,1)S(1)}, bf16[512,256]{1,0:T(8,128)(2,1)S(1)}, u32[]{:S(2)}, u32[]{:S(2)}) collective-permute-start(bf16[512,256]{1,0:T(8,128)(2,1)S(1)} %fusion.3), channel_id=1, source_target_pairs={{0,2},{1,3},{2,4},{3,5},{4,6},{5,7},{6,0},{7,1},{8,10},{9,11},{10,... | collective-permute-start | bytes 786440 | tf_op jit(solution)/shard_map/ppermute | solution.py:13
  179.6 15.6 %collective-permute-start.16 = (bf16[512,256]{1,0:T(8,128)(2,1)S(1)}, bf16[512,256]{1,0:T(8,128)(2,1)S(1)}, u32[]{:S(2)}, u32[]{:S(2)}) collective-permute-start(bf16[512,256]{1,0:T(8,128)(2,1)S(1)} %fusion.1), channel_id=1, source_target_pairs={{0,2},{1,3},{2,4},{3,5},{4,6},{5,7},{6,0},{7,1},{8,10},{9,11},{10,... | collective-permute-start | bytes 786440 | tf_op jit(solution)/shard_map/ppermute | solution.py:13
  189.8 11.1 %collective-permute-start.36 = (bf16[512,256]{1,0:T(8,128)(2,1)S(1)}, bf16[512,256]{1,0:T(8,128)(2,1)S(1)}, u32[]{:S(2)}, u32[]{:S(2)}) collective-permute-start(bf16[512,256]{1,0:T(8,128)(2,1)S(1)} %add_convert_fusion.1), channel_id=1, source_target_pairs={{0,2},{1,3},{2,4},{3,5},{4,6},{5,7},{6,0},{7,1},{8,10},{9,11},{10,... | collective-permute-start | bytes 786440 | tf_op jit(solution)/shard_map/ppermute | solution.py:13
  195.5 11.1 %collective-permute-start.17 = (bf16[512,256]{1,0:T(8,128)(2,1)S(1)}, bf16[512,256]{1,0:T(8,128)(2,1)S(1)}, u32[]{:S(2)}, u32[]{:S(2)}) collective-permute-start(bf16[512,256]{1,0:T(8,128)(2,1)S(1)} %add_convert_fusion.5), channel_id=1, source_target_pairs={{0,2},{1,3},{2,4},{3,5},{4,6},{5,7},{6,0},{7,1},{8,10},{9,11},{10,... | collective-permute-start | bytes 786440 | tf_op jit(solution)/shard_map/ppermute | solution.py:13
  201.3 9.7 %collective-permute-start.37 = (bf16[512,256]{1,0:T(8,128)(2,1)S(1)}, bf16[512,256]{1,0:T(8,128)(2,1)S(1)}, u32[]{:S(2)}, u32[]{:S(2)}) collective-permute-start(bf16[512,256]{1,0:T(8,128)(2,1)S(1)} %add_convert_fusion), channel_id=1, source_target_pairs={{0,2},{1,3},{2,4},{3,5},{4,6},{5,7},{6,0},{7,1},{8,10},{9,11},{10,... | collective-permute-start | bytes 786440 | tf_op jit(solution)/shard_map/ppermute | solution.py:13
  (11 other events, 122.7 us)

commit v4 on v3

v4 whole, which is shorter than its diff:
```python
import jax
import jax.numpy as jnp
from jax import lax
from jax.sharding import PartitionSpec as P

STEPS = 2


def from_behind(value, axis, steps):
    count = lax.axis_size(axis)
    pairs = [(source, (source + steps) % count) for source in range(count)]
    return lax.ppermute(value, axis, pairs)


def tie(*values):
    return lax.optimization_barrier(values)


def shards(tokens, targets, params, momentum, push_weight):
    inputs = tokens[0]
    rows, width = inputs.shape
    features = params.shape[2]
    count = lax.axis_size("fsdp")
    half = count // 2
    block = width // count
    place = lax.div(lax.axis_index("fsdp"), 2)
    lane = lax.rem(lax.axis_index("fsdp"), 2)
    swap = [(i, i ^ 1) for i in range(count)]
    key_scale = width ** (-0.5)
    part = features // 2
    contract = (((0,), (0,)), ((), ()))
    wide = jnp.float32
    narrow = jnp.bfloat16

    def chunk(array, c):
        return array[:, c * part : (c + 1) * part]

    def half_columns(side):
        pieces = []
        for back in range(half):
            start = (2 * lax.rem(place - back + half, half) + side) * block
            pieces.append(lax.dynamic_slice_in_dim(inputs, start, block, 1))
        return jnp.concatenate(pieces, axis=1)

    outgoing, params, momentum = tie(half_columns(1 - lane), params, momentum)
    theirs = lax.ppermute(outgoing, "fsdp", swap)
    mine = half_columns(lane)

    def debias(numerators, weight):
        return (numerators / weight[0]).astype(narrow)

    def column_block(array, back):
        return array[:, back * block : (back + 1) * block]

    def gather(rows_in):
        pieces = [rows_in]
        for _ in range(half - 1):
            pieces.append(from_behind(pieces[-1], "fsdp", 2))
        return pieces

    def product(left, pieces, total):
        for back, piece in enumerate(pieces):
            total = total + key_scale * jnp.dot(
                column_block(left, back), piece, preferred_element_type=wide
            )
        return total

    def partial(own_grad, other_grad, back):
        return lax.dot_general(
            column_block(mine, back), own_grad, contract, preferred_element_type=wide
        ) + lax.dot_general(
            column_block(theirs, back), other_grad, contract, preferred_element_type=wide
        )

    weights = [push_weight]
    for step in range(STEPS):
        weights.append(0.5 * weights[-1] + 0.5 * from_behind(weights[-1], "group", 2**step))

    state = [chunk(params[0], c) for c in range(2)]
    moment = [chunk(momentum[0], c) for c in range(2)]
    target = [chunk(targets[0], c).astype(wide) for c in range(2)]

    for step in range(STEPS):
        last = step == STEPS - 1
        if step == 0:
            debiased = [debias(state[c], weights[step]) for c in range(2)]
        pieces = [gather(debiased[c]) for c in range(2)]
        if step == 0:
            whole = params[0] - (0.2 * 0.9) * momentum[0]
            whole, *weights = tie(whole, *weights)
            before = 0.5 * (whole + from_behind(whole, "group", 2**step))
            before = [chunk(before, c) for c in range(2)]
        else:
            before = [state[c] - (0.2 * 0.9) * moment[c] for c in range(2)]
            before = list(tie(*before))
            got = from_behind(before[0], "group", 2**step)
            got, before[1] = tie(got, before[1])
            before[0] = 0.5 * (before[0] + got)
            before[1] = 0.5 * (before[1] + from_behind(before[1], "group", 2**step))

        own = [product(mine, pieces[c], -target[c]) for c in range(2)]
        other = [product(theirs, pieces[c], 0.0) for c in range(2)]
        got = []
        for c in range(2):
            sent = jnp.concatenate([other[c], own[c]]).astype(narrow)
            if c == 0:
                sent, before[0] = tie(sent, before[0])
            got.append(lax.ppermute(sent, "fsdp", swap))

        def gradients(c):
            received = got[c].astype(wide)
            own_grad = (key_scale * (own[c] + received[:rows])).astype(narrow)
            other_grad = (key_scale * (other[c] + received[rows:])).astype(narrow)
            return own_grad, other_grad

        grads = gradients(0)
        first = from_behind(partial(*grads, 1).astype(narrow), "fsdp", 2)
        first, got[1], before[1] = tie(first, got[1], before[1])
        grads = [grads, gradients(1)]
        second = from_behind(partial(*grads[1], 1).astype(narrow), "fsdp", 2)
        arrived = [first, second]
        for back in range(2, half):
            for c in range(2):
                total = arrived[c].astype(wide) + partial(*grads[c], back)
                arrived[c] = from_behind(total.astype(narrow), "fsdp", 2)
        for c in range(2):
            total = arrived[c].astype(wide) + partial(*grads[c], 0)
            behind = from_behind(total.astype(narrow), "group", 2**step)
            if c == 0 and last:
                behind, arrived[1] = tie(behind, arrived[1])
            moment[c] = 0.9 * moment[c] + total
            state[c] = before[c] - 0.1 * (total + behind.astype(wide))
            if not last:
                state[c], moment[c] = tie(state[c], moment[c])
                debiased[c] = debias(state[c], weights[step + 1])
                if c == 0:
                    debiased[c], arrived[1] = tie(debiased[c], arrived[1])
    new_params = jnp.concatenate([s / weights[STEPS][0] for s in state], axis=1)
    return new_params[None], jnp.concatenate(moment, axis=1)[None]


def solution(mesh):
    return jax.shard_map(
        shards,
        mesh=mesh,
        in_specs=(
            P("group", "fsdp", None),
            P("group", "fsdp", None),
            P("group", "fsdp", None),
            P("group", "fsdp", None),
            P("group"),
        ),
        out_specs=(P("group", "fsdp", None), P("group", "fsdp", None)),
        check_vma=False,
    )
```

time: 225 us -> 212 us (0.942)
  waiting for transfers between devices: 163 us -> 154 us
  starting transfers between devices: 24.3 us -> 19 us
    ppermute x5, waiting for transfers between devices: 26 us -> 13.7 us  [the longest x4 13.7 us: shards(): got.append(lax.ppermute(sent, 'fsdp', swap))]
    ppermute x34 -> x33, starting transfers between devices: 17.5 us -> 13.2 us  [from_behind(): return lax.ppermute(value, axis, pairs)]
    ppermute x34 -> x33, waiting for transfers between devices: 137 us -> 141 us  [from_behind(): return lax.ppermute(value, axis, pairs)]
  transfers between devices with their start and end apart: 39 -> 38, of which waited for: 34 -> 28; matrix products, arithmetic and copies ran while one was open for 12% -> 13% of each run, Pallas kernels for 0% -> 0%
where the time goes in v4:
time: 212 us; the launch traced here: 211 us
  waiting for transfers between devices  154 us (73%)
  matrix products  26.4 us (12%)
  starting transfers between devices  19 us (9%)
  other arithmetic  6.81 us (3%)
  between operations  3.34 us (2%)
    ppermute x33, waiting for transfers between devices, from_behind(): return lax.ppermute(value, axis, pairs)  141 us
    dot_general x32, matrix products, product(): jnp.dot(column_block(left, back), piece, preferred_element_type=wide)  15.5 us
    ppermute x4, waiting for transfers between devices, shards(): got.append(lax.ppermute(sent, 'fsdp', swap))  13.7 us
    ppermute x33, starting transfers between devices, from_behind(): return lax.ppermute(value, axis, pairs)  13.2 us
    dot_general x16, matrix products, partial(): lax.dot_general(column_block(mine, back), own_grad, contract, preferred_e...  5.45 us
    dot_general x16, matrix products, partial(): lax.dot_general(column_block(theirs, back), other_grad, contract, preferr...  5.4 us
    ppermute x4, starting transfers between devices, shards(): got.append(lax.ppermute(sent, 'fsdp', swap))  4.31 us
  transfers between devices with their start and end apart: 38, of which 28 were waited for; matrix products, arithmetic and copies ran while one was open for 13% of the time, Pallas kernels for 0%

profile of v4, /device:TPU:0, one launch (start us, length us, event | category | flops | bytes accessed | tf_op | source)
XLA Modules:
  0.0 211.5 jit_solution(4672100708547252355)
XLA Ops:
  4.8 2.7 %collective-permute-start.1 = (bf16[512,256]{1,0:T(8,128)(2,1)S(1)}, bf16[512,256]{1,0:T(8,128)(2,1)}, u32[]{:S(2)}, u32[]{:S(2)}) collective-permute-start(bf16[512,256]{1,0:T(8,128)(2,1)S(1)} %get-tuple-element.65), channel_id=1, source_target_pairs={{0,2},{1,3},{2,4},{3,5},{4,6},{5,7},{6,0},{7,1},{8,10},{9,11},{10,... | collective-permute-start | bytes 786440 | tf_op jit(solution)/shard_map/ppermute | solution.py:12
  10.6 1.8 multiply_subtract_fusion
  12.4 2.0 fusion.5
  16.4 2.9 %collective-permute-start.5 = (f32[1]{0:T(128)}, f32[1]{0:T(128)}, u32[]{:S(2)}, u32[]{:S(2)}) collective-permute-start(f32[1]{0:T(128)} %add.344), channel_id=1, source_target_pairs={{0,16},{8,24},{16,0},{24,8},{1,17},{9,25},{17,1},{25,9},{2,18},{10... | collective-permute-start | bytes 20 | tf_op jit(solution)/shard_map/ppermute | solution.py:12
  25.4 6.0 %collective-permute-done.2 = bf16[512,256]{1,0:T(8,128)(2,1)S(1)} collective-permute-done((bf16[512,256]{1,0:T(8,128)(2,1)}, bf16[512,256]{1,0:T(8,128)(2,1)S(1)}, u32[]{:S(2)}, u32[]{:S(2)}) %collective-permute-start.2) | collective-permute-done | bytes 262176 | tf_op jit(solution)/shard_map/ppermute | solution.py:12
  31.5 5.6 %collective-permute-done.10 = bf16[512,256]{1,0:T(8,128)(2,1)S(1)} collective-permute-done((bf16[512,256]{1,0:T(8,128)(2,1)}, bf16[512,256]{1,0:T(8,128)(2,1)S(1)}, u32[]{:S(2)}, u32[]{:S(2)}) %collective-permute-start.10) | collective-permute-done | bytes 262176 | tf_op jit(solution)/shard_map/ppermute | solution.py:12
  37.7 5.1 %collective-permute-done.3 = bf16[512,256]{1,0:T(8,128)(2,1)S(1)} collective-permute-done((bf16[512,256]{1,0:T(8,128)(2,1)S(1)}, bf16[512,256]{1,0:T(8,128)(2,1)S(1)}, u32[]{:S(2)}, u32[]{:S(2)}) %collective-permute-start.3) | collective-permute-done | bytes 262176 | tf_op jit(solution)/shard_map/ppermute | solution.py:12
  43.0 5.3 %collective-permute-done.11 = bf16[512,256]{1,0:T(8,128)(2,1)S(1)} collective-permute-done((bf16[512,256]{1,0:T(8,128)(2,1)S(1)}, bf16[512,256]{1,0:T(8,128)(2,1)S(1)}, u32[]{:S(2)}, u32[]{:S(2)}) %collective-permute-start.11) | collective-permute-done | bytes 262176 | tf_op jit(solution)/shard_map/ppermute | solution.py:12
  55.2 7.8 %collective-permute-done.7 = bf16[768,256]{1,0:T(8,128)(2,1)S(1)} collective-permute-done((bf16[768,256]{1,0:T(8,128)(2,1)S(1)}, bf16[768,256]{1,0:T(8,128)(2,1)S(1)}, u32[]{:S(2)}, u32[]{:S(2)}) %collective-permute-start.7) | collective-permute-done | bytes 393248 | tf_op jit(solution)/shard_map/ppermute | solution.py:108
  65.0 5.9 %collective-permute-done.12 = bf16[768,256]{1,0:T(8,128)(2,1)S(1)} collective-permute-done((bf16[768,256]{1,0:T(8,128)(2,1)S(1)}, bf16[768,256]{1,0:T(8,128)(2,1)S(1)}, u32[]{:S(2)}, u32[]{:S(2)}) %collective-permute-start.12) | collective-permute-done | bytes 393248 | tf_op jit(solution)/shard_map/ppermute | solution.py:108
  70.9 2.4 %collective-permute-done.8 = bf16[512,256]{1,0:T(8,128)(2,1)S(1)} collective-permute-done((bf16[512,256]{1,0:T(8,128)(2,1)S(1)}, bf16[512,256]{1,0:T(8,128)(2,1)S(1)}, u32[]{:S(2)}, u32[]{:S(2)}) %collective-permute-start.8) | collective-permute-done | bytes 262176 | tf_op jit(solution)/shard_map/ppermute | solution.py:12
  75.7 9.9 %collective-permute-done.13 = bf16[512,256]{1,0:T(8,128)(2,1)S(1)} collective-permute-done((bf16[512,256]{1,0:T(8,128)(2,1)S(1)}, bf16[512,256]{1,0:T(8,128)(2,1)S(1)}, u32[]{:S(2)}, u32[]{:S(2)}) %collective-permute-start.13) | collective-permute-done | bytes 262176 | tf_op jit(solution)/shard_map/ppermute | solution.py:12
  86.0 5.2 %collective-permute-done.16 = bf16[512,256]{1,0:T(8,128)(2,1)S(1)} collective-permute-done((bf16[512,256]{1,0:T(8,128)(2,1)S(1)}, bf16[512,256]{1,0:T(8,128)(2,1)S(1)}, u32[]{:S(2)}, u32[]{:S(2)}) %collective-permute-start.16) | collective-permute-done | bytes 262176 | tf_op jit(solution)/shard_map/ppermute | solution.py:12
  91.6 5.0 %collective-permute-done.14 = bf16[512,256]{1,0:T(8,128)(2,1)S(1)} collective-permute-done((bf16[512,256]{1,0:T(8,128)(2,1)S(1)}, bf16[512,256]{1,0:T(8,128)(2,1)S(1)}, u32[]{:S(2)}, u32[]{:S(2)}) %collective-permute-start.14) | collective-permute-done | bytes 262176 | tf_op jit(solution)/shard_map/ppermute | solution.py:12
  97.1 2.7 %collective-permute-done.17 = bf16[512,256]{1,0:T(8,128)(2,1)S(1)} collective-permute-done((bf16[512,256]{1,0:T(8,128)(2,1)S(1)}, bf16[512,256]{1,0:T(8,128)(2,1)S(1)}, u32[]{:S(2)}, u32[]{:S(2)}) %collective-permute-start.17) | collective-permute-done | bytes 262176 | tf_op jit(solution)/shard_map/ppermute | solution.py:12
  100.2 2.7 %collective-permute-done.15 = bf16[512,256]{1,0:T(8,128)(2,1)S(1)} collective-permute-done((bf16[512,256]{1,0:T(8,128)(2,1)S(1)}, bf16[512,256]{1,0:T(8,128)(2,1)S(1)}, u32[]{:S(2)}, u32[]{:S(2)}) %collective-permute-start.15) | collective-permute-done | bytes 262176 | tf_op jit(solution)/shard_map/ppermute | solution.py:12
  103.1 5.2 %collective-permute-done.18 = bf16[512,256]{1,0:T(8,128)(2,1)S(1)} collective-permute-done((bf16[512,256]{1,0:T(8,128)(2,1)S(1)}, bf16[512,256]{1,0:T(8,128)(2,1)S(1)}, u32[]{:S(2)}, u32[]{:S(2)}) %collective-permute-start.18) | collective-permute-done | bytes 262176 | tf_op jit(solution)/shard_map/ppermute | solution.py:12
  109.0 5.5 %collective-permute-done.22 = bf16[512,256]{1,0:T(8,128)(2,1)S(1)} collective-permute-done((bf16[512,256]{1,0:T(8,128)(2,1)S(1)}, bf16[512,256]{1,0:T(8,128)(2,1)S(1)}, u32[]{:S(2)}, u32[]{:S(2)}) %collective-permute-start.22) | collective-permute-done | bytes 262176 | tf_op jit(solution)/shard_map/ppermute | solution.py:12
  114.7 5.1 %collective-permute-done.19 = bf16[512,256]{1,0:T(8,128)(2,1)S(1)} collective-permute-done((bf16[512,256]{1,0:T(8,128)(2,1)S(1)}, bf16[512,256]{1,0:T(8,128)(2,1)S(1)}, u32[]{:S(2)}, u32[]{:S(2)}) %collective-permute-start.19) | collective-permute-done | bytes 262176 | tf_op jit(solution)/shard_map/ppermute | solution.py:12
  122.5 8.9 %collective-permute-done.26 = bf16[512,256]{1,0:T(8,128)(2,1)S(1)} collective-permute-done((bf16[512,256]{1,0:T(8,128)(2,1)S(1)}, bf16[512,256]{1,0:T(8,128)(2,1)S(1)}, u32[]{:S(2)}, u32[]{:S(2)}) %collective-permute-start.26) | collective-permute-done | bytes 262176 | tf_op jit(solution)/shard_map/ppermute | solution.py:12
  131.7 5.3 %collective-permute-done.20 = bf16[512,256]{1,0:T(8,128)(2,1)S(1)} collective-permute-done((bf16[512,256]{1,0:T(8,128)(2,1)S(1)}, bf16[512,256]{1,0:T(8,128)(2,1)S(1)}, u32[]{:S(2)}, u32[]{:S(2)}) %collective-permute-start.20) | collective-permute-done | bytes 262176 | tf_op jit(solution)/shard_map/ppermute | solution.py:12
  139.4 8.0 %collective-permute-done.21 = bf16[512,256]{1,0:T(8,128)(2,1)S(1)} collective-permute-done((bf16[512,256]{1,0:T(8,128)(2,1)S(1)}, bf16[512,256]{1,0:T(8,128)(2,1)S(1)}, u32[]{:S(2)}, u32[]{:S(2)}) %collective-permute-start.21) | collective-permute-done | bytes 262176 | tf_op jit(solution)/shard_map/ppermute | solution.py:12
  149.2 8.5 %collective-permute-done.28 = bf16[512,256]{1,0:T(8,128)(2,1)S(1)} collective-permute-done((bf16[512,256]{1,0:T(8,128)(2,1)S(1)}, bf16[512,256]{1,0:T(8,128)(2,1)S(1)}, u32[]{:S(2)}, u32[]{:S(2)}) %collective-permute-start.28) | collective-permute-done | bytes 262176 | tf_op jit(solution)/shard_map/ppermute | solution.py:12
  161.9 7.4 %collective-permute-done.25 = bf16[512,256]{1,0:T(8,128)(2,1)S(1)} collective-permute-done((bf16[512,256]{1,0:T(8,128)(2,1)S(1)}, bf16[512,256]{1,0:T(8,128)(2,1)S(1)}, u32[]{:S(2)}, u32[]{:S(2)}) %collective-permute-start.25) | collective-permute-done | bytes 262176 | tf_op jit(solution)/shard_map/ppermute | solution.py:12
  171.3 8.8 %collective-permute-done.31 = bf16[512,256]{1,0:T(8,128)(2,1)S(1)} collective-permute-done((bf16[512,256]{1,0:T(8,128)(2,1)S(1)}, bf16[512,256]{1,0:T(8,128)(2,1)S(1)}, u32[]{:S(2)}, u32[]{:S(2)}) %collective-permute-start.31) | collective-permute-done | bytes 262176 | tf_op jit(solution)/shard_map/ppermute | solution.py:12
  180.5 5.2 %collective-permute-done.34 = bf16[512,256]{1,0:T(8,128)(2,1)S(1)} collective-permute-done((bf16[512,256]{1,0:T(8,128)(2,1)S(1)}, bf16[512,256]{1,0:T(8,128)(2,1)S(1)}, u32[]{:S(2)}, u32[]{:S(2)}) %collective-permute-start.34) | collective-permute-done | bytes 262176 | tf_op jit(solution)/shard_map/ppermute | solution.py:12
  186.1 4.3 %collective-permute-done.32 = bf16[512,256]{1,0:T(8,128)(2,1)S(1)} collective-permute-done((bf16[512,256]{1,0:T(8,128)(2,1)S(1)}, bf16[512,256]{1,0:T(8,128)(2,1)S(1)}, u32[]{:S(2)}, u32[]{:S(2)}) %collective-permute-start.32) | collective-permute-done | bytes 262176 | tf_op jit(solution)/shard_map/ppermute | solution.py:12
  190.8 3.5 %collective-permute-done.35 = bf16[512,256]{1,0:T(8,128)(2,1)S(1)} collective-permute-done((bf16[512,256]{1,0:T(8,128)(2,1)S(1)}, bf16[512,256]{1,0:T(8,128)(2,1)S(1)}, u32[]{:S(2)}, u32[]{:S(2)}) %collective-permute-start.35) | collective-permute-done | bytes 262176 | tf_op jit(solution)/shard_map/ppermute | solution.py:12
  195.1 2.1 collective-permute-done.33
  197.1 5.7 %collective-permute-done.36 = bf16[512,256]{1,0:T(8,128)(2,1)S(1)} collective-permute-done((bf16[512,256]{1,0:T(8,128)(2,1)S(1)}, bf16[512,256]{1,0:T(8,128)(2,1)S(1)}, u32[]{:S(2)}, u32[]{:S(2)}) %collective-permute-start.36) | collective-permute-done | bytes 262176 | tf_op jit(solution)/shard_map/ppermute | solution.py:12
  203.5 6.2 %collective-permute-done.37 = bf16[512,256]{1,0:T(8,128)(2,1)S(1)} collective-permute-done((bf16[512,256]{1,0:T(8,128)(2,1)S(1)}, bf16[512,256]{1,0:T(8,128)(2,1)S(1)}, u32[]{:S(2)}, u32[]{:S(2)}) %collective-permute-start.37) | collective-permute-done | bytes 262176 | tf_op jit(solution)/shard_map/ppermute | solution.py:12
  209.8 1.6 maximum_bitcast_fusion
  (143 shorter events, 43.8 us)
Async XLA Ops:
  0.6 15.2 %collective-permute-start.4 = (f32[1]{0:T(128)}, f32[1]{0:T(128)}, u32[]{:S(2)}, u32[]{:S(2)}) collective-permute-start(f32[1]{0:T(128)} %param.9), channel_id=1, source_target_pairs={{0,8},{8,16},{16,24},{24,0},{1,9},{9,17},{17,25},{25,1},{2,10},{10... | collective-permute-start | bytes 20 | tf_op jit(solution)/shard_map/ppermute | solution.py:12
  4.8 15.9 %collective-permute-start.1 = (bf16[512,256]{1,0:T(8,128)(2,1)S(1)}, bf16[512,256]{1,0:T(8,128)(2,1)}, u32[]{:S(2)}, u32[]{:S(2)}) collective-permute-start(bf16[512,256]{1,0:T(8,128)(2,1)S(1)} %get-tuple-element.65), channel_id=1, source_target_pairs={{0,2},{1,3},{2,4},{3,5},{4,6},{5,7},{6,0},{7,1},{8,10},{9,11},{10,... | collective-permute-start | bytes 786440 | tf_op jit(solution)/shard_map/ppermute | solution.py:12
  7.5 41.4 %collective-permute-start = (bf16[384,2048]{1,0:T(8,128)(2,1)}, bf16[384,2048]{1,0:T(8,128)(2,1)S(1)}, u32[]{:S(2)}, u32[]{:S(2)}) collective-permute-start(bf16[384,2048]{1,0:T(8,128)(2,1)} %pad_maximum_fusion), channel_id=1, source_target_pairs={{0,1},{1,0},{2,3},{3,2},{4,5},{5,4},{6,7},{7,6},{8,9},{9,8},{10,11... | collective-permute-start | bytes 4718600 | tf_op jit(solution)/shard_map/ppermute | solution.py:46
  9.0 13.4 %collective-permute-start.9 = (bf16[512,256]{1,0:T(8,128)(2,1)S(1)}, bf16[512,256]{1,0:T(8,128)(2,1)}, u32[]{:S(2)}, u32[]{:S(2)}) collective-permute-start(bf16[512,256]{1,0:T(8,128)(2,1)S(1)} %get-tuple-element.64), channel_id=1, source_target_pairs={{0,2},{1,3},{2,4},{3,5},{4,6},{5,7},{6,0},{7,1},{8,10},{9,11},{10,... | collective-permute-start | bytes 786440 | tf_op jit(solution)/shard_map/ppermute | solution.py:12
  20.7 27.9 %collective-permute-start.6 = (f32[512,512]{1,0:T(8,128)S(1)}, f32[512,512]{1,0:T(8,128)S(1)}, u32[]{:S(2)}, u32[]{:S(2)}) collective-permute-start(f32[512,512]{1,0:T(8,128)S(1)} %multiply_subtract_fusion), channel_id=1, source_target_pairs={{0,8},{8,16},{16,24},{24,0},{1,9},{9,17},{17,25},{25,1},{2,10},{10... | collective-permute-start | bytes 3145736 | tf_op jit(solution)/shard_map/ppermute | solution.py:12
  20.8 10.7 %collective-permute-start.2 = (bf16[512,256]{1,0:T(8,128)(2,1)}, bf16[512,256]{1,0:T(8,128)(2,1)S(1)}, u32[]{:S(2)}, u32[]{:S(2)}) collective-permute-start(bf16[512,256]{1,0:T(8,128)(2,1)} %collective-permute-done.1), channel_id=1, source_target_pairs={{0,2},{1,3},{2,4},{3,5},{4,6},{5,7},{6,0},{7,1},{8,10},{9,11},{10,... | collective-permute-start | bytes 786440 | tf_op jit(solution)/shard_map/ppermute | solution.py:12
  22.4 14.7 %collective-permute-start.10 = (bf16[512,256]{1,0:T(8,128)(2,1)}, bf16[512,256]{1,0:T(8,128)(2,1)S(1)}, u32[]{:S(2)}, u32[]{:S(2)}) collective-permute-start(bf16[512,256]{1,0:T(8,128)(2,1)} %collective-permute-done.9), channel_id=1, source_target_pairs={{0,2},{1,3},{2,4},{3,5},{4,6},{5,7},{6,0},{7,1},{8,10},{9,11},{10,... | collective-permute-start | bytes 786440 | tf_op jit(solution)/shard_map/ppermute | solution.py:12
  31.5 11.2 %collective-permute-start.3 = (bf16[512,256]{1,0:T(8,128)(2,1)S(1)}, bf16[512,256]{1,0:T(8,128)(2,1)S(1)}, u32[]{:S(2)}, u32[]{:S(2)}) collective-permute-start(bf16[512,256]{1,0:T(8,128)(2,1)S(1)} %collective-permute-done.2), channel_id=1, source_target_pairs={{0,2},{1,3},{2,4},{3,5},{4,6},{5,7},{6,0},{7,1},{8,10},{9,11},{10,... | collective-permute-start | bytes 786440 | tf_op jit(solution)/shard_map/ppermute | solution.py:12
  37.1 11.2 %collective-permute-start.11 = (bf16[512,256]{1,0:T(8,128)(2,1)S(1)}, bf16[512,256]{1,0:T(8,128)(2,1)S(1)}, u32[]{:S(2)}, u32[]{:S(2)}) collective-permute-start(bf16[512,256]{1,0:T(8,128)(2,1)S(1)} %collective-permute-done.10), channel_id=1, source_target_pairs={{0,2},{1,3},{2,4},{3,5},{4,6},{5,7},{6,0},{7,1},{8,10},{9,11},{10,... | collective-permute-start | bytes 786440 | tf_op jit(solution)/shard_map/ppermute | solution.py:12
  51.0 12.0 %collective-permute-start.7 = (bf16[768,256]{1,0:T(8,128)(2,1)S(1)}, bf16[768,256]{1,0:T(8,128)(2,1)S(1)}, u32[]{:S(2)}, u32[]{:S(2)}) collective-permute-start(bf16[768,256]{1,0:T(8,128)(2,1)S(1)} %pad_maximum_fusion.1), channel_id=1, source_target_pairs={{0,1},{1,0},{2,3},{3,2},{4,5},{5,4},{6,7},{7,6},{8,9},{9,8},{10,11... | collective-permute-start | bytes 1179656 | tf_op jit(solution)/shard_map/ppermute | solution.py:108
  53.7 17.2 %collective-permute-start.12 = (bf16[768,256]{1,0:T(8,128)(2,1)S(1)}, bf16[768,256]{1,0:T(8,128)(2,1)S(1)}, u32[]{:S(2)}, u32[]{:S(2)}) collective-permute-start(bf16[768,256]{1,0:T(8,128)(2,1)S(1)} %pad_maximum_fusion.2), channel_id=1, source_target_pairs={{0,1},{1,0},{2,3},{3,2},{4,5},{5,4},{6,7},{7,6},{8,9},{9,8},{10,11... | collective-permute-start | bytes 1179656 | tf_op jit(solution)/shard_map/ppermute | solution.py:108
  64.2 9.0 %collective-permute-start.8 = (bf16[512,256]{1,0:T(8,128)(2,1)S(1)}, bf16[512,256]{1,0:T(8,128)(2,1)S(1)}, u32[]{:S(2)}, u32[]{:S(2)}) collective-permute-start(bf16[512,256]{1,0:T(8,128)(2,1)S(1)} %fusion), channel_id=1, source_target_pairs={{0,2},{1,3},{2,4},{3,5},{4,6},{5,7},{6,0},{7,1},{8,10},{9,11},{10,... | collective-permute-start | bytes 786440 | tf_op jit(solution)/shard_map/ppermute | solution.py:12
  74.5 11.1 %collective-permute-start.13 = (bf16[512,256]{1,0:T(8,128)(2,1)S(1)}, bf16[512,256]{1,0:T(8,128)(2,1)S(1)}, u32[]{:S(2)}, u32[]{:S(2)}) collective-permute-start(bf16[512,256]{1,0:T(8,128)(2,1)S(1)} %add_convert_fusion.7), channel_id=1, source_target_pairs={{0,2},{1,3},{2,4},{3,5},{4,6},{5,7},{6,0},{7,1},{8,10},{9,11},{10,... | collective-permute-start | bytes 786440 | tf_op jit(solution)/shard_map/ppermute | solution.py:12
  75.3 16.0 %collective-permute-start.16 = (bf16[512,256]{1,0:T(8,128)(2,1)S(1)}, bf16[512,256]{1,0:T(8,128)(2,1)S(1)}, u32[]{:S(2)}, u32[]{:S(2)}) collective-permute-start(bf16[512,256]{1,0:T(8,128)(2,1)S(1)} %fusion.1), channel_id=1, source_target_pairs={{0,2},{1,3},{2,4},{3,5},{4,6},{5,7},{6,0},{7,1},{8,10},{9,11},{10,... | collective-permute-start | bytes 786440 | tf_op jit(solution)/shard_map/ppermute | solution.py:12
  85.9 10.7 %collective-permute-start.14 = (bf16[512,256]{1,0:T(8,128)(2,1)S(1)}, bf16[512,256]{1,0:T(8,128)(2,1)S(1)}, u32[]{:S(2)}, u32[]{:S(2)}) collective-permute-start(bf16[512,256]{1,0:T(8,128)(2,1)S(1)} %add_convert_fusion.6), channel_id=1, source_target_pairs={{0,2},{1,3},{2,4},{3,5},{4,6},{5,7},{6,0},{7,1},{8,10},{9,11},{10,... | collective-permute-start | bytes 786440 | tf_op jit(solution)/shard_map/ppermute | solution.py:12
  100.1 8.2 %collective-permute-start.18 = (bf16[512,256]{1,0:T(8,128)(2,1)S(1)}, bf16[512,256]{1,0:T(8,128)(2,1)S(1)}, u32[]{:S(2)}, u32[]{:S(2)}) collective-permute-start(bf16[512,256]{1,0:T(8,128)(2,1)S(1)} %add_convert_fusion.4), channel_id=1, source_target_pairs={{0,2},{1,3},{2,4},{3,5},{4,6},{5,7},{6,0},{7,1},{8,10},{9,11},{10,... | collective-permute-start | bytes 786440 | tf_op jit(solution)/shard_map/ppermute | solution.py:12
  108.8 11.1 %collective-permute-start.19 = (bf16[512,256]{1,0:T(8,128)(2,1)S(1)}, bf16[512,256]{1,0:T(8,128)(2,1)S(1)}, u32[]{:S(2)}, u32[]{:S(2)}) collective-permute-start(bf16[512,256]{1,0:T(8,128)(2,1)S(1)} %get-tuple-element.40), channel_id=1, source_target_pairs={{0,2},{1,3},{2,4},{3,5},{4,6},{5,7},{6,0},{7,1},{8,10},{9,11},{10,... | collective-permute-start | bytes 786440 | tf_op jit(solution)/shard_map/ppermute | solution.py:12
  120.4 11.0 %collective-permute-start.26 = (bf16[512,256]{1,0:T(8,128)(2,1)S(1)}, bf16[512,256]{1,0:T(8,128)(2,1)S(1)}, u32[]{:S(2)}, u32[]{:S(2)}) collective-permute-start(bf16[512,256]{1,0:T(8,128)(2,1)S(1)} %get-tuple-element.82), channel_id=1, source_target_pairs={{0,2},{1,3},{2,4},{3,5},{4,6},{5,7},{6,0},{7,1},{8,10},{9,11},{10,... | collective-permute-start | bytes 786440 | tf_op jit(solution)/shard_map/ppermute | solution.py:12
  120.8 16.3 %collective-permute-start.20 = (bf16[512,256]{1,0:T(8,128)(2,1)S(1)}, bf16[512,256]{1,0:T(8,128)(2,1)S(1)}, u32[]{:S(2)}, u32[]{:S(2)}) collective-permute-start(bf16[512,256]{1,0:T(8,128)(2,1)S(1)} %collective-permute-done.19), channel_id=1, source_target_pairs={{0,2},{1,3},{2,4},{3,5},{4,6},{5,7},{6,0},{7,1},{8,10},{9,11},{10,... | collective-permute-start | bytes 786440 | tf_op jit(solution)/shard_map/ppermute | solution.py:12
  121.4 16.8 %collective-permute-start.23 = (f32[512,256]{1,0:T(8,128)S(1)}, f32[512,256]{1,0:T(8,128)S(1)}, u32[]{:S(2)}, u32[]{:S(2)}) collective-permute-start(f32[512,256]{1,0:T(8,128)S(1)} %get-tuple-element.46), channel_id=1, source_target_pairs={{0,16},{8,24},{16,0},{24,8},{1,17},{9,25},{17,1},{25,9},{2,18},{10... | collective-permute-start | bytes 1572872 | tf_op jit(solution)/shard_map/ppermute | solution.py:12
  131.4 17.2 %collective-permute-start.27 = (bf16[512,256]{1,0:T(8,128)(2,1)S(1)}, bf16[512,256]{1,0:T(8,128)(2,1)S(1)}, u32[]{:S(2)}, u32[]{:S(2)}) collective-permute-start(bf16[512,256]{1,0:T(8,128)(2,1)S(1)} %collective-permute-done.26), channel_id=1, source_target_pairs={{0,2},{1,3},{2,4},{3,5},{4,6},{5,7},{6,0},{7,1},{8,10},{9,11},{10,... | collective-permute-start | bytes 786440 | tf_op jit(solution)/shard_map/ppermute | solution.py:12
  137.1 10.4 %collective-permute-start.21 = (bf16[512,256]{1,0:T(8,128)(2,1)S(1)}, bf16[512,256]{1,0:T(8,128)(2,1)S(1)}, u32[]{:S(2)}, u32[]{:S(2)}) collective-permute-start(bf16[512,256]{1,0:T(8,128)(2,1)S(1)} %collective-permute-done.20), channel_id=1, source_target_pairs={{0,2},{1,3},{2,4},{3,5},{4,6},{5,7},{6,0},{7,1},{8,10},{9,11},{10,... | collective-permute-start | bytes 786440 | tf_op jit(solution)/shard_map/ppermute | solution.py:12
  138.2 23.6 %collective-permute-start.30 = (f32[512,256]{1,0:T(8,128)S(1)}, f32[512,256]{1,0:T(8,128)S(1)}, u32[]{:S(2)}, u32[]{:S(2)}) collective-permute-start(f32[512,256]{1,0:T(8,128)S(1)} %get-tuple-element.51), channel_id=1, source_target_pairs={{0,16},{8,24},{16,0},{24,8},{1,17},{9,25},{17,1},{25,9},{2,18},{10... | collective-permute-start | bytes 1572872 | tf_op jit(solution)/shard_map/ppermute | solution.py:12
  148.1 11.8 %collective-permute-start.24 = (bf16[768,256]{1,0:T(8,128)(2,1)S(1)}, bf16[768,256]{1,0:T(8,128)(2,1)S(1)}, u32[]{:S(2)}, u32[]{:S(2)}) collective-permute-start(bf16[768,256]{1,0:T(8,128)(2,1)S(1)} %pad_maximum_fusion.3), channel_id=1, source_target_pairs={{0,1},{1,0},{2,3},{3,2},{4,5},{5,4},{6,7},{7,6},{8,9},{9,8},{10,11... | collective-permute-start | bytes 1179656 | tf_op jit(solution)/shard_map/ppermute | solution.py:108
  148.7 9.0 %collective-permute-start.28 = (bf16[512,256]{1,0:T(8,128)(2,1)S(1)}, bf16[512,256]{1,0:T(8,128)(2,1)S(1)}, u32[]{:S(2)}, u32[]{:S(2)}) collective-permute-start(bf16[512,256]{1,0:T(8,128)(2,1)S(1)} %collective-permute-done.27), channel_id=1, source_target_pairs={{0,2},{1,3},{2,4},{3,5},{4,6},{5,7},{6,0},{7,1},{8,10},{9,11},{10,... | collective-permute-start | bytes 786440 | tf_op jit(solution)/shard_map/ppermute | solution.py:12
  158.3 11.0 %collective-permute-start.29 = (bf16[768,256]{1,0:T(8,128)(2,1)S(1)}, bf16[768,256]{1,0:T(8,128)(2,1)S(1)}, u32[]{:S(2)}, u32[]{:S(2)}) collective-permute-start(bf16[768,256]{1,0:T(8,128)(2,1)S(1)} %pad_maximum_fusion.4), channel_id=1, source_target_pairs={{0,1},{1,0},{2,3},{3,2},{4,5},{5,4},{6,7},{7,6},{8,9},{9,8},{10,11... | collective-permute-start | bytes 1179656 | tf_op jit(solution)/shard_map/ppermute | solution.py:108
  161.0 8.2 %collective-permute-start.25 = (bf16[512,256]{1,0:T(8,128)(2,1)S(1)}, bf16[512,256]{1,0:T(8,128)(2,1)S(1)}, u32[]{:S(2)}, u32[]{:S(2)}) collective-permute-start(bf16[512,256]{1,0:T(8,128)(2,1)S(1)} %fusion.2), channel_id=1, source_target_pairs={{0,2},{1,3},{2,4},{3,5},{4,6},{5,7},{6,0},{7,1},{8,10},{9,11},{10,... | collective-permute-start | bytes 786440 | tf_op jit(solution)/shard_map/ppermute | solution.py:12
  169.6 10.5 %collective-permute-start.31 = (bf16[512,256]{1,0:T(8,128)(2,1)S(1)}, bf16[512,256]{1,0:T(8,128)(2,1)S(1)}, u32[]{:S(2)}, u32[]{:S(2)}) collective-permute-start(bf16[512,256]{1,0:T(8,128)(2,1)S(1)} %add_convert_fusion.3), channel_id=1, source_target_pairs={{0,2},{1,3},{2,4},{3,5},{4,6},{5,7},{6,0},{7,1},{8,10},{9,11},{10,... | collective-permute-start | bytes 786440 | tf_op jit(solution)/shard_map/ppermute | solution.py:12
  170.9 14.8 %collective-permute-start.34 = (bf16[512,256]{1,0:T(8,128)(2,1)S(1)}, bf16[512,256]{1,0:T(8,128)(2,1)S(1)}, u32[]{:S(2)}, u32[]{:S(2)}) collective-permute-start(bf16[512,256]{1,0:T(8,128)(2,1)S(1)} %fusion.3), channel_id=1, source_target_pairs={{0,2},{1,3},{2,4},{3,5},{4,6},{5,7},{6,0},{7,1},{8,10},{9,11},{10,... | collective-permute-start | bytes 786440 | tf_op jit(solution)/shard_map/ppermute | solution.py:12
  180.4 10.0 %collective-permute-start.32 = (bf16[512,256]{1,0:T(8,128)(2,1)S(1)}, bf16[512,256]{1,0:T(8,128)(2,1)S(1)}, u32[]{:S(2)}, u32[]{:S(2)}) collective-permute-start(bf16[512,256]{1,0:T(8,128)(2,1)S(1)} %add_convert_fusion.2), channel_id=1, source_target_pairs={{0,2},{1,3},{2,4},{3,5},{4,6},{5,7},{6,0},{7,1},{8,10},{9,11},{10,... | collective-permute-start | bytes 786440 | tf_op jit(solution)/shard_map/ppermute | solution.py:12
  186.0 8.3 %collective-permute-start.35 = (bf16[512,256]{1,0:T(8,128)(2,1)S(1)}, bf16[512,256]{1,0:T(8,128)(2,1)S(1)}, u32[]{:S(2)}, u32[]{:S(2)}) collective-permute-start(bf16[512,256]{1,0:T(8,128)(2,1)S(1)} %add_convert_fusion.1), channel_id=1, source_target_pairs={{0,2},{1,3},{2,4},{3,5},{4,6},{5,7},{6,0},{7,1},{8,10},{9,11},{10,... | collective-permute-start | bytes 786440 | tf_op jit(solution)/shard_map/ppermute | solution.py:12
  194.7 8.2 %collective-permute-start.36 = (bf16[512,256]{1,0:T(8,128)(2,1)S(1)}, bf16[512,256]{1,0:T(8,128)(2,1)S(1)}, u32[]{:S(2)}, u32[]{:S(2)}) collective-permute-start(bf16[512,256]{1,0:T(8,128)(2,1)S(1)} %add_convert_fusion), channel_id=1, source_target_pairs={{0,2},{1,3},{2,4},{3,5},{4,6},{5,7},{6,0},{7,1},{8,10},{9,11},{10,... | collective-permute-start | bytes 786440 | tf_op jit(solution)/shard_map/ppermute | solution.py:12
  (10 other events, 97.0 us)

commit v5 on v4

--- a/solution.py
+++ b/solution.py
@@ -1,6 +1,8 @@
 import jax
 import jax.numpy as jnp
 from jax import lax
+from jax.experimental import pallas as pl
+from jax.experimental.pallas import tpu as pltpu
 from jax.sharding import PartitionSpec as P
 
 STEPS = 2
@@ -14,6 +16,40 @@
 
 def tie(*values):
     return lax.optimization_barrier(values)
+
+
+def select_columns(inputs, starts, block):
+    rows = inputs.shape[0]
+    count = starts.shape[0]
+
+    def kernel(starts_ref, inputs_ref, out_ref, sems):
+        copies = []
+        for i in range(count):
+            start = pl.multiple_of(starts_ref[i], block)
+            copies.append(
+                pltpu.make_async_copy(
+                    inputs_ref.at[:, pl.ds(start, block)],
+                    out_ref.at[:, pl.ds(i * block, block)],
+                    sems.at[i],
+                )
+            )
+        for copy in copies:
+            copy.start()
+        for copy in copies:
+            copy.wait()
+
+    size = rows * count * block * inputs.dtype.itemsize
+    return pl.pallas_call(
+        kernel,
+        out_shape=jax.ShapeDtypeStruct((rows, count * block), inputs.dtype),
+        in_specs=[
+            pl.BlockSpec(memory_space=pltpu.SMEM),
+            pl.BlockSpec(memory_space=pl.ANY),
+        ],
+        out_specs=pl.BlockSpec(memory_space=pl.ANY),
+        scratch_shapes=[pltpu.SemaphoreType.DMA((count,))],
+        cost_estimate=pl.CostEstimate(flops=0, bytes_accessed=2 * size, transcendentals=0),
+    )(starts, inputs)
 
 
 def shards(tokens, targets, params, momentum, push_weight):
@@ -42,7 +78,10 @@
             pieces.append(lax.dynamic_slice_in_dim(inputs, start, block, 1))
         return jnp.concatenate(pieces, axis=1)
 
-    outgoing, params, momentum = tie(half_columns(1 - lane), params, momentum)
+    behind = [lax.rem(place - back + half, half) for back in range(half)]
+    starts = jnp.stack([(2 * at + 1 - lane) * block for at in behind])
+    outgoing = select_columns(inputs, starts.astype(jnp.int32), block)
+    outgoing, params, momentum, push_weight = tie(outgoing, params, momentum, push_weight)
     theirs = lax.ppermute(outgoing, "fsdp", swap)
     mine = half_columns(lane)
 
@@ -52,9 +91,8 @@
     def column_block(array, back):
         return array[:, back * block : (back + 1) * block]
 
-    def gather(rows_in):
-        pieces = [rows_in]
-        for _ in range(half - 1):
+    def gather(pieces):
+        while len(pieces) < half:
             pieces.append(from_behind(pieces[-1], "fsdp", 2))
         return pieces
 
@@ -83,7 +121,7 @@
     for step in range(STEPS):
         last = step == STEPS - 1
         if step == 0:
-            debiased = [debias(state[c], weights[step]) for c in range(2)]
+            debiased = [[debias(state[c], weights[step])] for c in range(2)]
         pieces = [gather(debiased[c]) for c in range(2)]
         if step == 0:
             whole = params[0] - (0.2 * 0.9) * momentum[0]
@@ -93,10 +131,11 @@
         else:
             before = [state[c] - (0.2 * 0.9) * moment[c] for c in range(2)]
             before = list(tie(*before))
-            got = from_behind(before[0], "group", 2**step)
+            got = from_behind(before[0].astype(narrow), "group", 2**step)
             got, before[1] = tie(got, before[1])
-            before[0] = 0.5 * (before[0] + got)
-            before[1] = 0.5 * (before[1] + from_behind(before[1], "group", 2**step))
+            before[0] = 0.5 * (before[0] + got.astype(wide))
+            got = from_behind(before[1].astype(narrow), "group", 2**step)
+            before[1] = 0.5 * (before[1] + got.astype(wide))
 
         own = [product(mine, pieces[c], -target[c]) for c in range(2)]
         other = [product(theirs, pieces[c], 0.0) for c in range(2)]
@@ -134,7 +173,10 @@
                 state[c], moment[c] = tie(state[c], moment[c])
                 debiased[c] = debias(state[c], weights[step + 1])
                 if c == 0:
-                    debiased[c], arrived[1] = tie(debiased[c], arrived[1])
+                    debiased[c] = [debiased[c], from_behind(debiased[c], "fsdp", 2)]
+                    debiased[c][1], arrived[1] = tie(debiased[c][1], arrived[1])
+                else:
+                    debiased[c] = [debiased[c]]
     new_params = jnp.concatenate([s / weights[STEPS][0] for s in state], axis=1)
     return new_params[None], jnp.concatenate(moment, axis=1)[None]
 

time: 212 us -> 257 us (1.21)
  Pallas kernels: 0 us -> 49.6 us
  waiting for transfers between devices: 154 us -> 147 us
  starting transfers between devices: 19 us -> 23.3 us
    pallas_call x0 -> x1, Pallas kernels: none -> 49.6 us  [select_columns(): pl.pallas_call(kernel, out_shape=jax.ShapeDtypeStruct((rows, count * bloc...]
    ppermute x33, waiting for transfers between devices: 141 us -> 128 us  [from_behind(): return lax.ppermute(value, axis, pairs)]
    ppermute x4, waiting for transfers between devices: 13.7 us -> 19 us  [shards(): got.append(lax.ppermute(sent, 'fsdp', swap))]
    ppermute x33, starting transfers between devices: 13.2 us -> 17.4 us  [from_behind(): return lax.ppermute(value, axis, pairs)]
  transfers between devices with their start and end apart: 38 -> 38, of which waited for: 28 -> 27; matrix products, arithmetic and copies ran while one was open for 13% -> 10% of each run, Pallas kernels for 0% -> 0%
where the time goes in v5:
time: 257 us; the launch traced here: 256 us
  waiting for transfers between devices  147 us (57%)
  Pallas kernels  49.6 us (19%)
  matrix products  26.4 us (10%)
  starting transfers between devices  23.3 us (9%)
  other arithmetic  6.09 us (2%)
  between operations  3.62 us (1%)
    ppermute x33, waiting for transfers between devices, from_behind(): return lax.ppermute(value, axis, pairs)  128 us
    pallas_call x1, Pallas kernels, select_columns(): pl.pallas_call(kernel, out_shape=jax.ShapeDtypeStruct((rows, count * bloc...  49.6 us
    ppermute x4, waiting for transfers between devices, shards(): got.append(lax.ppermute(sent, 'fsdp', swap))  19 us
    ppermute x33, starting transfers between devices, from_behind(): return lax.ppermute(value, axis, pairs)  17.4 us
    dot_general x32, matrix products, product(): jnp.dot(column_block(left, back), piece, preferred_element_type=wide)  15.5 us
    dot_general x16, matrix products, partial(): lax.dot_general(column_block(mine, back), own_grad, contract, preferred_e...  5.45 us
    dot_general x16, matrix products, partial(): lax.dot_general(column_block(theirs, back), other_grad, contract, preferr...  5.4 us
  transfers between devices with their start and end apart: 38, of which 27 were waited for; matrix products, arithmetic and copies ran while one was open for 10% of the time, Pallas kernels for 0%

profile of v5, /device:TPU:0, one launch (start us, length us, event | category | flops | bytes accessed | tf_op | source)
XLA Modules:
  0.0 256.4 jit_solution(10128851337413316512)
XLA Ops:
  1.9 49.6 %shard_map.68 = bf16[384,2048]{1,0:T(8,128)(2,1)} custom-call(s32[4]{0:T(128)} %pad_add_fusion.starts_ref, bf16[384,4096]{1,0:T(8,128)(2,1)} %bitcast.158), custom_call_target="tpu_custom_call" | custom-call | bytes 3145728 | tf_op jit(solution)/shard_map/pallas_call | solution.py:42
  51.6 3.1 %collective-permute-start.1 = (bf16[512,256]{1,0:T(8,128)(2,1)S(1)}, bf16[512,256]{1,0:T(8,128)(2,1)}, u32[]{:S(2)}, u32[]{:S(2)}) collective-permute-start(bf16[512,256]{1,0:T(8,128)(2,1)S(1)} %get-tuple-element.63), channel_id=1, source_target_pairs={{0,2},{1,3},{2,4},{3,5},{4,6},{5,7},{6,0},{7,1},{8,10},{9,11},{10,... | collective-permute-start | bytes 786440 | tf_op jit(solution)/shard_map/ppermute | solution.py:14
  57.8 1.8 multiply_subtract_fusion
  59.6 2.0 fusion.5
  63.7 2.9 %collective-permute-start.5 = (f32[1]{0:T(128)}, f32[1]{0:T(128)}, u32[]{:S(2)}, u32[]{:S(2)}) collective-permute-start(f32[1]{0:T(128)} %add.328), channel_id=1, source_target_pairs={{0,16},{8,24},{16,0},{24,8},{1,17},{9,25},{17,1},{25,9},{2,18},{10... | collective-permute-start | bytes 20 | tf_op jit(solution)/shard_map/ppermute | solution.py:14
  73.4 6.5 %collective-permute-done.2 = bf16[512,256]{1,0:T(8,128)(2,1)S(1)} collective-permute-done((bf16[512,256]{1,0:T(8,128)(2,1)}, bf16[512,256]{1,0:T(8,128)(2,1)S(1)}, u32[]{:S(2)}, u32[]{:S(2)}) %collective-permute-start.2) | collective-permute-done | bytes 262176 | tf_op jit(solution)/shard_map/ppermute | solution.py:14
  79.9 5.6 %collective-permute-done.10 = bf16[512,256]{1,0:T(8,128)(2,1)S(1)} collective-permute-done((bf16[512,256]{1,0:T(8,128)(2,1)}, bf16[512,256]{1,0:T(8,128)(2,1)S(1)}, u32[]{:S(2)}, u32[]{:S(2)}) %collective-permute-start.10) | collective-permute-done | bytes 262176 | tf_op jit(solution)/shard_map/ppermute | solution.py:14
  86.0 5.1 %collective-permute-done.3 = bf16[512,256]{1,0:T(8,128)(2,1)S(1)} collective-permute-done((bf16[512,256]{1,0:T(8,128)(2,1)S(1)}, bf16[512,256]{1,0:T(8,128)(2,1)S(1)}, u32[]{:S(2)}, u32[]{:S(2)}) %collective-permute-start.3) | collective-permute-done | bytes 262176 | tf_op jit(solution)/shard_map/ppermute | solution.py:14
  91.4 5.3 %collective-permute-done.11 = bf16[512,256]{1,0:T(8,128)(2,1)S(1)} collective-permute-done((bf16[512,256]{1,0:T(8,128)(2,1)S(1)}, bf16[512,256]{1,0:T(8,128)(2,1)S(1)}, u32[]{:S(2)}, u32[]{:S(2)}) %collective-permute-start.11) | collective-permute-done | bytes 262176 | tf_op jit(solution)/shard_map/ppermute | solution.py:14
  103.6 7.8 %collective-permute-done.7 = bf16[768,256]{1,0:T(8,128)(2,1)S(1)} collective-permute-done((bf16[768,256]{1,0:T(8,128)(2,1)S(1)}, bf16[768,256]{1,0:T(8,128)(2,1)S(1)}, u32[]{:S(2)}, u32[]{:S(2)}) %collective-permute-start.7) | collective-permute-done | bytes 393248 | tf_op jit(solution)/shard_map/ppermute | solution.py:147
  113.4 5.6 %collective-permute-done.12 = bf16[768,256]{1,0:T(8,128)(2,1)S(1)} collective-permute-done((bf16[768,256]{1,0:T(8,128)(2,1)S(1)}, bf16[768,256]{1,0:T(8,128)(2,1)S(1)}, u32[]{:S(2)}, u32[]{:S(2)}) %collective-permute-start.12) | collective-permute-done | bytes 393248 | tf_op jit(solution)/shard_map/ppermute | solution.py:147
  119.0 2.1 collective-permute-done.8
  123.2 9.4 %collective-permute-done.13 = bf16[512,256]{1,0:T(8,128)(2,1)S(1)} collective-permute-done((bf16[512,256]{1,0:T(8,128)(2,1)S(1)}, bf16[512,256]{1,0:T(8,128)(2,1)S(1)}, u32[]{:S(2)}, u32[]{:S(2)}) %collective-permute-start.13) | collective-permute-done | bytes 262176 | tf_op jit(solution)/shard_map/ppermute | solution.py:14
  133.0 5.2 %collective-permute-done.17 = bf16[512,256]{1,0:T(8,128)(2,1)S(1)} collective-permute-done((bf16[512,256]{1,0:T(8,128)(2,1)S(1)}, bf16[512,256]{1,0:T(8,128)(2,1)S(1)}, u32[]{:S(2)}, u32[]{:S(2)}) %collective-permute-start.17) | collective-permute-done | bytes 262176 | tf_op jit(solution)/shard_map/ppermute | solution.py:14
  138.6 4.5 %collective-permute-done.14 = bf16[512,256]{1,0:T(8,128)(2,1)S(1)} collective-permute-done((bf16[512,256]{1,0:T(8,128)(2,1)S(1)}, bf16[512,256]{1,0:T(8,128)(2,1)S(1)}, u32[]{:S(2)}, u32[]{:S(2)}) %collective-permute-start.14) | collective-permute-done | bytes 262176 | tf_op jit(solution)/shard_map/ppermute | solution.py:14
  143.6 3.2 %collective-permute-done.18 = bf16[512,256]{1,0:T(8,128)(2,1)S(1)} collective-permute-done((bf16[512,256]{1,0:T(8,128)(2,1)S(1)}, bf16[512,256]{1,0:T(8,128)(2,1)S(1)}, u32[]{:S(2)}, u32[]{:S(2)}) %collective-permute-start.18) | collective-permute-done | bytes 262176 | tf_op jit(solution)/shard_map/ppermute | solution.py:14
  147.2 2.1 collective-permute-done.15
  150.0 6.7 %collective-permute-done.19 = bf16[512,256]{1,0:T(8,128)(2,1)S(1)} collective-permute-done((bf16[512,256]{1,0:T(8,128)(2,1)S(1)}, bf16[512,256]{1,0:T(8,128)(2,1)S(1)}, u32[]{:S(2)}, u32[]{:S(2)}) %collective-permute-start.19) | collective-permute-done | bytes 262176 | tf_op jit(solution)/shard_map/ppermute | solution.py:14
  156.7 2.8 %collective-permute-done.16 = bf16[512,256]{1,0:T(8,128)(2,1)S(1)} collective-permute-done((bf16[512,256]{1,0:T(8,128)(2,1)S(1)}, bf16[512,256]{1,0:T(8,128)(2,1)S(1)}, u32[]{:S(2)}, u32[]{:S(2)}) %collective-permute-start.16) | collective-permute-done | bytes 262176 | tf_op jit(solution)/shard_map/ppermute | solution.py:14
  160.7 5.0 %collective-permute-done.22 = bf16[512,256]{1,0:T(8,128)(2,1)S(1)} collective-permute-done((bf16[512,256]{1,0:T(8,128)(2,1)S(1)}, bf16[512,256]{1,0:T(8,128)(2,1)S(1)}, u32[]{:S(2)}, u32[]{:S(2)}) %collective-permute-start.22) | collective-permute-done | bytes 262176 | tf_op jit(solution)/shard_map/ppermute | solution.py:14
  166.0 2.3 collective-permute-start.23
  171.2 11.4 %collective-permute-done.21 = bf16[512,256]{1,0:T(8,128)(2,1)S(1)} collective-permute-done((bf16[512,256]{1,0:T(8,128)(2,1)S(1)}, bf16[512,256]{1,0:T(8,128)(2,1)S(1)}, u32[]{:S(2)}, u32[]{:S(2)}) %collective-permute-start.21) | collective-permute-done | bytes 262176 | tf_op jit(solution)/shard_map/ppermute | solution.py:14
  186.0 7.5 %collective-permute-done.27 = bf16[512,256]{1,0:T(8,128)(2,1)S(1)} collective-permute-done((bf16[512,256]{1,0:T(8,128)(2,1)S(1)}, bf16[512,256]{1,0:T(8,128)(2,1)S(1)}, u32[]{:S(2)}, u32[]{:S(2)}) %collective-permute-start.27) | collective-permute-done | bytes 262176 | tf_op jit(solution)/shard_map/ppermute | solution.py:14
  195.4 8.3 %collective-permute-done.28 = bf16[512,256]{1,0:T(8,128)(2,1)S(1)} collective-permute-done((bf16[512,256]{1,0:T(8,128)(2,1)S(1)}, bf16[512,256]{1,0:T(8,128)(2,1)S(1)}, u32[]{:S(2)}, u32[]{:S(2)}) %collective-permute-start.28) | collective-permute-done | bytes 262176 | tf_op jit(solution)/shard_map/ppermute | solution.py:14
  206.6 5.5 %collective-permute-done.29 = bf16[768,256]{1,0:T(8,128)(2,1)S(1)} collective-permute-done((bf16[768,256]{1,0:T(8,128)(2,1)S(1)}, bf16[768,256]{1,0:T(8,128)(2,1)S(1)}, u32[]{:S(2)}, u32[]{:S(2)}) %collective-permute-start.29) | collective-permute-done | bytes 393248 | tf_op jit(solution)/shard_map/ppermute | solution.py:147
  214.2 9.3 %collective-permute-done.31 = bf16[512,256]{1,0:T(8,128)(2,1)S(1)} collective-permute-done((bf16[512,256]{1,0:T(8,128)(2,1)S(1)}, bf16[512,256]{1,0:T(8,128)(2,1)S(1)}, u32[]{:S(2)}, u32[]{:S(2)}) %collective-permute-start.31) | collective-permute-done | bytes 262176 | tf_op jit(solution)/shard_map/ppermute | solution.py:14
  224.0 5.0 %collective-permute-done.34 = bf16[512,256]{1,0:T(8,128)(2,1)S(1)} collective-permute-done((bf16[512,256]{1,0:T(8,128)(2,1)S(1)}, bf16[512,256]{1,0:T(8,128)(2,1)S(1)}, u32[]{:S(2)}, u32[]{:S(2)}) %collective-permute-start.34) | collective-permute-done | bytes 262176 | tf_op jit(solution)/shard_map/ppermute | solution.py:14
  229.4 2.7 %collective-permute-done.32 = bf16[512,256]{1,0:T(8,128)(2,1)S(1)} collective-permute-done((bf16[512,256]{1,0:T(8,128)(2,1)S(1)}, bf16[512,256]{1,0:T(8,128)(2,1)S(1)}, u32[]{:S(2)}, u32[]{:S(2)}) %collective-permute-start.32) | collective-permute-done | bytes 262176 | tf_op jit(solution)/shard_map/ppermute | solution.py:14
  233.8 5.5 %collective-permute-done.35 = bf16[512,256]{1,0:T(8,128)(2,1)S(1)} collective-permute-done((bf16[512,256]{1,0:T(8,128)(2,1)S(1)}, bf16[512,256]{1,0:T(8,128)(2,1)S(1)}, u32[]{:S(2)}, u32[]{:S(2)}) %collective-permute-start.35) | collective-permute-done | bytes 262176 | tf_op jit(solution)/shard_map/ppermute | solution.py:14
  240.0 7.8 %collective-permute-done.36 = bf16[512,256]{1,0:T(8,128)(2,1)S(1)} collective-permute-done((bf16[512,256]{1,0:T(8,128)(2,1)S(1)}, bf16[512,256]{1,0:T(8,128)(2,1)S(1)}, u32[]{:S(2)}, u32[]{:S(2)}) %collective-permute-start.36) | collective-permute-done | bytes 262176 | tf_op jit(solution)/shard_map/ppermute | solution.py:14
  249.7 4.9 %collective-permute-done.37 = bf16[512,256]{1,0:T(8,128)(2,1)S(1)} collective-permute-done((bf16[512,256]{1,0:T(8,128)(2,1)S(1)}, bf16[512,256]{1,0:T(8,128)(2,1)S(1)}, u32[]{:S(2)}, u32[]{:S(2)}) %collective-permute-start.37) | collective-permute-done | bytes 262176 | tf_op jit(solution)/shard_map/ppermute | solution.py:14
  254.8 1.6 maximum_bitcast_fusion
  (145 shorter events, 44.4 us)
Async XLA Ops:
  51.6 17.1 %collective-permute-start.1 = (bf16[512,256]{1,0:T(8,128)(2,1)S(1)}, bf16[512,256]{1,0:T(8,128)(2,1)}, u32[]{:S(2)}, u32[]{:S(2)}) collective-permute-start(bf16[512,256]{1,0:T(8,128)(2,1)S(1)} %get-tuple-element.63), channel_id=1, source_target_pairs={{0,2},{1,3},{2,4},{3,5},{4,6},{5,7},{6,0},{7,1},{8,10},{9,11},{10,... | collective-permute-start | bytes 786440 | tf_op jit(solution)/shard_map/ppermute | solution.py:14
  54.7 42.6 %collective-permute-start = (bf16[384,2048]{1,0:T(8,128)(2,1)}, bf16[384,2048]{1,0:T(8,128)(2,1)S(1)}, u32[]{:S(2)}, u32[]{:S(2)}) collective-permute-start(bf16[384,2048]{1,0:T(8,128)(2,1)} %shard_map.68), channel_id=1, source_target_pairs={{0,1},{1,0},{2,3},{3,2},{4,5},{5,4},{6,7},{7,6},{8,9},{9,8},{10,11... | collective-permute-start | bytes 4718600 | tf_op jit(solution)/shard_map/ppermute | solution.py:85
  56.2 14.0 %collective-permute-start.9 = (bf16[512,256]{1,0:T(8,128)(2,1)S(1)}, bf16[512,256]{1,0:T(8,128)(2,1)}, u32[]{:S(2)}, u32[]{:S(2)}) collective-permute-start(bf16[512,256]{1,0:T(8,128)(2,1)S(1)} %get-tuple-element.62), channel_id=1, source_target_pairs={{0,2},{1,3},{2,4},{3,5},{4,6},{5,7},{6,0},{7,1},{8,10},{9,11},{10,... | collective-permute-start | bytes 786440 | tf_op jit(solution)/shard_map/ppermute | solution.py:14
  68.0 29.0 %collective-permute-start.6 = (f32[512,512]{1,0:T(8,128)S(1)}, f32[512,512]{1,0:T(8,128)S(1)}, u32[]{:S(2)}, u32[]{:S(2)}) collective-permute-start(f32[512,512]{1,0:T(8,128)S(1)} %multiply_subtract_fusion), channel_id=1, source_target_pairs={{0,8},{8,16},{16,24},{24,0},{1,9},{9,17},{17,25},{25,1},{2,10},{10... | collective-permute-start | bytes 3145736 | tf_op jit(solution)/shard_map/ppermute | solution.py:14
  68.7 11.2 %collective-permute-start.2 = (bf16[512,256]{1,0:T(8,128)(2,1)}, bf16[512,256]{1,0:T(8,128)(2,1)S(1)}, u32[]{:S(2)}, u32[]{:S(2)}) collective-permute-start(bf16[512,256]{1,0:T(8,128)(2,1)} %collective-permute-done.1), channel_id=1, source_target_pairs={{0,2},{1,3},{2,4},{3,5},{4,6},{5,7},{6,0},{7,1},{8,10},{9,11},{10,... | collective-permute-start | bytes 786440 | tf_op jit(solution)/shard_map/ppermute | solution.py:14
  70.2 15.3 %collective-permute-start.10 = (bf16[512,256]{1,0:T(8,128)(2,1)}, bf16[512,256]{1,0:T(8,128)(2,1)S(1)}, u32[]{:S(2)}, u32[]{:S(2)}) collective-permute-start(bf16[512,256]{1,0:T(8,128)(2,1)} %collective-permute-done.9), channel_id=1, source_target_pairs={{0,2},{1,3},{2,4},{3,5},{4,6},{5,7},{6,0},{7,1},{8,10},{9,11},{10,... | collective-permute-start | bytes 786440 | tf_op jit(solution)/shard_map/ppermute | solution.py:14
  79.9 11.2 %collective-permute-start.3 = (bf16[512,256]{1,0:T(8,128)(2,1)S(1)}, bf16[512,256]{1,0:T(8,128)(2,1)S(1)}, u32[]{:S(2)}, u32[]{:S(2)}) collective-permute-start(bf16[512,256]{1,0:T(8,128)(2,1)S(1)} %collective-permute-done.2), channel_id=1, source_target_pairs={{0,2},{1,3},{2,4},{3,5},{4,6},{5,7},{6,0},{7,1},{8,10},{9,11},{10,... | collective-permute-start | bytes 786440 | tf_op jit(solution)/shard_map/ppermute | solution.py:14
  85.5 11.2 %collective-permute-start.11 = (bf16[512,256]{1,0:T(8,128)(2,1)S(1)}, bf16[512,256]{1,0:T(8,128)(2,1)S(1)}, u32[]{:S(2)}, u32[]{:S(2)}) collective-permute-start(bf16[512,256]{1,0:T(8,128)(2,1)S(1)} %collective-permute-done.10), channel_id=1, source_target_pairs={{0,2},{1,3},{2,4},{3,5},{4,6},{5,7},{6,0},{7,1},{8,10},{9,11},{10,... | collective-permute-start | bytes 786440 | tf_op jit(solution)/shard_map/ppermute | solution.py:14
  99.4 12.0 %collective-permute-start.7 = (bf16[768,256]{1,0:T(8,128)(2,1)S(1)}, bf16[768,256]{1,0:T(8,128)(2,1)S(1)}, u32[]{:S(2)}, u32[]{:S(2)}) collective-permute-start(bf16[768,256]{1,0:T(8,128)(2,1)S(1)} %pad_maximum_fusion), channel_id=1, source_target_pairs={{0,1},{1,0},{2,3},{3,2},{4,5},{5,4},{6,7},{7,6},{8,9},{9,8},{10,11... | collective-permute-start | bytes 1179656 | tf_op jit(solution)/shard_map/ppermute | solution.py:147
  102.0 17.0 %collective-permute-start.12 = (bf16[768,256]{1,0:T(8,128)(2,1)S(1)}, bf16[768,256]{1,0:T(8,128)(2,1)S(1)}, u32[]{:S(2)}, u32[]{:S(2)}) collective-permute-start(bf16[768,256]{1,0:T(8,128)(2,1)S(1)} %pad_maximum_fusion.1), channel_id=1, source_target_pairs={{0,1},{1,0},{2,3},{3,2},{4,5},{5,4},{6,7},{7,6},{8,9},{9,8},{10,11... | collective-permute-start | bytes 1179656 | tf_op jit(solution)/shard_map/ppermute | solution.py:147
  112.6 8.5 %collective-permute-start.8 = (bf16[512,256]{1,0:T(8,128)(2,1)S(1)}, bf16[512,256]{1,0:T(8,128)(2,1)S(1)}, u32[]{:S(2)}, u32[]{:S(2)}) collective-permute-start(bf16[512,256]{1,0:T(8,128)(2,1)S(1)} %fusion), channel_id=1, source_target_pairs={{0,2},{1,3},{2,4},{3,5},{4,6},{5,7},{6,0},{7,1},{8,10},{9,11},{10,... | collective-permute-start | bytes 786440 | tf_op jit(solution)/shard_map/ppermute | solution.py:14
  121.5 11.1 %collective-permute-start.13 = (bf16[512,256]{1,0:T(8,128)(2,1)S(1)}, bf16[512,256]{1,0:T(8,128)(2,1)S(1)}, u32[]{:S(2)}, u32[]{:S(2)}) collective-permute-start(bf16[512,256]{1,0:T(8,128)(2,1)S(1)} %add_convert_fusion.7), channel_id=1, source_target_pairs={{0,2},{1,3},{2,4},{3,5},{4,6},{5,7},{6,0},{7,1},{8,10},{9,11},{10,... | collective-permute-start | bytes 786440 | tf_op jit(solution)/shard_map/ppermute | solution.py:14
  122.8 15.4 %collective-permute-start.17 = (bf16[512,256]{1,0:T(8,128)(2,1)S(1)}, bf16[512,256]{1,0:T(8,128)(2,1)S(1)}, u32[]{:S(2)}, u32[]{:S(2)}) collective-permute-start(bf16[512,256]{1,0:T(8,128)(2,1)S(1)} %fusion.1), channel_id=1, source_target_pairs={{0,2},{1,3},{2,4},{3,5},{4,6},{5,7},{6,0},{7,1},{8,10},{9,11},{10,... | collective-permute-start | bytes 786440 | tf_op jit(solution)/shard_map/ppermute | solution.py:14
  132.9 10.2 %collective-permute-start.14 = (bf16[512,256]{1,0:T(8,128)(2,1)S(1)}, bf16[512,256]{1,0:T(8,128)(2,1)S(1)}, u32[]{:S(2)}, u32[]{:S(2)}) collective-permute-start(bf16[512,256]{1,0:T(8,128)(2,1)S(1)} %add_convert_fusion.6), channel_id=1, source_target_pairs={{0,2},{1,3},{2,4},{3,5},{4,6},{5,7},{6,0},{7,1},{8,10},{9,11},{10,... | collective-permute-start | bytes 786440 | tf_op jit(solution)/shard_map/ppermute | solution.py:14
  138.6 8.2 %collective-permute-start.18 = (bf16[512,256]{1,0:T(8,128)(2,1)S(1)}, bf16[512,256]{1,0:T(8,128)(2,1)S(1)}, u32[]{:S(2)}, u32[]{:S(2)}) collective-permute-start(bf16[512,256]{1,0:T(8,128)(2,1)S(1)} %add_convert_fusion.5), channel_id=1, source_target_pairs={{0,2},{1,3},{2,4},{3,5},{4,6},{5,7},{6,0},{7,1},{8,10},{9,11},{10,... | collective-permute-start | bytes 786440 | tf_op jit(solution)/shard_map/ppermute | solution.py:14
  147.1 9.6 %collective-permute-start.19 = (bf16[512,256]{1,0:T(8,128)(2,1)S(1)}, bf16[512,256]{1,0:T(8,128)(2,1)S(1)}, u32[]{:S(2)}, u32[]{:S(2)}) collective-permute-start(bf16[512,256]{1,0:T(8,128)(2,1)S(1)} %add_convert_fusion.4), channel_id=1, source_target_pairs={{0,2},{1,3},{2,4},{3,5},{4,6},{5,7},{6,0},{7,1},{8,10},{9,11},{10,... | collective-permute-start | bytes 786440 | tf_op jit(solution)/shard_map/ppermute | solution.py:14
  149.6 9.9 %collective-permute-start.16 = (bf16[512,256]{1,0:T(8,128)(2,1)S(1)}, bf16[512,256]{1,0:T(8,128)(2,1)S(1)}, u32[]{:S(2)}, u32[]{:S(2)}) collective-permute-start(bf16[512,256]{1,0:T(8,128)(2,1)S(1)} %get-tuple-element.83), channel_id=1, source_target_pairs={{0,2},{1,3},{2,4},{3,5},{4,6},{5,7},{6,0},{7,1},{8,10},{9,11},{10,... | collective-permute-start | bytes 786440 | tf_op jit(solution)/shard_map/ppermute | solution.py:14
  160.2 9.8 %collective-permute-start.20 = (bf16[512,256]{1,0:T(8,128)(2,1)S(1)}, bf16[512,256]{1,0:T(8,128)(2,1)S(1)}, u32[]{:S(2)}, u32[]{:S(2)}) collective-permute-start(bf16[512,256]{1,0:T(8,128)(2,1)S(1)} %collective-permute-done.16), channel_id=1, source_target_pairs={{0,2},{1,3},{2,4},{3,5},{4,6},{5,7},{6,0},{7,1},{8,10},{9,11},{10,... | collective-permute-start | bytes 786440 | tf_op jit(solution)/shard_map/ppermute | solution.py:14
  166.0 17.2 %collective-permute-start.23 = (bf16[512,256]{1,0:T(8,128)(2,1)S(1)}, bf16[512,256]{1,0:T(8,128)(2,1)S(1)}, u32[]{:S(2)}, u32[]{:S(2)}) collective-permute-start(bf16[512,256]{1,0:T(8,128)(2,1)S(1)} %convert_element_type.193), channel_id=1, source_target_pairs={{0,16},{8,24},{16,0},{24,8},{1,17},{9,25},{17,1},{25,9},{2,18},{10... | collective-permute-start | bytes 786440 | tf_op jit(solution)/shard_map/ppermute | solution.py:14
  168.3 16.9 %collective-permute-start.26 = (bf16[512,256]{1,0:T(8,128)(2,1)S(1)}, bf16[512,256]{1,0:T(8,128)(2,1)S(1)}, u32[]{:S(2)}, u32[]{:S(2)}) collective-permute-start(bf16[512,256]{1,0:T(8,128)(2,1)S(1)} %get-tuple-element.80), channel_id=1, source_target_pairs={{0,2},{1,3},{2,4},{3,5},{4,6},{5,7},{6,0},{7,1},{8,10},{9,11},{10,... | collective-permute-start | bytes 786440 | tf_op jit(solution)/shard_map/ppermute | solution.py:14
  170.3 12.3 %collective-permute-start.21 = (bf16[512,256]{1,0:T(8,128)(2,1)S(1)}, bf16[512,256]{1,0:T(8,128)(2,1)S(1)}, u32[]{:S(2)}, u32[]{:S(2)}) collective-permute-start(bf16[512,256]{1,0:T(8,128)(2,1)S(1)} %collective-permute-done.20), channel_id=1, source_target_pairs={{0,2},{1,3},{2,4},{3,5},{4,6},{5,7},{6,0},{7,1},{8,10},{9,11},{10,... | collective-permute-start | bytes 786440 | tf_op jit(solution)/shard_map/ppermute | solution.py:14
  183.3 10.8 %collective-permute-start.24 = (bf16[768,256]{1,0:T(8,128)(2,1)S(1)}, bf16[768,256]{1,0:T(8,128)(2,1)S(1)}, u32[]{:S(2)}, u32[]{:S(2)}) collective-permute-start(bf16[768,256]{1,0:T(8,128)(2,1)S(1)} %pad_maximum_fusion.2), channel_id=1, source_target_pairs={{0,1},{1,0},{2,3},{3,2},{4,5},{5,4},{6,7},{7,6},{8,9},{9,8},{10,11... | collective-permute-start | bytes 1179656 | tf_op jit(solution)/shard_map/ppermute | solution.py:147
  183.9 9.6 %collective-permute-start.30 = (bf16[512,256]{1,0:T(8,128)(2,1)S(1)}, bf16[512,256]{1,0:T(8,128)(2,1)S(1)}, u32[]{:S(2)}, u32[]{:S(2)}) collective-permute-start(bf16[512,256]{1,0:T(8,128)(2,1)S(1)} %convert_element_type.200), channel_id=1, source_target_pairs={{0,16},{8,24},{16,0},{24,8},{1,17},{9,25},{17,1},{25,9},{2,18},{10... | collective-permute-start | bytes 786440 | tf_op jit(solution)/shard_map/ppermute | solution.py:14
  185.2 8.4 %collective-permute-start.27 = (bf16[512,256]{1,0:T(8,128)(2,1)S(1)}, bf16[512,256]{1,0:T(8,128)(2,1)S(1)}, u32[]{:S(2)}, u32[]{:S(2)}) collective-permute-start(bf16[512,256]{1,0:T(8,128)(2,1)S(1)} %collective-permute-done.26), channel_id=1, source_target_pairs={{0,2},{1,3},{2,4},{3,5},{4,6},{5,7},{6,0},{7,1},{8,10},{9,11},{10,... | collective-permute-start | bytes 786440 | tf_op jit(solution)/shard_map/ppermute | solution.py:14
  193.5 10.2 %collective-permute-start.28 = (bf16[512,256]{1,0:T(8,128)(2,1)S(1)}, bf16[512,256]{1,0:T(8,128)(2,1)S(1)}, u32[]{:S(2)}, u32[]{:S(2)}) collective-permute-start(bf16[512,256]{1,0:T(8,128)(2,1)S(1)} %collective-permute-done.27), channel_id=1, source_target_pairs={{0,2},{1,3},{2,4},{3,5},{4,6},{5,7},{6,0},{7,1},{8,10},{9,11},{10,... | collective-permute-start | bytes 786440 | tf_op jit(solution)/shard_map/ppermute | solution.py:14
  195.0 11.6 %collective-permute-start.25 = (bf16[512,256]{1,0:T(8,128)(2,1)S(1)}, bf16[512,256]{1,0:T(8,128)(2,1)S(1)}, u32[]{:S(2)}, u32[]{:S(2)}) collective-permute-start(bf16[512,256]{1,0:T(8,128)(2,1)S(1)} %fusion.2), channel_id=1, source_target_pairs={{0,2},{1,3},{2,4},{3,5},{4,6},{5,7},{6,0},{7,1},{8,10},{9,11},{10,... | collective-permute-start | bytes 786440 | tf_op jit(solution)/shard_map/ppermute | solution.py:14
  204.3 7.8 %collective-permute-start.29 = (bf16[768,256]{1,0:T(8,128)(2,1)S(1)}, bf16[768,256]{1,0:T(8,128)(2,1)S(1)}, u32[]{:S(2)}, u32[]{:S(2)}) collective-permute-start(bf16[768,256]{1,0:T(8,128)(2,1)S(1)} %pad_maximum_fusion.3), channel_id=1, source_target_pairs={{0,1},{1,0},{2,3},{3,2},{4,5},{5,4},{6,7},{7,6},{8,9},{9,8},{10,11... | collective-permute-start | bytes 1179656 | tf_op jit(solution)/shard_map/ppermute | solution.py:147
  212.5 11.0 %collective-permute-start.31 = (bf16[512,256]{1,0:T(8,128)(2,1)S(1)}, bf16[512,256]{1,0:T(8,128)(2,1)S(1)}, u32[]{:S(2)}, u32[]{:S(2)}) collective-permute-start(bf16[512,256]{1,0:T(8,128)(2,1)S(1)} %add_convert_fusion.3), channel_id=1, source_target_pairs={{0,2},{1,3},{2,4},{3,5},{4,6},{5,7},{6,0},{7,1},{8,10},{9,11},{10,... | collective-permute-start | bytes 786440 | tf_op jit(solution)/shard_map/ppermute | solution.py:14
  213.8 15.2 %collective-permute-start.34 = (bf16[512,256]{1,0:T(8,128)(2,1)S(1)}, bf16[512,256]{1,0:T(8,128)(2,1)S(1)}, u32[]{:S(2)}, u32[]{:S(2)}) collective-permute-start(bf16[512,256]{1,0:T(8,128)(2,1)S(1)} %fusion.3), channel_id=1, source_target_pairs={{0,2},{1,3},{2,4},{3,5},{4,6},{5,7},{6,0},{7,1},{8,10},{9,11},{10,... | collective-permute-start | bytes 786440 | tf_op jit(solution)/shard_map/ppermute | solution.py:14
  223.9 8.2 %collective-permute-start.32 = (bf16[512,256]{1,0:T(8,128)(2,1)S(1)}, bf16[512,256]{1,0:T(8,128)(2,1)S(1)}, u32[]{:S(2)}, u32[]{:S(2)}) collective-permute-start(bf16[512,256]{1,0:T(8,128)(2,1)S(1)} %add_convert_fusion.2), channel_id=1, source_target_pairs={{0,2},{1,3},{2,4},{3,5},{4,6},{5,7},{6,0},{7,1},{8,10},{9,11},{10,... | collective-permute-start | bytes 786440 | tf_op jit(solution)/shard_map/ppermute | solution.py:14
  229.3 10.0 %collective-permute-start.35 = (bf16[512,256]{1,0:T(8,128)(2,1)S(1)}, bf16[512,256]{1,0:T(8,128)(2,1)S(1)}, u32[]{:S(2)}, u32[]{:S(2)}) collective-permute-start(bf16[512,256]{1,0:T(8,128)(2,1)S(1)} %add_convert_fusion.1), channel_id=1, source_target_pairs={{0,2},{1,3},{2,4},{3,5},{4,6},{5,7},{6,0},{7,1},{8,10},{9,11},{10,... | collective-permute-start | bytes 786440 | tf_op jit(solution)/shard_map/ppermute | solution.py:14
  239.6 8.2 %collective-permute-start.36 = (bf16[512,256]{1,0:T(8,128)(2,1)S(1)}, bf16[512,256]{1,0:T(8,128)(2,1)S(1)}, u32[]{:S(2)}, u32[]{:S(2)}) collective-permute-start(bf16[512,256]{1,0:T(8,128)(2,1)S(1)} %add_convert_fusion), channel_id=1, source_target_pairs={{0,2},{1,3},{2,4},{3,5},{4,6},{5,7},{6,0},{7,1},{8,10},{9,11},{10,... | collective-permute-start | bytes 786440 | tf_op jit(solution)/shard_map/ppermute | solution.py:14
  (10 other events, 122.2 us)

commit v6 on v4

v6 whole, which is shorter than its diff:
```python
import jax
import jax.numpy as jnp
from jax import lax
from jax.experimental import pallas as pl
from jax.experimental.pallas import tpu as pltpu
from jax.sharding import PartitionSpec as P

STEPS = 2


def from_behind(value, axis, steps):
    count = lax.axis_size(axis)
    pairs = [(source, (source + steps) % count) for source in range(count)]
    return lax.ppermute(value, axis, pairs)


def after(value, *earlier):
    return lax.optimization_barrier((value, *earlier))[0]


def select_columns(inputs, starts, block):
    rows = inputs.shape[0]
    count = starts.shape[0]

    def kernel(starts_ref, inputs_ref, out_ref):
        out_ref[...] = inputs_ref[...]

    size = rows * count * block * inputs.dtype.itemsize
    return pl.pallas_call(
        kernel,
        out_shape=jax.ShapeDtypeStruct((rows, count * block), inputs.dtype),
        grid_spec=pltpu.PrefetchScalarGridSpec(
            num_scalar_prefetch=1,
            grid=(count,),
            in_specs=[pl.BlockSpec((rows, block), lambda i, starts: (0, starts[i]))],
            out_specs=pl.BlockSpec((rows, block), lambda i, starts: (0, i)),
        ),
        cost_estimate=pl.CostEstimate(flops=0, bytes_accessed=2 * size, transcendentals=0),
    )(starts, inputs)


def shards(tokens, targets, params, momentum, push_weight):
    inputs = tokens[0]
    rows, width = inputs.shape
    features = params.shape[2]
    count = lax.axis_size("fsdp")
    half = count // 2
    block = width // count
    place = lax.div(lax.axis_index("fsdp"), 2)
    lane = lax.rem(lax.axis_index("fsdp"), 2)
    swap = [(i, i ^ 1) for i in range(count)]
    key_scale = width ** (-0.5)
    part = features // 2
    contract = (((0,), (0,)), ((), ()))
    wide = jnp.float32
    narrow = jnp.bfloat16

    def chunk(array, c):
        return array[:, c * part : (c + 1) * part]

    def half_columns(side):
        pieces = []
        for back in range(half):
            start = (2 * lax.rem(place - back + half, half) + side) * block
            pieces.append(lax.dynamic_slice_in_dim(inputs, start, block, 1))
        return jnp.concatenate(pieces, axis=1)

    behind = [lax.rem(place - back + half, half) for back in range(half)]
    starts = jnp.stack([2 * at + 1 - lane for at in behind])
    outgoing = select_columns(inputs, starts.astype(jnp.int32), block)
    params = after(params, outgoing)
    momentum = after(momentum, outgoing)
    theirs = lax.ppermute(outgoing, "fsdp", swap)
    mine = half_columns(lane)

    def debias(numerators, weight):
        return (numerators / weight[0]).astype(narrow)

    def column_block(array, back):
        return array[:, back * block : (back + 1) * block]

    def gather(pieces):
        while len(pieces) < half:
            pieces.append(from_behind(pieces[-1], "fsdp", 2))
        return pieces

    def product(left, pieces, total):
        for back, piece in enumerate(pieces):
            total = total + key_scale * jnp.dot(
                column_block(left, back), piece, preferred_element_type=wide
            )
        return total

    def partial(own_grad, other_grad, back):
        return lax.dot_general(
            column_block(mine, back), own_grad, contract, preferred_element_type=wide
        ) + lax.dot_general(
            column_block(theirs, back), other_grad, contract, preferred_element_type=wide
        )

    state = [chunk(params[0], c) for c in range(2)]
    moment = [chunk(momentum[0], c) for c in range(2)]
    target = [chunk(targets[0], c).astype(wide) for c in range(2)]

    weights = [push_weight]
    debiased = [[debias(state[c], push_weight)] for c in range(2)]

    for step in range(STEPS):
        last = step == STEPS - 1
        pieces = debiased
        for back in range(1, half):
            for c in range(2):
                if len(pieces[c]) == back:
                    pieces[c].append(from_behind(pieces[c][-1], "fsdp", 2))
        if step == 0:
            whole = params[0] - (0.2 * 0.9) * momentum[0]
            got = from_behind(whole, "group", 2**step)
            before = 0.5 * (whole + got)
            before = [chunk(before, c) for c in range(2)]
            ready = [got, got]
        else:
            pieces[0][-1] = after(pieces[0][-1], pieces[1][-3])
            own = [state[c] - (0.2 * 0.9) * moment[c] for c in range(2)]
            late = after(own[0].astype(narrow), own[1])
            before, ready = [], []
            for c in range(2):
                got = from_behind(late, "group", 2**step)
                before.append(0.5 * (own[c] + got.astype(wide)))
                ready.append(got)
                late = after(own[1].astype(narrow), got)

        own = [product(mine, pieces[c], -target[c]) for c in range(2)]
        other = [product(theirs, pieces[c], 0.0) for c in range(2)]
        got = []
        for c in range(2):
            sent = jnp.concatenate([other[c], own[c]]).astype(narrow)
            sent = after(sent, ready[c])
            got.append(lax.ppermute(sent, "fsdp", swap))
            if step == 0 and c == 0:
                weights[0] = after(weights[0], sent)
                for hop in range(STEPS):
                    came = from_behind(weights[-1], "group", 2**hop)
                    weights.append(0.5 * (weights[-1] + came))

        def gradients(c):
            received = got[c].astype(wide)
            own_grad = (key_scale * (own[c] + received[:rows])).astype(narrow)
            other_grad = (key_scale * (other[c] + received[rows:])).astype(narrow)
            return own_grad, other_grad

        grads = gradients(0)
        def pass_on(total):
            total = total.astype(narrow)
            return total, from_behind(total, "fsdp", 2)

        def add(c, back):
            return arrived[c].astype(wide) + partial(*grads[c], back)

        arrived = [pass_on(after(partial(*grads, 1).astype(narrow), sent))[1]]
        grads = [grads]
        gone, arrived[0] = pass_on(add(0, 2))
        got[1] = after(got[1], gone, *weights)
        grads.append(gradients(1))
        arrived.append(pass_on(partial(*grads[1], 1))[1])
        for back in range(3, half + 1):
            if back < half:
                arrived[0] = pass_on(add(0, back))[1]
            arrived[1] = pass_on(add(1, back - 1))[1]
        for c in range(2):
            total = add(c, 0)
            behind = from_behind(total.astype(narrow), "group", 2**step)
            if c == 0 and last:
                arrived[1] = after(arrived[1], behind)
            moment[c] = 0.9 * moment[c] + total
            state[c] = before[c] - 0.1 * (total + behind.astype(wide))
            if not last:
                debiased[c] = [debias(state[c], weights[step + 1])]
                if c == 0:
                    debiased[c].append(from_behind(debiased[c][0], "fsdp", 2))
                    arrived[1] = after(arrived[1], debiased[c][1])
    new_params = jnp.concatenate([s / weights[STEPS][0] for s in state], axis=1)
    return new_params[None], jnp.concatenate(moment, axis=1)[None]


def solution(mesh):
    return jax.shard_map(
        shards,
        mesh=mesh,
        in_specs=(
            P("group", "fsdp", None),
            P("group", "fsdp", None),
            P("group", "fsdp", None),
            P("group", "fsdp", None),
            P("group"),
        ),
        out_specs=(P("group", "fsdp", None), P("group", "fsdp", None)),
        check_vma=False,
    )
```

time: 212 us -> 206 us (0.972)
  waiting for transfers between devices: 154 us -> 139 us
  Pallas kernels: 0 us -> 4.35 us
  starting transfers between devices: 19 us -> 22.6 us
  other arithmetic: 6.81 us -> 9.48 us
    ppermute x4, waiting for transfers between devices: 13.7 us -> 1.23 us  [shards(): got.append(lax.ppermute(sent, 'fsdp', swap))]
    pallas_call x0 -> x1, Pallas kernels: none -> 4.35 us  [select_columns(): pl.pallas_call(kernel, out_shape=jax.ShapeDtypeStruct((rows, count * bloc...]
    ppermute x33, waiting for transfers between devices: 141 us -> 138 us  [from_behind(): return lax.ppermute(value, axis, pairs)]
  transfers between devices with their start and end apart: 38 -> 38, of which waited for: 28 -> 31; matrix products, arithmetic and copies ran while one was open for 13% -> 15% of each run, Pallas kernels for 0% -> 0%
where the time goes in v6:
time: 206 us; the launch traced here: 205 us
  waiting for transfers between devices  139 us (67%)
  matrix products  26.5 us (13%)
  starting transfers between devices  22.6 us (11%)
  other arithmetic  9.48 us (5%)
  Pallas kernels  4.35 us (2%)
  between operations  3.27 us (2%)
    ppermute x33, waiting for transfers between devices, from_behind(): return lax.ppermute(value, axis, pairs)  138 us
    dot_general x32, matrix products, product(): jnp.dot(column_block(left, back), piece, preferred_element_type=wide)  15.5 us
    ppermute x33, starting transfers between devices, from_behind(): return lax.ppermute(value, axis, pairs)  15.3 us
    dot_general x16, matrix products, partial(): lax.dot_general(column_block(mine, back), own_grad, contract, preferred_e...  5.52 us
    dot_general x16, matrix products, partial(): lax.dot_general(column_block(theirs, back), other_grad, contract, preferr...  5.41 us
    ppermute x4, starting transfers between devices, shards(): got.append(lax.ppermute(sent, 'fsdp', swap))  4.38 us
    pallas_call x1, Pallas kernels, select_columns(): pl.pallas_call(kernel, out_shape=jax.ShapeDtypeStruct((rows, count * bloc...  4.35 us
  transfers between devices with their start and end apart: 38, of which 31 were waited for; matrix products, arithmetic and copies ran while one was open for 15% of the time, Pallas kernels for 0%

profile of v6, /device:TPU:0, one launch (start us, length us, event | category | flops | bytes accessed | tf_op | source)
XLA Modules:
  0.0 205.4 jit_solution(13048988146910373342)
XLA Ops:
  1.3 4.3 %shard_map.68 = bf16[384,2048]{1,0:T(8,128)(2,1)} custom-call(s32[4]{0:T(128)} %pad_add_fusion.starts_ref, bf16[384,4096]{1,0:T(8,128)(2,1)} %bitcast.158), custom_call_target="tpu_custom_call" | custom-call | bytes 3145728 | tf_op jit(solution)/shard_map/pallas_call | solution.py:29
  5.6 2.9 %collective-permute-start.4 = (bf16[384,2048]{1,0:T(8,128)(2,1)}, bf16[384,2048]{1,0:T(8,128)(2,1)S(1)}, u32[]{:S(2)}, u32[]{:S(2)}) collective-permute-start(bf16[384,2048]{1,0:T(8,128)(2,1)} %shard_map.68), channel_id=1, source_target_pairs={{0,1},{1,0},{2,3},{3,2},{4,5},{5,4},{6,7},{7,6},{8,9},{9,8},{10,11... | collective-permute-start | bytes 4718600 | tf_op jit(solution)/shard_map/ppermute | solution.py:73
  12.1 2.4 %multiply_subtract_fusion = f32[512,512]{1,0:T(8,128)} fusion(f32[1,512,512]{2,1,0:T(8,128)S(1)} %copy-done.1, f32[1,512,512]{2,1,0:T(8,128)} %param.7), kind=kLoop, calls=%fused_computation.71 | loop fusion | flops 524288 | bytes 3145728 | tf_op jit(solution)/shard_map/sub | solution.py:116
  16.1 2.0 fusion.4
  21.2 4.2 %collective-permute-done.6 = bf16[512,256]{1,0:T(8,128)(2,1)} collective-permute-done((bf16[512,256]{1,0:T(8,128)(2,1)S(1)}, bf16[512,256]{1,0:T(8,128)(2,1)}, u32[]{:S(2)}, u32[]{:S(2)}) %collective-permute-start.6) | collective-permute-done | bytes 262176 | tf_op jit(solution)/shard_map/ppermute | solution.py:14
  28.3 3.3 %collective-permute-done.2 = bf16[512,256]{1,0:T(8,128)(2,1)S(1)} collective-permute-done((bf16[512,256]{1,0:T(8,128)(2,1)}, bf16[512,256]{1,0:T(8,128)(2,1)S(1)}, u32[]{:S(2)}, u32[]{:S(2)}) %collective-permute-start.2) | collective-permute-done | bytes 262176 | tf_op jit(solution)/shard_map/ppermute | solution.py:14
  31.5 5.6 %collective-permute-done.7 = bf16[512,256]{1,0:T(8,128)(2,1)S(1)} collective-permute-done((bf16[512,256]{1,0:T(8,128)(2,1)}, bf16[512,256]{1,0:T(8,128)(2,1)S(1)}, u32[]{:S(2)}, u32[]{:S(2)}) %collective-permute-start.7) | collective-permute-done | bytes 262176 | tf_op jit(solution)/shard_map/ppermute | solution.py:14
  37.7 5.1 %collective-permute-done.3 = bf16[512,256]{1,0:T(8,128)(2,1)S(1)} collective-permute-done((bf16[512,256]{1,0:T(8,128)(2,1)S(1)}, bf16[512,256]{1,0:T(8,128)(2,1)S(1)}, u32[]{:S(2)}, u32[]{:S(2)}) %collective-permute-start.3) | collective-permute-done | bytes 262176 | tf_op jit(solution)/shard_map/ppermute | solution.py:14
  43.1 5.2 %collective-permute-done.8 = bf16[512,256]{1,0:T(8,128)(2,1)S(1)} collective-permute-done((bf16[512,256]{1,0:T(8,128)(2,1)S(1)}, bf16[512,256]{1,0:T(8,128)(2,1)S(1)}, u32[]{:S(2)}, u32[]{:S(2)}) %collective-permute-start.8) | collective-permute-done | bytes 262176 | tf_op jit(solution)/shard_map/ppermute | solution.py:14
  59.0 2.9 %collective-permute-start.15 = (f32[1]{0:T(128)}, f32[1]{0:T(128)}, u32[]{:S(2)}, u32[]{:S(2)}) collective-permute-start(f32[1]{0:T(128)} %mul.205), channel_id=1, source_target_pairs={{0,16},{8,24},{16,0},{24,8},{1,17},{9,25},{17,1},{25,9},{2,18},{10... | collective-permute-start | bytes 20 | tf_op jit(solution)/shard_map/ppermute | solution.py:14
  66.5 7.5 %collective-permute-done.9 = bf16[512,256]{1,0:T(8,128)(2,1)S(1)} collective-permute-done((bf16[512,256]{1,0:T(8,128)(2,1)S(1)}, bf16[512,256]{1,0:T(8,128)(2,1)S(1)}, u32[]{:S(2)}, u32[]{:S(2)}) %collective-permute-start.9) | collective-permute-done | bytes 262176 | tf_op jit(solution)/shard_map/ppermute | solution.py:14
  76.0 9.1 %collective-permute-done.10 = bf16[512,256]{1,0:T(8,128)(2,1)S(1)} collective-permute-done((bf16[512,256]{1,0:T(8,128)(2,1)S(1)}, bf16[512,256]{1,0:T(8,128)(2,1)S(1)}, u32[]{:S(2)}, u32[]{:S(2)}) %collective-permute-start.10) | collective-permute-done | bytes 262176 | tf_op jit(solution)/shard_map/ppermute | solution.py:14
  85.5 5.2 %collective-permute-done.16 = bf16[512,256]{1,0:T(8,128)(2,1)S(1)} collective-permute-done((bf16[512,256]{1,0:T(8,128)(2,1)S(1)}, bf16[512,256]{1,0:T(8,128)(2,1)S(1)}, u32[]{:S(2)}, u32[]{:S(2)}) %collective-permute-start.16) | collective-permute-done | bytes 262176 | tf_op jit(solution)/shard_map/ppermute | solution.py:14
  91.1 4.3 %collective-permute-done.11 = bf16[512,256]{1,0:T(8,128)(2,1)S(1)} collective-permute-done((bf16[512,256]{1,0:T(8,128)(2,1)S(1)}, bf16[512,256]{1,0:T(8,128)(2,1)S(1)}, u32[]{:S(2)}, u32[]{:S(2)}) %collective-permute-start.11) | collective-permute-done | bytes 262176 | tf_op jit(solution)/shard_map/ppermute | solution.py:14
  95.8 3.5 %collective-permute-done.17 = bf16[512,256]{1,0:T(8,128)(2,1)S(1)} collective-permute-done((bf16[512,256]{1,0:T(8,128)(2,1)S(1)}, bf16[512,256]{1,0:T(8,128)(2,1)S(1)}, u32[]{:S(2)}, u32[]{:S(2)}) %collective-permute-start.17) | collective-permute-done | bytes 262176 | tf_op jit(solution)/shard_map/ppermute | solution.py:14
  102.5 7.4 %collective-permute-done.18 = bf16[512,256]{1,0:T(8,128)(2,1)S(1)} collective-permute-done((bf16[512,256]{1,0:T(8,128)(2,1)S(1)}, bf16[512,256]{1,0:T(8,128)(2,1)S(1)}, u32[]{:S(2)}, u32[]{:S(2)}) %collective-permute-start.18) | collective-permute-done | bytes 262176 | tf_op jit(solution)/shard_map/ppermute | solution.py:14
  109.9 2.8 %collective-permute-done.19 = bf16[512,256]{1,0:T(8,128)(2,1)S(1)} collective-permute-done((bf16[512,256]{1,0:T(8,128)(2,1)S(1)}, bf16[512,256]{1,0:T(8,128)(2,1)S(1)}, u32[]{:S(2)}, u32[]{:S(2)}) %collective-permute-start.19) | collective-permute-done | bytes 262176 | tf_op jit(solution)/shard_map/ppermute | solution.py:14
  114.2 4.7 %collective-permute-done.20 = bf16[512,256]{1,0:T(8,128)(2,1)S(1)} collective-permute-done((bf16[512,256]{1,0:T(8,128)(2,1)S(1)}, bf16[512,256]{1,0:T(8,128)(2,1)S(1)}, u32[]{:S(2)}, u32[]{:S(2)}) %collective-permute-start.20) | collective-permute-done | bytes 262176 | tf_op jit(solution)/shard_map/ppermute | solution.py:14
  119.2 5.0 %collective-permute-done.22 = bf16[512,256]{1,0:T(8,128)(2,1)S(1)} collective-permute-done((bf16[512,256]{1,0:T(8,128)(2,1)S(1)}, bf16[512,256]{1,0:T(8,128)(2,1)S(1)}, u32[]{:S(2)}, u32[]{:S(2)}) %collective-permute-start.22) | collective-permute-done | bytes 262176 | tf_op jit(solution)/shard_map/ppermute | solution.py:14
  126.2 4.1 %collective-permute-done.24 = bf16[512,256]{1,0:T(8,128)(2,1)S(1)} collective-permute-done((bf16[512,256]{1,0:T(8,128)(2,1)S(1)}, bf16[512,256]{1,0:T(8,128)(2,1)S(1)}, u32[]{:S(2)}, u32[]{:S(2)}) %collective-permute-start.24) | collective-permute-done | bytes 262176 | tf_op jit(solution)/shard_map/ppermute | solution.py:14
  130.2 5.3 %collective-permute-done.23 = bf16[512,256]{1,0:T(8,128)(2,1)S(1)} collective-permute-done((bf16[512,256]{1,0:T(8,128)(2,1)S(1)}, bf16[512,256]{1,0:T(8,128)(2,1)S(1)}, u32[]{:S(2)}, u32[]{:S(2)}) %collective-permute-start.23) | collective-permute-done | bytes 262176 | tf_op jit(solution)/shard_map/ppermute | solution.py:14
  138.8 8.1 %collective-permute-done.26 = bf16[512,256]{1,0:T(8,128)(2,1)S(1)} collective-permute-done((bf16[512,256]{1,0:T(8,128)(2,1)S(1)}, bf16[512,256]{1,0:T(8,128)(2,1)S(1)}, u32[]{:S(2)}, u32[]{:S(2)}) %collective-permute-start.26) | collective-permute-done | bytes 262176 | tf_op jit(solution)/shard_map/ppermute | solution.py:14
  148.6 6.4 %collective-permute-done.27 = bf16[512,256]{1,0:T(8,128)(2,1)S(1)} collective-permute-done((bf16[512,256]{1,0:T(8,128)(2,1)S(1)}, bf16[512,256]{1,0:T(8,128)(2,1)S(1)}, u32[]{:S(2)}, u32[]{:S(2)}) %collective-permute-start.27) | collective-permute-done | bytes 262176 | tf_op jit(solution)/shard_map/ppermute | solution.py:14
  158.0 5.8 %collective-permute-done.29 = bf16[512,256]{1,0:T(8,128)(2,1)S(1)} collective-permute-done((bf16[512,256]{1,0:T(8,128)(2,1)S(1)}, bf16[512,256]{1,0:T(8,128)(2,1)S(1)}, u32[]{:S(2)}, u32[]{:S(2)}) %collective-permute-start.29) | collective-permute-done | bytes 262176 | tf_op jit(solution)/shard_map/ppermute | solution.py:14
  165.9 7.7 %collective-permute-done.30 = bf16[512,256]{1,0:T(8,128)(2,1)S(1)} collective-permute-done((bf16[512,256]{1,0:T(8,128)(2,1)S(1)}, bf16[512,256]{1,0:T(8,128)(2,1)S(1)}, u32[]{:S(2)}, u32[]{:S(2)}) %collective-permute-start.30) | collective-permute-done | bytes 262176 | tf_op jit(solution)/shard_map/ppermute | solution.py:14
  174.1 5.2 %collective-permute-done.34 = bf16[512,256]{1,0:T(8,128)(2,1)S(1)} collective-permute-done((bf16[512,256]{1,0:T(8,128)(2,1)S(1)}, bf16[512,256]{1,0:T(8,128)(2,1)S(1)}, u32[]{:S(2)}, u32[]{:S(2)}) %collective-permute-start.34) | collective-permute-done | bytes 262176 | tf_op jit(solution)/shard_map/ppermute | solution.py:14
  179.7 4.3 %collective-permute-done.31 = bf16[512,256]{1,0:T(8,128)(2,1)S(1)} collective-permute-done((bf16[512,256]{1,0:T(8,128)(2,1)S(1)}, bf16[512,256]{1,0:T(8,128)(2,1)S(1)}, u32[]{:S(2)}, u32[]{:S(2)}) %collective-permute-start.31) | collective-permute-done | bytes 262176 | tf_op jit(solution)/shard_map/ppermute | solution.py:14
  184.3 2.3 %collective-permute-start.32 = (bf16[512,256]{1,0:T(8,128)(2,1)S(1)}, bf16[512,256]{1,0:T(8,128)(2,1)S(1)}, u32[]{:S(2)}, u32[]{:S(2)}) collective-permute-start(bf16[512,256]{1,0:T(8,128)(2,1)S(1)} %get-tuple-element.74), channel_id=1, source_target_pairs={{0,16},{8,24},{16,0},{24,8},{1,17},{9,25},{17,1},{25,9},{2,18},{10... | collective-permute-start | bytes 786440 | tf_op jit(solution)/shard_map/ppermute | solution.py:14
  188.7 2.3 %collective-permute-done.32 = bf16[512,256]{1,0:T(8,128)(2,1)S(1)} collective-permute-done((bf16[512,256]{1,0:T(8,128)(2,1)S(1)}, bf16[512,256]{1,0:T(8,128)(2,1)S(1)}, u32[]{:S(2)}, u32[]{:S(2)}) %collective-permute-start.32) | collective-permute-done | bytes 262176 | tf_op jit(solution)/shard_map/ppermute | solution.py:14
  191.0 5.5 %collective-permute-done.36 = bf16[512,256]{1,0:T(8,128)(2,1)S(1)} collective-permute-done((bf16[512,256]{1,0:T(8,128)(2,1)S(1)}, bf16[512,256]{1,0:T(8,128)(2,1)S(1)}, u32[]{:S(2)}, u32[]{:S(2)}) %collective-permute-start.36) | collective-permute-done | bytes 262176 | tf_op jit(solution)/shard_map/ppermute | solution.py:14
  196.8 2.3 %collective-permute-start.37 = (bf16[512,256]{1,0:T(8,128)(2,1)S(1)}, bf16[512,256]{1,0:T(8,128)(2,1)S(1)}, u32[]{:S(2)}, u32[]{:S(2)}) collective-permute-start(bf16[512,256]{1,0:T(8,128)(2,1)S(1)} %get-tuple-element.76), channel_id=1, source_target_pairs={{0,16},{8,24},{16,0},{24,8},{1,17},{9,25},{17,1},{25,9},{2,18},{10... | collective-permute-start | bytes 786440 | tf_op jit(solution)/shard_map/ppermute | solution.py:14
  199.4 4.1 %collective-permute-done.37 = bf16[512,256]{1,0:T(8,128)(2,1)S(1)} collective-permute-done((bf16[512,256]{1,0:T(8,128)(2,1)S(1)}, bf16[512,256]{1,0:T(8,128)(2,1)S(1)}, u32[]{:S(2)}, u32[]{:S(2)}) %collective-permute-start.37) | collective-permute-done | bytes 262176 | tf_op jit(solution)/shard_map/ppermute | solution.py:14
  (137 shorter events, 51.3 us)
Async XLA Ops:
  5.6 44.7 %collective-permute-start.4 = (bf16[384,2048]{1,0:T(8,128)(2,1)}, bf16[384,2048]{1,0:T(8,128)(2,1)S(1)}, u32[]{:S(2)}, u32[]{:S(2)}) collective-permute-start(bf16[384,2048]{1,0:T(8,128)(2,1)} %shard_map.68), channel_id=1, source_target_pairs={{0,1},{1,0},{2,3},{3,2},{4,5},{5,4},{6,7},{7,6},{8,9},{9,8},{10,11... | collective-permute-start | bytes 4718600 | tf_op jit(solution)/shard_map/ppermute | solution.py:73
  10.5 9.8 %collective-permute-start.1 = (bf16[512,256]{1,0:T(8,128)(2,1)S(1)}, bf16[512,256]{1,0:T(8,128)(2,1)}, u32[]{:S(2)}, u32[]{:S(2)}) collective-permute-start(bf16[512,256]{1,0:T(8,128)(2,1)S(1)} %get-tuple-element.43), channel_id=1, source_target_pairs={{0,2},{1,3},{2,4},{3,5},{4,6},{5,7},{6,0},{7,1},{8,10},{9,11},{10,... | collective-permute-start | bytes 786440 | tf_op jit(solution)/shard_map/ppermute | solution.py:14
  14.6 34.0 %collective-permute-start = (f32[512,512]{1,0:T(8,128)}, f32[512,512]{1,0:T(8,128)}, u32[]{:S(2)}, u32[]{:S(2)}) collective-permute-start(f32[512,512]{1,0:T(8,128)} %multiply_subtract_fusion), channel_id=1, source_target_pairs={{0,8},{8,16},{16,24},{24,0},{1,9},{9,17},{17,25},{25,1},{2,10},{10... | collective-permute-start | bytes 3145736 | tf_op jit(solution)/shard_map/ppermute | solution.py:14
  14.6 10.9 %collective-permute-start.6 = (bf16[512,256]{1,0:T(8,128)(2,1)S(1)}, bf16[512,256]{1,0:T(8,128)(2,1)}, u32[]{:S(2)}, u32[]{:S(2)}) collective-permute-start(bf16[512,256]{1,0:T(8,128)(2,1)S(1)} %get-tuple-element.42), channel_id=1, source_target_pairs={{0,2},{1,3},{2,4},{3,5},{4,6},{5,7},{6,0},{7,1},{8,10},{9,11},{10,... | collective-permute-start | bytes 786440 | tf_op jit(solution)/shard_map/ppermute | solution.py:14
  20.3 11.3 %collective-permute-start.2 = (bf16[512,256]{1,0:T(8,128)(2,1)}, bf16[512,256]{1,0:T(8,128)(2,1)S(1)}, u32[]{:S(2)}, u32[]{:S(2)}) collective-permute-start(bf16[512,256]{1,0:T(8,128)(2,1)} %collective-permute-done.1), channel_id=1, source_target_pairs={{0,2},{1,3},{2,4},{3,5},{4,6},{5,7},{6,0},{7,1},{8,10},{9,11},{10,... | collective-permute-start | bytes 786440 | tf_op jit(solution)/shard_map/ppermute | solution.py:14
  25.4 11.7 %collective-permute-start.7 = (bf16[512,256]{1,0:T(8,128)(2,1)}, bf16[512,256]{1,0:T(8,128)(2,1)S(1)}, u32[]{:S(2)}, u32[]{:S(2)}) collective-permute-start(bf16[512,256]{1,0:T(8,128)(2,1)} %collective-permute-done.6), channel_id=1, source_target_pairs={{0,2},{1,3},{2,4},{3,5},{4,6},{5,7},{6,0},{7,1},{8,10},{9,11},{10,... | collective-permute-start | bytes 786440 | tf_op jit(solution)/shard_map/ppermute | solution.py:14
  31.5 11.2 %collective-permute-start.3 = (bf16[512,256]{1,0:T(8,128)(2,1)S(1)}, bf16[512,256]{1,0:T(8,128)(2,1)S(1)}, u32[]{:S(2)}, u32[]{:S(2)}) collective-permute-start(bf16[512,256]{1,0:T(8,128)(2,1)S(1)} %collective-permute-done.2), channel_id=1, source_target_pairs={{0,2},{1,3},{2,4},{3,5},{4,6},{5,7},{6,0},{7,1},{8,10},{9,11},{10,... | collective-permute-start | bytes 786440 | tf_op jit(solution)/shard_map/ppermute | solution.py:14
  37.2 11.1 %collective-permute-start.8 = (bf16[512,256]{1,0:T(8,128)(2,1)S(1)}, bf16[512,256]{1,0:T(8,128)(2,1)S(1)}, u32[]{:S(2)}, u32[]{:S(2)}) collective-permute-start(bf16[512,256]{1,0:T(8,128)(2,1)S(1)} %collective-permute-done.7), channel_id=1, source_target_pairs={{0,2},{1,3},{2,4},{3,5},{4,6},{5,7},{6,0},{7,1},{8,10},{9,11},{10,... | collective-permute-start | bytes 786440 | tf_op jit(solution)/shard_map/ppermute | solution.py:14
  52.4 12.0 %collective-permute-start.5 = (bf16[768,256]{1,0:T(8,128)(2,1)S(1)}, bf16[768,256]{1,0:T(8,128)(2,1)S(1)}, u32[]{:S(2)}, u32[]{:S(2)}) collective-permute-start(bf16[768,256]{1,0:T(8,128)(2,1)S(1)} %pad_maximum_fusion), channel_id=1, source_target_pairs={{0,1},{1,0},{2,3},{3,2},{4,5},{5,4},{6,7},{7,6},{8,9},{9,8},{10,11... | collective-permute-start | bytes 1179656 | tf_op jit(solution)/shard_map/ppermute | solution.py:138
  55.2 19.1 %collective-permute-start.13 = (bf16[768,256]{1,0:T(8,128)(2,1)S(1)}, bf16[768,256]{1,0:T(8,128)(2,1)S(1)}, u32[]{:S(2)}, u32[]{:S(2)}) collective-permute-start(bf16[768,256]{1,0:T(8,128)(2,1)S(1)} %pad_maximum_fusion.1), channel_id=1, source_target_pairs={{0,1},{1,0},{2,3},{3,2},{4,5},{5,4},{6,7},{7,6},{8,9},{9,8},{10,11... | collective-permute-start | bytes 1179656 | tf_op jit(solution)/shard_map/ppermute | solution.py:138
  65.7 8.2 %collective-permute-start.9 = (bf16[512,256]{1,0:T(8,128)(2,1)S(1)}, bf16[512,256]{1,0:T(8,128)(2,1)S(1)}, u32[]{:S(2)}, u32[]{:S(2)}) collective-permute-start(bf16[512,256]{1,0:T(8,128)(2,1)S(1)} %fusion), channel_id=1, source_target_pairs={{0,2},{1,3},{2,4},{3,5},{4,6},{5,7},{6,0},{7,1},{8,10},{9,11},{10,... | collective-permute-start | bytes 786440 | tf_op jit(solution)/shard_map/ppermute | solution.py:14
  74.3 10.8 %collective-permute-start.10 = (bf16[512,256]{1,0:T(8,128)(2,1)S(1)}, bf16[512,256]{1,0:T(8,128)(2,1)S(1)}, u32[]{:S(2)}, u32[]{:S(2)}) collective-permute-start(bf16[512,256]{1,0:T(8,128)(2,1)S(1)} %add_convert_fusion.7), channel_id=1, source_target_pairs={{0,2},{1,3},{2,4},{3,5},{4,6},{5,7},{6,0},{7,1},{8,10},{9,11},{10,... | collective-permute-start | bytes 786440 | tf_op jit(solution)/shard_map/ppermute | solution.py:14
  75.6 15.1 %collective-permute-start.16 = (bf16[512,256]{1,0:T(8,128)(2,1)S(1)}, bf16[512,256]{1,0:T(8,128)(2,1)S(1)}, u32[]{:S(2)}, u32[]{:S(2)}) collective-permute-start(bf16[512,256]{1,0:T(8,128)(2,1)S(1)} %fusion.1), channel_id=1, source_target_pairs={{0,2},{1,3},{2,4},{3,5},{4,6},{5,7},{6,0},{7,1},{8,10},{9,11},{10,... | collective-permute-start | bytes 786440 | tf_op jit(solution)/shard_map/ppermute | solution.py:14
  85.4 9.9 %collective-permute-start.11 = (bf16[512,256]{1,0:T(8,128)(2,1)S(1)}, bf16[512,256]{1,0:T(8,128)(2,1)S(1)}, u32[]{:S(2)}, u32[]{:S(2)}) collective-permute-start(bf16[512,256]{1,0:T(8,128)(2,1)S(1)} %add_convert_fusion.6), channel_id=1, source_target_pairs={{0,2},{1,3},{2,4},{3,5},{4,6},{5,7},{6,0},{7,1},{8,10},{9,11},{10,... | collective-permute-start | bytes 786440 | tf_op jit(solution)/shard_map/ppermute | solution.py:14
  91.0 8.2 %collective-permute-start.17 = (bf16[512,256]{1,0:T(8,128)(2,1)S(1)}, bf16[512,256]{1,0:T(8,128)(2,1)S(1)}, u32[]{:S(2)}, u32[]{:S(2)}) collective-permute-start(bf16[512,256]{1,0:T(8,128)(2,1)S(1)} %add_convert_fusion.5), channel_id=1, source_target_pairs={{0,2},{1,3},{2,4},{3,5},{4,6},{5,7},{6,0},{7,1},{8,10},{9,11},{10,... | collective-permute-start | bytes 786440 | tf_op jit(solution)/shard_map/ppermute | solution.py:14
  99.6 10.3 %collective-permute-start.18 = (bf16[512,256]{1,0:T(8,128)(2,1)S(1)}, bf16[512,256]{1,0:T(8,128)(2,1)S(1)}, u32[]{:S(2)}, u32[]{:S(2)}) collective-permute-start(bf16[512,256]{1,0:T(8,128)(2,1)S(1)} %add_convert_fusion.4), channel_id=1, source_target_pairs={{0,2},{1,3},{2,4},{3,5},{4,6},{5,7},{6,0},{7,1},{8,10},{9,11},{10,... | collective-permute-start | bytes 786440 | tf_op jit(solution)/shard_map/ppermute | solution.py:14
  101.8 10.9 %collective-permute-start.19 = (bf16[512,256]{1,0:T(8,128)(2,1)S(1)}, bf16[512,256]{1,0:T(8,128)(2,1)S(1)}, u32[]{:S(2)}, u32[]{:S(2)}) collective-permute-start(bf16[512,256]{1,0:T(8,128)(2,1)S(1)} %divide_convert_fusion.1), channel_id=1, source_target_pairs={{0,2},{1,3},{2,4},{3,5},{4,6},{5,7},{6,0},{7,1},{8,10},{9,11},{10,... | collective-permute-start | bytes 786440 | tf_op jit(solution)/shard_map/ppermute | solution.py:14
  113.1 11.1 %collective-permute-start.22 = (bf16[512,256]{1,0:T(8,128)(2,1)S(1)}, bf16[512,256]{1,0:T(8,128)(2,1)S(1)}, u32[]{:S(2)}, u32[]{:S(2)}) collective-permute-start(bf16[512,256]{1,0:T(8,128)(2,1)S(1)} %collective-permute-done.19), channel_id=1, source_target_pairs={{0,2},{1,3},{2,4},{3,5},{4,6},{5,7},{6,0},{7,1},{8,10},{9,11},{10,... | collective-permute-start | bytes 786440 | tf_op jit(solution)/shard_map/ppermute | solution.py:14
  119.1 11.1 %collective-permute-start.24 = (bf16[512,256]{1,0:T(8,128)(2,1)S(1)}, bf16[512,256]{1,0:T(8,128)(2,1)S(1)}, u32[]{:S(2)}, u32[]{:S(2)}) collective-permute-start(bf16[512,256]{1,0:T(8,128)(2,1)S(1)} %get-tuple-element.39), channel_id=1, source_target_pairs={{0,2},{1,3},{2,4},{3,5},{4,6},{5,7},{6,0},{7,1},{8,10},{9,11},{10,... | collective-permute-start | bytes 786440 | tf_op jit(solution)/shard_map/ppermute | solution.py:14
  124.2 11.4 %collective-permute-start.23 = (bf16[512,256]{1,0:T(8,128)(2,1)S(1)}, bf16[512,256]{1,0:T(8,128)(2,1)S(1)}, u32[]{:S(2)}, u32[]{:S(2)}) collective-permute-start(bf16[512,256]{1,0:T(8,128)(2,1)S(1)} %collective-permute-done.22), channel_id=1, source_target_pairs={{0,2},{1,3},{2,4},{3,5},{4,6},{5,7},{6,0},{7,1},{8,10},{9,11},{10,... | collective-permute-start | bytes 786440 | tf_op jit(solution)/shard_map/ppermute | solution.py:14
  124.5 11.9 %collective-permute-start.21 = (bf16[512,256]{1,0:T(8,128)(2,1)S(1)}, bf16[512,256]{1,0:T(8,128)(2,1)S(1)}, u32[]{:S(2)}, u32[]{:S(2)}) collective-permute-start(bf16[512,256]{1,0:T(8,128)(2,1)S(1)} %get-tuple-element.26), channel_id=1, source_target_pairs={{0,16},{8,24},{16,0},{24,8},{1,17},{9,25},{17,1},{25,9},{2,18},{10... | collective-permute-start | bytes 786440 | tf_op jit(solution)/shard_map/ppermute | solution.py:14
  136.4 11.0 %collective-permute-start.25 = (bf16[768,256]{1,0:T(8,128)(2,1)S(1)}, bf16[768,256]{1,0:T(8,128)(2,1)S(1)}, u32[]{:S(2)}, u32[]{:S(2)}) collective-permute-start(bf16[768,256]{1,0:T(8,128)(2,1)S(1)} %pad_maximum_fusion.2), channel_id=1, source_target_pairs={{0,1},{1,0},{2,3},{3,2},{4,5},{5,4},{6,7},{7,6},{8,9},{9,8},{10,11... | collective-permute-start | bytes 1179656 | tf_op jit(solution)/shard_map/ppermute | solution.py:138
  137.0 18.6 %collective-permute-start.28 = (bf16[512,256]{1,0:T(8,128)(2,1)S(1)}, bf16[512,256]{1,0:T(8,128)(2,1)S(1)}, u32[]{:S(2)}, u32[]{:S(2)}) collective-permute-start(bf16[512,256]{1,0:T(8,128)(2,1)S(1)} %get-tuple-element.29), channel_id=1, source_target_pairs={{0,16},{8,24},{16,0},{24,8},{1,17},{9,25},{17,1},{25,9},{2,18},{10... | collective-permute-start | bytes 786440 | tf_op jit(solution)/shard_map/ppermute | solution.py:14
  138.0 8.9 %collective-permute-start.26 = (bf16[512,256]{1,0:T(8,128)(2,1)S(1)}, bf16[512,256]{1,0:T(8,128)(2,1)S(1)}, u32[]{:S(2)}, u32[]{:S(2)}) collective-permute-start(bf16[512,256]{1,0:T(8,128)(2,1)S(1)} %collective-permute-done.24), channel_id=1, source_target_pairs={{0,2},{1,3},{2,4},{3,5},{4,6},{5,7},{6,0},{7,1},{8,10},{9,11},{10,... | collective-permute-start | bytes 786440 | tf_op jit(solution)/shard_map/ppermute | solution.py:14
  146.9 8.2 %collective-permute-start.27 = (bf16[512,256]{1,0:T(8,128)(2,1)S(1)}, bf16[512,256]{1,0:T(8,128)(2,1)S(1)}, u32[]{:S(2)}, u32[]{:S(2)}) collective-permute-start(bf16[512,256]{1,0:T(8,128)(2,1)S(1)} %collective-permute-done.26), channel_id=1, source_target_pairs={{0,2},{1,3},{2,4},{3,5},{4,6},{5,7},{6,0},{7,1},{8,10},{9,11},{10,... | collective-permute-start | bytes 786440 | tf_op jit(solution)/shard_map/ppermute | solution.py:14
  155.6 8.2 %collective-permute-start.29 = (bf16[512,256]{1,0:T(8,128)(2,1)S(1)}, bf16[512,256]{1,0:T(8,128)(2,1)S(1)}, u32[]{:S(2)}, u32[]{:S(2)}) collective-permute-start(bf16[512,256]{1,0:T(8,128)(2,1)S(1)} %fusion.2), channel_id=1, source_target_pairs={{0,2},{1,3},{2,4},{3,5},{4,6},{5,7},{6,0},{7,1},{8,10},{9,11},{10,... | collective-permute-start | bytes 786440 | tf_op jit(solution)/shard_map/ppermute | solution.py:14
  156.0 8.2 %collective-permute-start.33 = (bf16[768,256]{1,0:T(8,128)(2,1)S(1)}, bf16[768,256]{1,0:T(8,128)(2,1)S(1)}, u32[]{:S(2)}, u32[]{:S(2)}) collective-permute-start(bf16[768,256]{1,0:T(8,128)(2,1)S(1)} %pad_maximum_fusion.3), channel_id=1, source_target_pairs={{0,1},{1,0},{2,3},{3,2},{4,5},{5,4},{6,7},{7,6},{8,9},{9,8},{10,11... | collective-permute-start | bytes 1179656 | tf_op jit(solution)/shard_map/ppermute | solution.py:138
  164.2 9.5 %collective-permute-start.30 = (bf16[512,256]{1,0:T(8,128)(2,1)S(1)}, bf16[512,256]{1,0:T(8,128)(2,1)S(1)}, u32[]{:S(2)}, u32[]{:S(2)}) collective-permute-start(bf16[512,256]{1,0:T(8,128)(2,1)S(1)} %add_convert_fusion.3), channel_id=1, source_target_pairs={{0,2},{1,3},{2,4},{3,5},{4,6},{5,7},{6,0},{7,1},{8,10},{9,11},{10,... | collective-permute-start | bytes 786440 | tf_op jit(solution)/shard_map/ppermute | solution.py:14
  165.5 13.8 %collective-permute-start.34 = (bf16[512,256]{1,0:T(8,128)(2,1)S(1)}, bf16[512,256]{1,0:T(8,128)(2,1)S(1)}, u32[]{:S(2)}, u32[]{:S(2)}) collective-permute-start(bf16[512,256]{1,0:T(8,128)(2,1)S(1)} %fusion.3), channel_id=1, source_target_pairs={{0,2},{1,3},{2,4},{3,5},{4,6},{5,7},{6,0},{7,1},{8,10},{9,11},{10,... | collective-permute-start | bytes 786440 | tf_op jit(solution)/shard_map/ppermute | solution.py:14
  174.0 10.0 %collective-permute-start.31 = (bf16[512,256]{1,0:T(8,128)(2,1)S(1)}, bf16[512,256]{1,0:T(8,128)(2,1)S(1)}, u32[]{:S(2)}, u32[]{:S(2)}) collective-permute-start(bf16[512,256]{1,0:T(8,128)(2,1)S(1)} %add_convert_fusion.2), channel_id=1, source_target_pairs={{0,2},{1,3},{2,4},{3,5},{4,6},{5,7},{6,0},{7,1},{8,10},{9,11},{10,... | collective-permute-start | bytes 786440 | tf_op jit(solution)/shard_map/ppermute | solution.py:14
  179.6 8.3 %collective-permute-start.35 = (bf16[512,256]{1,0:T(8,128)(2,1)S(1)}, bf16[512,256]{1,0:T(8,128)(2,1)S(1)}, u32[]{:S(2)}, u32[]{:S(2)}) collective-permute-start(bf16[512,256]{1,0:T(8,128)(2,1)S(1)} %add_convert_fusion.1), channel_id=1, source_target_pairs={{0,2},{1,3},{2,4},{3,5},{4,6},{5,7},{6,0},{7,1},{8,10},{9,11},{10,... | collective-permute-start | bytes 786440 | tf_op jit(solution)/shard_map/ppermute | solution.py:14
  188.3 8.2 %collective-permute-start.36 = (bf16[512,256]{1,0:T(8,128)(2,1)S(1)}, bf16[512,256]{1,0:T(8,128)(2,1)S(1)}, u32[]{:S(2)}, u32[]{:S(2)}) collective-permute-start(bf16[512,256]{1,0:T(8,128)(2,1)S(1)} %add_convert_fusion), channel_id=1, source_target_pairs={{0,2},{1,3},{2,4},{3,5},{4,6},{5,7},{6,0},{7,1},{8,10},{9,11},{10,... | collective-permute-start | bytes 786440 | tf_op jit(solution)/shard_map/ppermute | solution.py:14
  (9 other events, 63.2 us)
